TPU v7x, 32 devices: a whole 2x2x4 slice. The times are simulated.
32 devices in a mesh: dp: 4 (over z), expert: 8 (over y, x, core).
Axes of the slice: x: 2, y: 2, z: 4, core: 2. Of those that a mesh axis runs over, the one named last changes fastest.
Arguments:
- tokens: bfloat16 [4096, 2048], P(('dp', 'expert')), may hold values from -6 to 6
- expert_ids: int32 [4096, 2], P(('dp', 'expert')), may hold values from 0 to 7, as said below
- slot_index: int32 [4096, 2], P(('dp', 'expert')), may hold values from 0 to 63, as said below
- routing_gates: float32 [4096, 2], P(('dp', 'expert')), may hold values from 0.2 to 1
- grad_out: bfloat16 [4096, 2048], P(('dp', 'expert')), may hold values from -1.5 to 1.5
- w_gate: bfloat16 [8, 2048, 768], P('expert', 'dp'), may hold values from -0.125 to 0.125
- w_up: bfloat16 [8, 2048, 768], P('expert', 'dp'), may hold values from -0.125 to 0.125
- w_down: bfloat16 [8, 2048, 768], P('expert', 'dp'), may hold values from -0.21875 to 0.21875
Outputs:
- layer_out: bfloat16 [4096, 2048], P(('dp', 'expert'))
- grad_tokens: bfloat16 [4096, 2048], P(('dp', 'expert'))
- grad_gates: float32 [4096, 2], P(('dp', 'expert'))
- grad_w_gate: bfloat16 [8, 2048, 768], P('expert', 'dp')
- grad_w_up: bfloat16 [8, 2048, 768], P('expert', 'dp')
- grad_w_down: bfloat16 [8, 2048, 768], P('expert', 'dp')
Inputs may be any that keep to these rules, and one draw needn't show every extreme that they name: `expert_ids`: each row names 2 different experts. In each aligned block of 128 rows no expert is named more than 64 times; for each group of 8 blocks in a row, some expert is named exactly 64 times in every block of the group. `slot_index`: within one aligned block of 128 rows, the pairs that name one expert have distinct places, 0 up to their number minus one.
All inputs are finite; a program needn't handle non-finite values.
Results may differ from a plain program's by a relative error of at most 0.014.
Values may be sent and summed in bfloat16 or wider, within the bound.
No kernel may reach another device: no remote copies, remote signals or barrier semaphores. Data moves between devices by JAX's collectives and lax.ppermute only.
A program may use at most 128 MiB of HBM per device.

v0:
```python
import jax
import jax.numpy as jnp
from jax import lax
from jax.sharding import PartitionSpec as P


def partial_term(left_rows, right_rows):
    return lax.dot_general(
        left_rows, right_rows, (((0,), (0,)), ((), ())), preferred_element_type=jnp.float32
    )


def on_device(tokens, expert_ids, slot_index, routing_gates, grad_out, w_gate, w_up, w_down):
    tok_dev, top_k = expert_ids.shape
    model_width = tokens.shape[1]
    experts = lax.axis_size("expert")
    capacity = 2 * tok_dev * top_k // experts
    target = (expert_ids * capacity + slot_index).reshape(-1)
    pair_index = jnp.arange(tok_dev * top_k, dtype=jnp.int32)
    source = jnp.full((experts * capacity,), -1, jnp.int32).at[target].set(pair_index)
    occupied = (source >= 0)[:, None]
    pair_safe = jnp.where(source >= 0, source, 0)
    token_safe = pair_safe // top_k
    zero_row = jnp.zeros((), jnp.bfloat16)
    outbound = jnp.where(occupied, tokens[token_safe], zero_row).reshape(
        experts, capacity, model_width
    )
    scaled = (routing_gates[:, :, None] * grad_out[:, None, :].astype(jnp.float32)).astype(
        jnp.bfloat16
    )
    scaled_rows = scaled.reshape(-1, model_width)
    grad_outbound = jnp.where(occupied, scaled_rows[pair_safe], zero_row).reshape(
        experts, capacity, model_width
    )
    gathered = (
        lax.all_gather(w_gate, "dp", axis=1, tiled=True),
        lax.all_gather(w_up, "dp", axis=1, tiled=True),
        lax.all_gather(w_down, "dp", axis=1, tiled=True),
    )
    full_gate = gathered[0][0]
    full_up = gathered[1][0]
    full_down = gathered[2][0]
    arrived = lax.all_to_all(outbound, "expert", split_axis=0, concat_axis=0, tiled=True)
    slot_count = arrived.shape[1]
    forward_flat_rows = arrived.reshape(-1, model_width)
    gate_pre = jnp.dot(forward_flat_rows, full_gate, preferred_element_type=jnp.float32)
    up_pre = jnp.dot(forward_flat_rows, full_up, preferred_element_type=jnp.float32)
    forward_hidden = (gate_pre * jax.nn.sigmoid(gate_pre) * up_pre).astype(jnp.bfloat16)
    produced = jnp.dot(forward_hidden, full_down.T, preferred_element_type=jnp.float32).astype(
        jnp.bfloat16
    )
    returned = lax.all_to_all(
        produced.reshape(experts, slot_count, model_width),
        "expert",
        split_axis=0,
        concat_axis=0,
        tiled=True,
    )
    returned, arrived, gate_stack, up_stack = (
        returned,
        arrived,
        gate_pre.reshape(experts, slot_count, -1),
        up_pre.reshape(experts, slot_count, -1),
    )
    grad_arrived = lax.all_to_all(grad_outbound, "expert", split_axis=0, concat_axis=0, tiled=True)
    by_pair = returned.reshape(-1, model_width)[target].reshape(tok_dev, top_k, model_width)
    layer_out = jnp.sum(by_pair.astype(jnp.float32) * routing_gates[:, :, None], axis=1).astype(
        jnp.bfloat16
    )
    grad_gates = jnp.einsum("tkd,td->tk", by_pair, grad_out, preferred_element_type=jnp.float32)
    flat_grad = grad_arrived.reshape(-1, model_width)
    flat_rows = arrived.reshape(-1, model_width)
    gate_flat = gate_stack.reshape(flat_grad.shape[0], -1)
    up_flat = up_stack.reshape(flat_grad.shape[0], -1)
    sigmoid_gate = jax.nn.sigmoid(gate_flat)
    active = gate_flat * sigmoid_gate
    hidden = (active * up_flat).astype(jnp.bfloat16)
    down_back = jnp.dot(flat_grad, full_down, preferred_element_type=jnp.float32)
    silu_slope = sigmoid_gate * (1.0 + gate_flat * (1.0 - sigmoid_gate))
    grad_gate_pre = (down_back * up_flat * silu_slope).astype(jnp.bfloat16)
    grad_up_pre = (down_back * active).astype(jnp.bfloat16)
    input_back = (
        jnp.dot(grad_gate_pre, full_gate.T, preferred_element_type=jnp.float32)
        + jnp.dot(grad_up_pre, full_up.T, preferred_element_type=jnp.float32)
    ).astype(jnp.bfloat16)
    input_return = lax.all_to_all(
        input_back.reshape(experts, capacity, model_width),
        "expert",
        split_axis=0,
        concat_axis=0,
        tiled=True,
    )
    back_pairs = input_return.reshape(-1, model_width)[target].reshape(tok_dev, top_k, model_width)
    grad_tokens = jnp.sum(back_pairs.astype(jnp.float32), axis=1).astype(jnp.bfloat16)
    stacked = lax.psum_scatter(
        jnp.concatenate(
            [
                partial_term(flat_rows, grad_gate_pre),
                partial_term(flat_rows, grad_up_pre),
                partial_term(flat_grad, hidden),
            ],
            axis=1,
        ).astype(jnp.bfloat16),
        "dp",
        scatter_dimension=0,
        tiled=True,
    ).astype(jnp.float32)
    inner = hidden.shape[1]
    grad_gate_w = stacked[:, :inner]
    grad_up_w = stacked[:, inner : 2 * inner]
    grad_down_w = stacked[:, 2 * inner :]
    return (
        layer_out,
        grad_tokens,
        grad_gates,
        grad_gate_w.astype(jnp.bfloat16)[None],
        grad_up_w.astype(jnp.bfloat16)[None],
        grad_down_w.astype(jnp.bfloat16)[None],
    )


def solution(mesh):
    in_specs = (
        P(("dp", "expert"), None),
        P(("dp", "expert"), None),
        P(("dp", "expert"), None),
        P(("dp", "expert"), None),
        P(("dp", "expert"), None),
        P("expert", "dp", None),
        P("expert", "dp", None),
        P("expert", "dp", None),
    )
    out_specs = (
        P(("dp", "expert"), None),
        P(("dp", "expert"), None),
        P(("dp", "expert"), None),
        P("expert", "dp", None),
        P("expert", "dp", None),
        P("expert", "dp", None),
    )
    return jax.shard_map(
        on_device, mesh=mesh, in_specs=in_specs, out_specs=out_specs, check_vma=False
    )
```

profile of v0, /device:TPU:0, one launch (start us, length us, event | category | flops | bytes accessed | tf_op | source)
XLA Modules:
  0.0 392.9 jit_solution(12360723195942460386)
XLA Ops:
  19.4 3.3 gather_fusion.2
  22.7 3.2 broadcast_select_fusion
  25.9 31.6 %all_to_all.20 = bf16[8,64,2048]{2,1,0:T(8,128)(2,1)S(1)} all-to-all(bf16[8,64,2048]{2,1,0:T(8,128)(2,1)S(1)} %get-tuple-element.27), channel_id=1, replica_groups=mesh['dp'=4,'expert'=8] {'expert'}, dimensions={0} | all-to-all | bytes 4194304 | tf_op jit(solution)/shard_map/all_to_all | solution.py:43
  57.5 4.4 %all-to-all-start.2 = ((bf16[8,64,2048]{2,1,0:T(8,128)(2,1)}), bf16[8,64,2048]{2,1,0:T(8,128)(2,1)}, u32[]{:S(2)}, u32[]{:S(2)}) async-start(bf16[8,64,2048]{2,1,0:T(8,128)(2,1)} %get-tuple-element.26), calls=%async_computation.2 | async-start | bytes 4194304 | tf_op jit(solution)/shard_map/all_to_all | solution.py:65
  62.1 13.7 %all-gather.6.cloned.1.call-done = bf16[1,2048,768]{2,1,0:T(8,128)(2,1)} async-done(((bf16[1,512,768]{2,1,0:T(8,128)(2,1)}), bf16[1,2048,768]{2,1,0:T(8,128)(2,1)}) %all-gather.6.cloned.1.call-update) | async-done | bytes 3145744 | tf_op jit(solution)/shard_map/all_gather | solution.py:37
  75.9 4.8 %fusion.6 = f32[512,768]{1,0:T(8,128)} fusion(bf16[512,2048]{1,0:T(8,128)(2,1)S(1)} %bitcast.55, bf16[1,2048,768]{2,1,0:T(8,128)(2,1)} %all-gather.6.cloned.1.call-done), kind=kOutput, calls=%fused_computation.16 | convolution fusion | flops 1610612736 | bytes 6815744 | tf_op jit(solution)/shard_map/dot_general | solution.py:47
  80.7 7.8 %all-to-all-done.2 = bf16[8,64,2048]{2,1,0:T(8,128)(2,1)} async-done(((bf16[8,64,2048]{2,1,0:T(8,128)(2,1)}), bf16[8,64,2048]{2,1,0:T(8,128)(2,1)}, u32[]{:S(2)}, u32[]{:S(2)}) %all-to-all-start.2) | async-done | bytes 2097184 | tf_op jit(solution)/shard_map/all_to_all | solution.py:65
  88.5 51.1 %all-gather.8.cloned.1.call-done = bf16[1,2048,768]{2,1,0:T(8,128)(2,1)} async-done(((bf16[1,512,768]{2,1,0:T(8,128)(2,1)}), bf16[1,2048,768]{2,1,0:T(8,128)(2,1)}) %all-gather.8.cloned.1.call-update) | async-done | bytes 3145744 | tf_op jit(solution)/shard_map/all_gather | solution.py:38
  139.6 5.4 %fusion = f32[512,768]{1,0:T(8,128)} fusion(bf16[512,2048]{1,0:T(8,128)(2,1)} %bitcast.9, bf16[1,2048,768]{2,1,0:T(8,128)(2,1)} %all-gather.8.cloned.1.call-done), kind=kOutput, calls=%fused_computation.10 | convolution fusion | flops 1610612736 | bytes 6815744 | tf_op jit(solution)/shard_map/dot_general | solution.py:78
  145.1 58.3 %all-gather.4.cloned.1.call-done = bf16[1,2048,768]{2,1,0:T(8,128)(2,1)} async-done(((bf16[1,512,768]{2,1,0:T(8,128)(2,1)}), bf16[1,2048,768]{2,1,0:T(8,128)(2,1)}) %all-gather.4.cloned.1.call-update) | async-done | bytes 3145744 | tf_op jit(solution)/shard_map/all_gather | solution.py:36
  203.4 5.1 %multiply_convert_fusion.2 = (bf16[512,768]{1,0:T(8,128)(2,1)S(1)}, bf16[512,768]{1,0:T(8,128)(2,1)S(1)}, bf16[512,768]{1,0:T(8,128)(2,1)S(1)}) fusion(f32[512,768]{1,0:T(8,128)} %fusion, f32[512,768]{1,0:T(8,128)} %fusion.6, bf16[512,2048]{1,0:T(8,128)(2,1)S(1)} %bitcast.56, bf16[1,2048,768]{2,1,0:T(8,128)(2,1)} %all-gather.4.cloned.1.call-done), kind=kOutput, calls=%fused_computation.28 | convolution fusion | flops 1616510976 | bytes 10747904 | tf_op jit(solution)/shard_map/dot_general | solution.py:46
  208.6 4.3 %convolution_convert_fusion = bf16[2048,768]{0,1:T(8,128)(2,1)S(1)} fusion(bf16[512,2048]{1,0:T(8,128)(2,1)} %bitcast.9, bf16[512,768]{1,0:T(8,128)(2,1)S(1)} %get-tuple-element.20), kind=kOutput, calls=%fused_computation.7 | convolution fusion | flops 1612185600 | bytes 6029312 | tf_op jit(solution)/shard_map/dot_general | solution.py:8
  216.6 4.5 %pad_maximum_fusion = bf16[2048,2304]{0,1:T(8,128)(2,1)} fusion(bf16[2048,768]{0,1:T(8,128)(2,1)S(1)} %convolution_convert_fusion, bf16[2048,768]{0,1:T(8,128)(2,1)S(1)} %convolution_convert_fusion.1, bf16[2048,768]{0,1:T(8,128)(2,1)S(1)} %convolution_convert_fusion.2), kind=kLoop, calls=%fused_computation.5 | loop fusion | flops 28311552 | bytes 18874368 | tf_op jit(solution)/shard_map/concatenate | solution.py:96
  222.9 4.3 %fusion.12 = bf16[512,2048]{1,0:T(8,128)(2,1)} fusion(bf16[512,768]{1,0:T(8,128)(2,1)} %copy-done.12, bf16[1,2048,768]{2,1,0:T(8,128)(2,1)S(1)} %copy-done.8), kind=kOutput, calls=%fused_computation.22 | convolution fusion | flops 1611661312 | bytes 6029312 | tf_op jit(solution)/shard_map/dot_general | solution.py:49
  227.2 3.8 all-to-all-start.1
  231.1 4.1 %fusion.4 = f32[512,2048]{1,0:T(8,128)S(1)} fusion(bf16[512,768]{1,0:T(8,128)(2,1)} %copy-done.11, bf16[1,2048,768]{2,1,0:T(8,128)(2,1)} %all-gather.6.cloned.1.call-done), kind=kOutput, calls=%fused_computation.14 | convolution fusion | flops 1610612736 | bytes 8126464 | tf_op jit(solution)/shard_map/dot_general | solution.py:84
  235.2 3.2 add_convert_fusion
  238.4 19.2 %all-to-all-done.1 = bf16[8,64,2048]{2,1,0:T(8,128)(2,1)S(1)} async-done(((bf16[8,64,2048]{2,1,0:T(8,128)(2,1)}), bf16[8,64,2048]{2,1,0:T(8,128)(2,1)S(1)}, u32[]{:S(2)}, u32[]{:S(2)}) %all-to-all-start.1) | async-done | bytes 2097184 | tf_op jit(solution)/shard_map/all_to_all | solution.py:52
  257.5 4.3 %all-to-all-start.3 = ((bf16[8,64,2048]{2,1,0:T(8,128)(2,1)}), bf16[8,64,2048]{2,1,0:T(8,128)(2,1)}, u32[]{:S(2)}, u32[]{:S(2)}) async-start(bf16[8,64,2048]{2,1,0:T(8,128)(2,1)} %bitcast.59), calls=%async_computation.3 | async-start | bytes 4194304 | tf_op jit(solution)/shard_map/all_to_all | solution.py:86
  267.2 21.3 %all-to-all-done.3 = bf16[8,64,2048]{2,1,0:T(8,128)(2,1)} async-done(((bf16[8,64,2048]{2,1,0:T(8,128)(2,1)}), bf16[8,64,2048]{2,1,0:T(8,128)(2,1)}, u32[]{:S(2)}, u32[]{:S(2)}) %all-to-all-start.3) | async-done | bytes 2097184 | tf_op jit(solution)/shard_map/all_to_all | solution.py:86
  288.5 4.2 %gather_fusion.3 = bf16[256,2048]{1,0:T(8,128)(2,1)S(1)} fusion(bf16[512,2048]{1,0:T(8,128)(2,1)} %bitcast.11, s32[1024]{0:T(1024)S(1)} %pad_clamp_fusion.1), kind=kCustom, calls=%fused_computation.3 | custom fusion | bytes 2098176 | tf_op jit(solution)/shard_map/gather | solution.py:93
  293.7 3.6 reduce_sum.22
  297.4 3.9 multiply_reduce_fusion
  301.2 79.9 %reduce-scatter.2.cloned.1.call-done = bf16[512,2304]{0,1:T(8,128)(2,1)} async-done(((bf16[2048,2304]{0,1:T(8,128)(2,1)}), bf16[512,2304]{0,1:T(8,128)(2,1)}) %reduce-scatter.2.cloned.1.call-update) | async-done | bytes 2359312 | tf_op jit(solution)/shard_map/reduce_scatter | solution.py:95
  (62 shorter events, 29.4 us)
Async XLA Ops:
  7.2 7.9 %copy-start = (bf16[128,2048]{1,0:T(8,128)(2,1)S(1)}, bf16[128,2048]{1,0:T(8,128)(2,1)}, u32[]{:S(2)}) copy-start(bf16[128,2048]{1,0:T(8,128)(2,1)} %param.8) | copy-start | bytes 1572868
  7.2 2.3 copy-start.5
  7.2 2.3 copy-start.6
  7.2 4.1 %copy-start.4 = (f32[128,2]{0,1:T(2,128)S(1)}, f32[128,2]{0,1:T(2,128)}, u32[]{:S(2)}) copy-start(f32[128,2]{0,1:T(2,128)} %param.11) | copy-start | bytes 3076
  7.2 4.3 %copy-start.2 = (bf16[128,2048]{1,0:T(8,128)(2,1)S(1)}, bf16[128,2048]{1,0:T(8,128)(2,1)}, u32[]{:S(2)}) copy-start(bf16[128,2048]{1,0:T(8,128)(2,1)} %param.12) | copy-start | bytes 1572868
  7.2 68.6 %all-gather.6.cloned.1.call-start = ((), (), s32[]{:S(2)}) async-start(), calls=%async_computation.6 | async-start | bytes 3932160 | tf_op jit(solution)/shard_map/all_gather | solution.py:37
  8.0 131.7 %all-gather.8.cloned.1.call-start = ((), (), s32[]{:S(2)}) async-start(), calls=%async_computation.7 | async-start | bytes 3932160 | tf_op jit(solution)/shard_map/all_gather | solution.py:38
  8.7 194.7 %all-gather.4.cloned.1.call-start = ((), (), s32[]{:S(2)}) async-start(), calls=%async_computation.5 | async-start | bytes 3932160 | tf_op jit(solution)/shard_map/all_gather | solution.py:36
  57.5 31.0 %all-to-all-start.2 = ((bf16[8,64,2048]{2,1,0:T(8,128)(2,1)}), bf16[8,64,2048]{2,1,0:T(8,128)(2,1)}, u32[]{:S(2)}, u32[]{:S(2)}) async-start(bf16[8,64,2048]{2,1,0:T(8,128)(2,1)} %get-tuple-element.26), calls=%async_computation.2 | async-start | bytes 4194304 | tf_op jit(solution)/shard_map/all_to_all | solution.py:65
  61.9 319.3 %reduce-scatter.2.cloned.1.call-start = ((), (), s32[]{:S(2)}) async-start(), calls=%async_computation.8 | async-start | bytes 11796480 | tf_op jit(solution)/shard_map/reduce_scatter | solution.py:95
  208.5 4.3 %copy-start.12 = (bf16[512,768]{1,0:T(8,128)(2,1)}, bf16[512,768]{1,0:T(8,128)(2,1)S(1)}, u32[]{:S(2)}) copy-start(bf16[512,768]{1,0:T(8,128)(2,1)S(1)} %get-tuple-element.20) | copy-start | bytes 2359300
  208.5 4.3 %copy-start.9 = (bf16[512,768]{1,0:T(8,128)(2,1)}, bf16[512,768]{1,0:T(8,128)(2,1)S(1)}, u32[]{:S(2)}) copy-start(bf16[512,768]{1,0:T(8,128)(2,1)S(1)} %get-tuple-element.18) | copy-start | bytes 2359300
  208.5 6.2 %copy-start.11 = (bf16[512,768]{1,0:T(8,128)(2,1)}, bf16[512,768]{1,0:T(8,128)(2,1)S(1)}, u32[]{:S(2)}) copy-start(bf16[512,768]{1,0:T(8,128)(2,1)S(1)} %get-tuple-element.19) | copy-start | bytes 2359300
  221.0 1.9 copy-start.8
  227.2 30.3 %all-to-all-start.1 = ((bf16[8,64,2048]{2,1,0:T(8,128)(2,1)}), bf16[8,64,2048]{2,1,0:T(8,128)(2,1)S(1)}, u32[]{:S(2)}, u32[]{:S(2)}) async-start(bf16[8,64,2048]{2,1,0:T(8,128)(2,1)} %bitcast.60), calls=%async_computation.1 | async-start | bytes 4194304 | tf_op jit(solution)/shard_map/all_to_all | solution.py:52
  231.0 4.1 %copy-start.7 = (bf16[1,2048,768]{2,1,0:T(8,128)(2,1)S(1)}, bf16[1,2048,768]{2,1,0:T(8,128)(2,1)}, u32[]{:S(2)}) copy-start(bf16[1,2048,768]{2,1,0:T(8,128)(2,1)} %all-gather.4.cloned.1.call-done) | copy-start | bytes 9437188
  231.0 4.1 %copy-start.10 = (bf16[512,768]{1,0:T(8,128)(2,1)S(1)}, bf16[512,768]{1,0:T(8,128)(2,1)}, u32[]{:S(2)}) copy-start(bf16[512,768]{1,0:T(8,128)(2,1)} %copy-done.9) | copy-start | bytes 2359300
  257.5 31.0 %all-to-all-start.3 = ((bf16[8,64,2048]{2,1,0:T(8,128)(2,1)}), bf16[8,64,2048]{2,1,0:T(8,128)(2,1)}, u32[]{:S(2)}, u32[]{:S(2)}) async-start(bf16[8,64,2048]{2,1,0:T(8,128)(2,1)} %bitcast.59), calls=%async_computation.3 | async-start | bytes 4194304 | tf_op jit(solution)/shard_map/all_to_all | solution.py:86
  263.2 1.0 copy-start.3
  382.9 3.5 copy-start.1
Sparse Core Ops, SparseCore 0:
  9.6 66.1 all-gather.5
  77.4 62.1 all-gather.7
  141.2 62.1 all-gather.3
  221.2 159.9 reduce-scatter.1
where the time goes:
time: 394 us; the launch traced here: 393 us
  waiting for transfers between devices  253 us (64%)
  matrix products  37.3 us (9%)
  blocking collectives  31.6 us (8%)
  local copies, waits for them, and re-layouts  26.6 us (7%)
  other arithmetic  17.1 us (4%)
  between operations  14.1 us (4%)
  starting transfers between devices  12.8 us (3%)
    reduce_scatter x1, waiting for transfers between devices, on_device(): lax.psum_scatter(jnp.concatenate([partial_term(flat_rows, grad_gate_pre),...  79.9 us
    all_gather x1, waiting for transfers between devices, on_device(): lax.all_gather(w_gate, 'dp', axis=1, tiled=True)  58.3 us
    all_gather x1, waiting for transfers between devices, on_device(): lax.all_gather(w_down, 'dp', axis=1, tiled=True)  51.1 us
    all_to_all x1, blocking collectives, on_device(): lax.all_to_all(outbound, 'expert', split_axis=0, concat_axis=0, tiled=True)  31.6 us
    all_to_all x1, waiting for transfers between devices, on_device(): lax.all_to_all(input_back.reshape(experts, capacity, model_width), 'exper...  21.3 us
    all_to_all x1, waiting for transfers between devices, on_device(): lax.all_to_all(produced.reshape(experts, slot_count, model_width), 'exper...  19.2 us
    all_gather x1, waiting for transfers between devices, on_device(): lax.all_gather(w_up, 'dp', axis=1, tiled=True)  13.7 us
    dot_general x3, matrix products, partial_term(): lax.dot_general(left_rows, right_rows, (((0,), (0,)), ((), ())), preferre...  7.97 us
  transfers between devices with their start and end apart: 7, of which 7 were waited for; matrix products, arithmetic and copies ran while one was open for 14% of the time, Pallas kernels for 0%

commit v1 on v0

v1 whole, which is shorter than its diff:
```python
import functools

import jax
import jax.numpy as jnp
from jax import lax
from jax.experimental import pallas as pl
from jax.experimental.pallas import tpu as pltpu
from jax.sharding import PartitionSpec as P

UNITS = (2, 2, 2)
BF16 = jnp.bfloat16
F32 = jnp.float32
VMEM_LIMIT = 56 * 2**20
WHOLE = pl.BlockSpec(memory_space=pltpu.VMEM)
SCALAR = pl.BlockSpec(memory_space=pltpu.SMEM)


def dot(a, b, ca, cb):
    return lax.dot_general(a, b, (((ca,), (cb,)), ((), ())), preferred_element_type=F32)


def call(body, name, out_shape, in_specs, flops, moved, **extra):
    return pl.pallas_call(
        body,
        name=name,
        out_shape=out_shape,
        in_specs=in_specs,
        compiler_params=pltpu.CompilerParams(vmem_limit_bytes=VMEM_LIMIT),
        cost_estimate=pl.CostEstimate(flops=flops, bytes_accessed=moved, transcendentals=0),
        **extra,
    )


def after(x, *done):
    return lax.optimization_barrier((x, *done))[0] if done else x


def dispatch_body(n, index_ref, target_ref, gates_ref, tokens_ref, grad_ref, out_ref):
    experts, cap = out_ref.shape[0], out_ref.shape[1] // 2
    top_k, tok_dev = target_ref.shape
    feat = tokens_ref.shape[1] // n
    slots = experts * cap
    slot = lax.broadcasted_iota(jnp.int32, (slots, tok_dev), 0)
    pick = jnp.zeros((slots, tok_dev), F32)
    gate = jnp.zeros((slots, 1), F32)
    for k in range(top_k):
        hit = slot == target_ref[k : k + 1, :]
        pick = pick + jnp.where(hit, 1.0, 0.0)
        gate = gate + jnp.sum(jnp.where(hit, gates_ref[k : k + 1, :], 0.0), axis=1, keepdims=True)
    pick = pick.astype(BF16)
    for m in range(n):
        here = slice(m * feat, (m + 1) * feat)
        from_ = pl.ds(pl.multiple_of(lax.rem(index_ref[0] + m, n) * feat, 128), feat)
        rows = dot(pick, tokens_ref[:, from_], 1, 0).astype(BF16)
        grows = (dot(pick, grad_ref[:, from_], 1, 0) * gate).astype(BF16)
        out_ref[:, :cap, here] = rows.reshape(experts, cap, feat)
        out_ref[:, cap:, here] = grows.reshape(experts, cap, feat)


def dispatch(index, target, gates, tokens, grad_out, experts, cap, n):
    width = tokens.shape[1]
    return call(
        functools.partial(dispatch_body, n),
        "dispatch",
        jax.ShapeDtypeStruct((experts, 2 * cap, width), BF16),
        [SCALAR, WHOLE, WHOLE, WHOLE, WHOLE],
        4 * experts * cap * tokens.shape[0] * width,
        4 * (experts * cap + tokens.shape[0]) * width,
        out_specs=WHOLE,
    )(index, target, gates, tokens, grad_out)


def part_body(n, index_ref, rows_ref, *refs):
    own, above, below = refs[0], refs[1:n], refs[n : 2 * n - 1]
    full_ref, hid_ref, both_ref = refs[2 * n - 1 : 2 * n + 2]
    terms = refs[2 * n + 2 :]
    feat, three = own.shape
    f = three // 3
    experts, cap = rows_ref.shape[0], rows_ref.shape[1] // 2
    slots = experts * cap
    full_ref[:feat] = own[...]
    for m in range(1, n):
        inside = index_ref[0] + m < n

        @pl.when(inside)
        def _():
            full_ref[m * feat : (m + 1) * feat] = above[m - 1][...]

        @pl.when(jnp.logical_not(inside))
        def _():
            full_ref[m * feat : (m + 1) * feat] = below[n - m - 1][...]

    group = max(1, 128 // cap)
    tile = group * cap

    def forward(t, carry):
        at = pl.ds(pl.multiple_of(t * tile, tile), tile)
        of = pl.ds(t * group, group)
        pre = dot(rows_ref[of, :cap, :].reshape(tile, -1), full_ref[:, : 2 * f], 1, 0)
        gate_pre, up_pre = pre[:, :f], pre[:, f:]
        down_back = dot(rows_ref[of, cap:, :].reshape(tile, -1), full_ref[:, 2 * f :], 1, 0)
        sig = jax.nn.sigmoid(gate_pre)
        active = gate_pre * sig
        hid_ref[at, :] = (active * up_pre).astype(BF16)
        slope = sig * (1.0 + gate_pre * (1.0 - sig))
        both_ref[at, :f] = (down_back * up_pre * slope).astype(BF16)
        both_ref[at, f:] = (down_back * active).astype(BF16)
        return carry

    lax.fori_loop(0, slots // tile, forward, 0)
    for m in range(n):
        cols = slice(m * feat, (m + 1) * feat)
        rows = rows_ref[:, :cap, cols].reshape(slots, feat)
        grows = rows_ref[:, cap:, cols].reshape(slots, feat)
        terms[m][:, : 2 * f] = dot(rows, both_ref[...], 0, 0).astype(BF16)
        terms[m][:, 2 * f :] = dot(grows, hid_ref[...], 0, 0).astype(BF16)


def part(index, rows, own, above, below, n):
    feat, three = own.shape
    experts, double, width = rows.shape
    slots = experts * double // 2
    f = three // 3
    sds = jax.ShapeDtypeStruct
    out_shape = [sds((width, three), BF16), sds((slots, f), BF16), sds((slots, 2 * f), BF16)]
    out_shape += [sds((feat, three), BF16)] * n
    res = call(
        functools.partial(part_body, n),
        "part",
        out_shape,
        [SCALAR] + [WHOLE] * (2 * n),
        12 * slots * width * f,
        2 * (2 * slots * width + 3 * width * three),
        out_specs=[WHOLE] * len(out_shape),
    )(index, rows, own, *above, *below)
    return res[0], res[1], res[2], list(res[3:])


def back_body(count, cap, *refs):
    hids, boths, fulls = refs[:count], refs[count : 2 * count], refs[2 * count : 3 * count]
    out_ref = refs[3 * count]
    experts, _, feat = out_ref.shape
    out = back = None
    for hid, both, full in zip(hids, boths, fulls):
        f = hid.shape[1]
        o = dot(hid[...], full[:, 2 * f :], 1, 1)
        b = dot(both[...], full[:, : 2 * f], 1, 1)
        out, back = (o, b) if out is None else (out + o, back + b)
    out_ref[:, :cap, :] = out.astype(BF16).reshape(experts, cap, feat)
    out_ref[:, cap:, :] = back.astype(BF16).reshape(experts, cap, feat)


def back_products(hids, boths, fulls, experts, n):
    count = len(hids)
    slots = hids[0].shape[0]
    cap = slots // experts
    width = fulls[0].shape[0]
    feat = width // n
    ffn = sum(h.shape[1] for h in hids)
    return pl.pallas_call(
        functools.partial(back_body, count, cap),
        name="back_products",
        out_shape=jax.ShapeDtypeStruct((experts, 2 * cap, width), BF16),
        grid=(n,),
        in_specs=[pl.BlockSpec(x.shape, lambda m: (0, 0)) for x in (*hids, *boths)]
        + [pl.BlockSpec((feat, x.shape[1]), lambda m: (m, 0)) for x in fulls],
        out_specs=pl.BlockSpec((experts, 2 * cap, feat), lambda m: (0, 0, m)),
        compiler_params=pltpu.CompilerParams(vmem_limit_bytes=VMEM_LIMIT),
        cost_estimate=pl.CostEstimate(
            flops=6 * slots * width * ffn,
            bytes_accessed=2 * (3 * ffn * width + 2 * slots * width),
            transcendentals=0,
        ),
    )(*hids, *boths, *fulls)


def combine_body(n, index_ref, target_ref, gates_ref, grad_ref, rows_ref, out_ref, dtok_ref, dgate_ref):
    tok_dev, top_k = target_ref.shape
    experts, cap = rows_ref.shape[0], rows_ref.shape[1] // 2
    slots = experts * cap
    feat = rows_ref.shape[2] // n
    slot = lax.broadcasted_iota(jnp.int32, (tok_dev, slots), 1)
    hits = [jnp.where(slot == target_ref[:, k : k + 1], 1.0, 0.0) for k in range(top_k)]
    either = sum(hits).astype(BF16)
    hits = [h.astype(BF16) for h in hits]
    sums = [jnp.zeros((tok_dev, 1), F32) for _ in range(top_k)]
    for m in range(n):
        here = slice(m * feat, (m + 1) * feat)
        to = pl.ds(pl.multiple_of(lax.rem(index_ref[0] + m, n) * feat, 128), feat)
        total = jnp.zeros((tok_dev, feat), F32)
        grad = grad_ref[:, to].astype(F32)
        rows = rows_ref[:, :cap, here].reshape(slots, feat)
        for k in range(top_k):
            picked = dot(hits[k], rows, 1, 0)
            total = total + picked * gates_ref[:, k : k + 1]
            sums[k] = sums[k] + jnp.sum(picked * grad, axis=1, keepdims=True)
        out_ref[:, to] = total.astype(BF16)
        dtok_ref[:, to] = dot(either, rows_ref[:, cap:, here].reshape(slots, feat), 1, 0).astype(BF16)
    for k in range(top_k):
        dgate_ref[:, k : k + 1] = sums[k]


def combine(index, target, gates, grad_out, rows, n):
    shape = jax.ShapeDtypeStruct(grad_out.shape, BF16)
    return call(
        functools.partial(combine_body, n),
        "combine",
        [shape, shape, jax.ShapeDtypeStruct(gates.shape, F32)],
        [SCALAR, WHOLE, WHOLE, WHOLE, WHOLE],
        3 * rows.shape[0] * rows.shape[1] * grad_out.size,
        2 * (rows.size + 3 * grad_out.size),
        out_specs=[WHOLE, WHOLE, WHOLE],
    )(index, target, gates, grad_out, rows)


def gather_step(step, n, up, down):
    return (
        lax.ppermute(up, "dp", [(j, j + 1) for j in range(step - 1, n - 1)]),
        lax.ppermute(down, "dp", [(j, j - 1) for j in range(n - step, 0, -1)]),
    )


def scatter_step(step, n, up, down):
    return (
        lax.ppermute(up, "dp", [(j, j + 1) for j in range(step)]),
        lax.ppermute(down, "dp", [(j, j - 1) for j in range(n - 1, n - 1 - step, -1)]),
    )


def add(a, b):
    return (a.astype(F32) + b.astype(F32)).astype(BF16)


def exchange(rows):
    return lax.all_to_all(rows, "expert", split_axis=0, concat_axis=0, tiled=True)


class Gather:
    def __init__(self, own, n):
        self.own, self.n, self.step = own, n, 0
        self.last = (own, own)
        self.below, self.above = [], []

    def go(self, waits=()):
        self.step += 1
        up, down = (after(x, *waits) for x in self.last)
        self.last = gather_step(self.step, self.n, up, down)
        self.below.append(self.last[0])
        self.above.append(self.last[1])


class Scatter:
    def __init__(self, terms, n):
        self.terms, self.n, self.step = terms, n, 0
        self.last = ()

    def go(self, waits=()):
        terms, n, step = self.terms, self.n, self.step
        if step:
            up, down = add(self.last[0], terms[n - 1 - step]), add(self.last[1], terms[step + 1])
        else:
            up, down = terms[n - 1], terms[1]
        self.step += 1
        self.last = scatter_step(self.step, n, after(up, *waits), after(down, *waits))

    def result(self):
        up, down = self.last
        return (up.astype(F32) + down.astype(F32) + self.terms[0].astype(F32)).astype(BF16)


def on_device(tokens, expert_ids, slot_index, routing_gates, grad_out, w_gate, w_up, w_down):
    tok_dev, top_k = expert_ids.shape
    experts = lax.axis_size("expert")
    n = lax.axis_size("dp")
    index = lax.axis_index("dp").astype(jnp.int32).reshape(1)
    capacity = 2 * tok_dev * top_k // experts
    unit = w_gate.shape[2] // sum(UNITS)
    edges = [sum(UNITS[:c]) * unit for c in range(len(UNITS) + 1)]
    spans = [slice(a, b) for a, b in zip(edges, edges[1:])]
    count = len(spans)

    owns = [jnp.concatenate([w[0, :, s] for w in (w_gate, w_up, w_down)], axis=1) for s in spans]
    target = expert_ids * capacity + slot_index
    if DISPATCH_AFTER_PACK:
        target = after(target, owns[0])
    sent = dispatch(index, target.T, routing_gates.T, tokens, grad_out, experts, capacity, n)

    fulls, hids, boths = [], [], []
    gathers = [Gather(own, n) for own in owns]
    scatters = []

    def run_part(c, waits=()):
        g = gathers[c]
        full, hid, both, terms = part(index, after(rows, *waits), g.own, g.above, g.below, n)
        fulls.append(full)
        hids.append(hid)
        boths.append(both)
        scatters.append(Scatter(terms, n))

    gathers[0].go()
    if EXCHANGE_AFTER_GATHER:
        sent = after(sent, *gathers[0].last)
    rows = exchange(sent)
    for _ in range(n - 2):
        gathers[0].go()
    history = [gathers[0].last]
    for c in range(1, count):
        for step in range(1, n):
            if step == 2:
                run_part(c - 1, PART_WAITS and sum(history[-1:], ()))
            waits = sum(history[-LAG:-LAG + 1 or None], ())
            if step == 2 and GATHER_AFTER_PART:
                waits += (hids[-1],)
            gathers[c].go(waits)
            done = gathers[c].last
            for s in scatters:
                if s.step < n - 1:
                    s.go()
                    done += s.last
            history.append(done)
    run_part(count - 1, TAIL_WAITS and sum(history[-1:], ()))
    old = scatters[-2] if count > 1 else None
    if old is not None:
        while old.step < n - 1:
            old.go()
    if SERIAL_TAIL:
        scatters[-1].go(old.last)
    out = back_products(hids, boths, fulls, experts, n)
    if RETURN_AFTER_SCATTER:
        if not SERIAL_TAIL:
            scatters[-1].go()
        out = after(out, *scatters[-1].last)
    returned = exchange(out)
    for s in scatters:
        while s.step < n - 1:
            s.go()
    grads = [s.result() for s in scatters]

    layer_out, grad_tokens, grad_gates = combine(index, target, routing_gates, grad_out, returned, n)
    stacked = []
    for k in range(3):
        pieces = []
        for s, g in zip(spans, grads):
            f = s.stop - s.start
            pieces.append(g[:, k * f : (k + 1) * f])
        stacked.append(jnp.concatenate(pieces, axis=1)[None])
    return (layer_out, grad_tokens, grad_gates, *stacked)


DISPATCH_AFTER_PACK = True
EXCHANGE_AFTER_GATHER = True
GATHER_AFTER_PART = True
PART_WAITS = ()
TAIL_WAITS = True
SERIAL_TAIL = False
RETURN_AFTER_SCATTER = False
LAG = 1


def solution(mesh):
    in_specs = (P(("dp", "expert"), None),) * 5 + (P("expert", "dp", None),) * 3
    out_specs = (P(("dp", "expert"), None),) * 3 + (P("expert", "dp", None),) * 3
    return jax.shard_map(
        on_device, mesh=mesh, in_specs=in_specs, out_specs=out_specs, check_vma=False
    )
```

time: 394 us -> 313 us (0.79)
  waiting for transfers between devices: 253 us -> 159 us
  starting transfers between devices: 12.8 us -> 84.8 us
  Pallas kernels: 0 us -> 46.6 us
  matrix products: 37.3 us -> 0 us
  blocking collectives: 31.6 us -> 0 us
  local copies, waits for them, and re-layouts: 26.6 us -> 7.9 us
  between operations: 14.1 us -> 1.48 us
  other arithmetic: 17.1 us -> 9.85 us
    ppermute x0 -> x36, waiting for transfers between devices: none -> 159 us  [the longest x9 80.9 us: scatter_step(): lax.ppermute(up, 'dp', [(j, j + 1) for j in range(step)])]
    all_gather x3 -> x0, waiting for transfers between devices: 123 us -> none  [the longest x1 58.3 us: on_device(): lax.all_gather(w_gate, 'dp', axis=1, tiled=True)]
    reduce_scatter x1 -> x0, waiting for transfers between devices: 79.9 us -> none  [on_device(): lax.psum_scatter(jnp.concatenate([partial_term(flat_rows, grad_gate_pre),...]
    ppermute x0 -> x36, starting transfers between devices: none -> 75.6 us  [the longest x9 35.7 us: scatter_step(): lax.ppermute(up, 'dp', [(j, j + 1) for j in range(step)])]
    all_to_all x3 -> x2, waiting for transfers between devices: 48.3 us -> 0.01 us  [exchange(): lax.all_to_all(rows, 'expert', split_axis=0, concat_axis=0, tiled=True)]
    pallas_call x0 -> x6, Pallas kernels: none -> 46.6 us  [the longest x3 27.5 us: part(): call(functools.partial(part_body, n), 'part', out_shape, [SCALAR] + [WHOL...]
    dot_general x10 -> x0, matrix products: 37.3 us -> none  [the longest x3 7.97 us: partial_term(): lax.dot_general(left_rows, right_rows, (((0,), (0,)), ((), ())), preferre...]
    all_to_all x1 -> x0, blocking collectives: 31.6 us -> none  [on_device(): lax.all_to_all(outbound, 'expert', split_axis=0, concat_axis=0, tiled=True)]
  transfers between devices with their start and end apart: 7 -> 38, of which waited for: 7 -> 16; matrix products, arithmetic and copies ran while one was open for 14% -> 4% of each run, Pallas kernels for 0% -> 11%
where the time goes in v1:
time: 313 us; the launch traced here: 310 us
  waiting for transfers between devices  159 us (51%)
  starting transfers between devices  84.8 us (27%)
  Pallas kernels  46.6 us (15%)
  other arithmetic  9.85 us (3%)
  local copies, waits for them, and re-layouts  7.9 us (3%)
    ppermute x9, waiting for transfers between devices, scatter_step(): lax.ppermute(up, 'dp', [(j, j + 1) for j in range(step)])  80.9 us
    ppermute x9, waiting for transfers between devices, gather_step(): lax.ppermute(down, 'dp', [(j, j - 1) for j in range(n - step, 0, -1)])  51.1 us
    ppermute x9, starting transfers between devices, scatter_step(): lax.ppermute(up, 'dp', [(j, j + 1) for j in range(step)])  35.7 us
    pallas_call x3, Pallas kernels, part(): call(functools.partial(part_body, n), 'part', out_shape, [SCALAR] + [WHOL...  27.5 us
    ppermute x9, waiting for transfers between devices, gather_step(): lax.ppermute(up, 'dp', [(j, j + 1) for j in range(step - 1, n - 1)])  27 us
    ppermute x9, starting transfers between devices, gather_step(): lax.ppermute(up, 'dp', [(j, j + 1) for j in range(step - 1, n - 1)])  18.9 us
    ppermute x9, starting transfers between devices, gather_step(): lax.ppermute(down, 'dp', [(j, j - 1) for j in range(n - step, 0, -1)])  11.6 us
    pallas_call x1, Pallas kernels, back_products(): pl.pallas_call(functools.partial(back_body, count, cap), name='back_produ...  9.97 us
  transfers between devices with their start and end apart: 38, of which 16 were waited for; matrix products, arithmetic and copies ran while one was open for 4% of the time, Pallas kernels for 11%

profile of v1, /device:TPU:0, one launch (start us, length us, event | category | flops | bytes accessed | tf_op | source)
XLA Modules:
  0.0 309.6 jit_solution(16005264098289722637)
XLA Ops:
  2.5 5.9 %collective-permute-start = (bf16[512,768]{1,0:T(8,128)(2,1)S(1)}, bf16[512,768]{1,0:T(8,128)(2,1)}, u32[]{:S(2)}, u32[]{:S(2)}) collective-permute-start(bf16[512,768]{1,0:T(8,128)(2,1)S(1)} %pad_maximum_fusion.refs_0_), channel_id=1, source_target_pairs={{0,8},{8,16},{16,24},{1,9},{9,17},{17,25},{2,10},{10,18},{18,26},{... | collective-permute-start | bytes 2359304 | tf_op jit(solution)/shard_map/ppermute | solution.py:218
  15.0 9.1 %collective-permute-done.refs_4_ = bf16[512,768]{1,0:T(8,128)(2,1)} collective-permute-done((bf16[512,768]{1,0:T(8,128)(2,1)S(1)}, bf16[512,768]{1,0:T(8,128)(2,1)}, u32[]{:S(2)}, u32[]{:S(2)}) %collective-permute-start) | collective-permute-done | bytes 786464 | tf_op jit(solution)/shard_map/ppermute | solution.py:218
  24.2 5.1 %collective-permute-done.1.refs_1_ = bf16[512,768]{1,0:T(8,128)(2,1)} collective-permute-done((bf16[512,768]{1,0:T(8,128)(2,1)S(1)}, bf16[512,768]{1,0:T(8,128)(2,1)}, u32[]{:S(2)}, u32[]{:S(2)}) %collective-permute-start.1) | collective-permute-done | bytes 786464 | tf_op jit(solution)/shard_map/ppermute | solution.py:219
  35.9 19.9 %collective-permute-done.2.refs_2_ = bf16[512,768]{1,0:T(8,128)(2,1)S(1)} collective-permute-done((bf16[512,768]{1,0:T(8,128)(2,1)}, bf16[512,768]{1,0:T(8,128)(2,1)S(1)}, u32[]{:S(2)}, u32[]{:S(2)}) %collective-permute-start.2) | collective-permute-done | bytes 786464 | tf_op jit(solution)/shard_map/ppermute | solution.py:219
  57.9 18.9 %collective-permute-done.3.refs_3_ = bf16[512,768]{1,0:T(8,128)(2,1)S(1)} collective-permute-done((bf16[512,768]{1,0:T(8,128)(2,1)S(1)}, bf16[512,768]{1,0:T(8,128)(2,1)S(1)}, u32[]{:S(2)}, u32[]{:S(2)}) %collective-permute-start.3) | collective-permute-done | bytes 786464 | tf_op jit(solution)/shard_map/ppermute | solution.py:219
  78.1 5.5 %collective-permute-start.7 = (bf16[512,768]{1,0:T(8,128)(2,1)S(1)}, bf16[512,768]{1,0:T(8,128)(2,1)}, u32[]{:S(2)}, u32[]{:S(2)}) collective-permute-start(bf16[512,768]{1,0:T(8,128)(2,1)S(1)} %pad_maximum_fusion.1.refs_0_), channel_id=1, source_target_pairs={{0,8},{8,16},{16,24},{1,9},{9,17},{17,25},{2,10},{10,18},{18,26},{... | collective-permute-start | bytes 2359304 | tf_op jit(solution)/shard_map/ppermute | solution.py:218
  83.6 9.2 %part.3 = (bf16[2048,768]{1,0:T(8,128)(2,1)}, bf16[512,256]{1,0:T(8,128)(2,1)}, bf16[512,512]{1,0:T(8,128)(2,1)}, bf16[512,768]{1,0:T(8,128)(2,1)}, bf16[512,768...) custom-call(s32[1]{0:T(128)} %bitcast.index_ref, bf16[8,128,2048]{2,1,0:T(8,128)(2,1)} %all-to-all-done.rows_ref, ...), custom_call_target="tpu_custom_call" | custom-call | flops 3221225472 | bytes 13631488 | tf_op jit(solution)/shard_map/part/pallas_call | solution.py:127
  102.7 12.5 %collective-permute-done.10 = bf16[512,768]{1,0:T(8,128)(2,1)S(1)} collective-permute-done((bf16[512,768]{1,0:T(8,128)(2,1)}, bf16[512,768]{1,0:T(8,128)(2,1)S(1)}, u32[]{:S(2)}, u32[]{:S(2)}) %collective-permute-start.10) | collective-permute-done | bytes 786464 | tf_op jit(solution)/shard_map/ppermute | solution.py:225
  117.5 5.0 %collective-permute-start.14 = (bf16[512,768]{1,0:T(8,128)(2,1)S(1)}, bf16[512,768]{1,0:T(8,128)(2,1)S(1)}, u32[]{:S(2)}, u32[]{:S(2)}) collective-permute-start(bf16[512,768]{1,0:T(8,128)(2,1)S(1)} %get-tuple-element.106), channel_id=1, source_target_pairs={{0,8},{8,16},{1,9},{9,17},{2,10},{10,18},{3,11},{11,19},{4,12},{12... | collective-permute-start | bytes 2359304 | tf_op jit(solution)/shard_map/ppermute | solution.py:225
  126.2 10.9 %collective-permute-done.14 = bf16[512,768]{1,0:T(8,128)(2,1)S(1)} collective-permute-done((bf16[512,768]{1,0:T(8,128)(2,1)S(1)}, bf16[512,768]{1,0:T(8,128)(2,1)S(1)}, u32[]{:S(2)}, u32[]{:S(2)}) %collective-permute-start.14) | collective-permute-done | bytes 786464 | tf_op jit(solution)/shard_map/ppermute | solution.py:225
  137.2 5.9 %collective-permute-start.18 = (bf16[512,768]{1,0:T(8,128)(2,1)S(1)}, bf16[512,768]{1,0:T(8,128)(2,1)S(1)}, u32[]{:S(2)}, u32[]{:S(2)}) collective-permute-start(bf16[512,768]{1,0:T(8,128)(2,1)S(1)} %add_convert_fusion.8), channel_id=1, source_target_pairs={{0,8},{8,16},{16,24},{1,9},{9,17},{17,25},{2,10},{10,18},{18,26},{... | collective-permute-start | bytes 2359304 | tf_op jit(solution)/shard_map/ppermute | solution.py:225
  149.3 9.2 %part.4 = (bf16[2048,768]{1,0:T(8,128)(2,1)}, bf16[512,256]{1,0:T(8,128)(2,1)}, bf16[512,512]{1,0:T(8,128)(2,1)}, bf16[512,768]{1,0:T(8,128)(2,1)}, bf16[512,768...) custom-call(s32[1]{0:T(128)} %bitcast.index_ref, bf16[8,128,2048]{2,1,0:T(8,128)(2,1)} %all-to-all-done.rows_ref, ...), custom_call_target="tpu_custom_call" | custom-call | flops 3221225472 | bytes 13631488 | tf_op jit(solution)/shard_map/part/pallas_call | solution.py:127
  163.8 14.1 %collective-permute-done.16.refs_4_ = bf16[512,768]{1,0:T(8,128)(2,1)S(1)} collective-permute-done((bf16[512,768]{1,0:T(8,128)(2,1)S(1)}, bf16[512,768]{1,0:T(8,128)(2,1)S(1)}, u32[]{:S(2)}, u32[]{:S(2)}) %collective-permute-start.16) | collective-permute-done | bytes 786464 | tf_op jit(solution)/shard_map/ppermute | solution.py:218
  180.0 11.3 %collective-permute-done.22 = bf16[512,768]{1,0:T(8,128)(2,1)S(1)} collective-permute-done((bf16[512,768]{1,0:T(8,128)(2,1)}, bf16[512,768]{1,0:T(8,128)(2,1)S(1)}, u32[]{:S(2)}, u32[]{:S(2)}) %collective-permute-start.22) | collective-permute-done | bytes 786464 | tf_op jit(solution)/shard_map/ppermute | solution.py:225
  200.1 10.4 %collective-permute-done.26 = bf16[512,768]{1,0:T(8,128)(2,1)S(1)} collective-permute-done((bf16[512,768]{1,0:T(8,128)(2,1)S(1)}, bf16[512,768]{1,0:T(8,128)(2,1)S(1)}, u32[]{:S(2)}, u32[]{:S(2)}) %collective-permute-start.26) | collective-permute-done | bytes 786464 | tf_op jit(solution)/shard_map/ppermute | solution.py:225
  217.5 9.2 %part.5 = (bf16[2048,768]{1,0:T(8,128)(2,1)}, bf16[512,256]{1,0:T(8,128)(2,1)}, bf16[512,512]{1,0:T(8,128)(2,1)}, bf16[512,768]{1,0:T(8,128)(2,1)}, bf16[512,768...) custom-call(s32[1]{0:T(128)} %bitcast.index_ref, bf16[8,128,2048]{2,1,0:T(8,128)(2,1)} %all-to-all-done.rows_ref, ...), custom_call_target="tpu_custom_call" | custom-call | flops 3221225472 | bytes 13631488 | tf_op jit(solution)/shard_map/part/pallas_call | solution.py:127
  230.5 10.0 %back_products.1 = bf16[8,128,2048]{2,1,0:T(8,128)(2,1)} custom-call(bf16[512,256]{1,0:T(8,128)(2,1)} %get-tuple-element.45.refs_0_, bf16[512,256]{1,0:T(8,128)(2,1)} %get-tuple-element.53.refs_1_, bf16[512,256]{1,0:T(8,128)(2,1)} %get-tuple-element.64.refs_2_, bf16[512,512]{1,0:T(8,128)(2,1)} %get-tuple-element.65.refs_3_, ...), custom_call_target="tpu_custom_call" | custom-call | flops 4831838208 | bytes 13631488 | tf_op jit(solution)/shard_map/back_products/pallas_call | solution.py:160
  240.5 4.7 %all-to-all-start.1 = ((bf16[8,128,2048]{2,1,0:T(8,128)(2,1)}), bf16[8,128,2048]{2,1,0:T(8,128)(2,1)}, u32[]{:S(2)}, u32[]{:S(2)}) async-start(bf16[8,128,2048]{2,1,0:T(8,128)(2,1)} %back_products.1), calls=%async_computation.1 | async-start | bytes 8388608 | tf_op jit(solution)/shard_map/all_to_all | solution.py:235
  250.7 5.2 %collective-permute-start.28 = (bf16[512,768]{1,0:T(8,128)(2,1)S(1)}, bf16[512,768]{1,0:T(8,128)(2,1)S(1)}, u32[]{:S(2)}, u32[]{:S(2)}) collective-permute-start(bf16[512,768]{1,0:T(8,128)(2,1)S(1)} %add_convert_fusion.5), channel_id=1, source_target_pairs={{0,8},{8,16},{16,24},{1,9},{9,17},{17,25},{2,10},{10,18},{18,26},{... | collective-permute-start | bytes 2359304 | tf_op jit(solution)/shard_map/ppermute | solution.py:225
  257.6 9.4 %collective-permute-done.31 = bf16[512,768]{1,0:T(8,128)(2,1)S(1)} collective-permute-done((bf16[512,768]{1,0:T(8,128)(2,1)S(1)}, bf16[512,768]{1,0:T(8,128)(2,1)S(1)}, u32[]{:S(2)}, u32[]{:S(2)}) %collective-permute-start.31) | collective-permute-done | bytes 786464 | tf_op jit(solution)/shard_map/ppermute | solution.py:225
  267.2 4.9 %collective-permute-start.32 = (bf16[512,768]{1,0:T(8,128)(2,1)S(1)}, bf16[512,768]{1,0:T(8,128)(2,1)S(1)}, u32[]{:S(2)}, u32[]{:S(2)}) collective-permute-start(bf16[512,768]{1,0:T(8,128)(2,1)S(1)} %add_convert_fusion.2), channel_id=1, source_target_pairs={{0,8},{8,16},{16,24},{1,9},{9,17},{17,25},{2,10},{10,18},{18,26},{... | collective-permute-start | bytes 2359304 | tf_op jit(solution)/shard_map/ppermute | solution.py:225
  273.7 10.1 %collective-permute-done.28 = bf16[512,768]{1,0:T(8,128)(2,1)S(1)} collective-permute-done((bf16[512,768]{1,0:T(8,128)(2,1)S(1)}, bf16[512,768]{1,0:T(8,128)(2,1)S(1)}, u32[]{:S(2)}, u32[]{:S(2)}) %collective-permute-start.28) | collective-permute-done | bytes 786464 | tf_op jit(solution)/shard_map/ppermute | solution.py:225
  284.2 16.2 %collective-permute-done.32 = bf16[512,768]{1,0:T(8,128)(2,1)S(1)} collective-permute-done((bf16[512,768]{1,0:T(8,128)(2,1)S(1)}, bf16[512,768]{1,0:T(8,128)(2,1)S(1)}, u32[]{:S(2)}, u32[]{:S(2)}) %collective-permute-start.32) | collective-permute-done | bytes 786464 | tf_op jit(solution)/shard_map/ppermute | solution.py:225
  303.5 4.6 %combine.1 = (bf16[128,2048]{1,0:T(8,128)(2,1)}, bf16[128,2048]{1,0:T(8,128)(2,1)}, f32[128,2]{1,0:T(8,128)}) custom-call(s32[1]{0:T(128)} %bitcast.index_ref, s32[128,2]{1,0:T(8,128)} %copy-done.17, f32[128,2]{1,0:T(8,128)} %copy.23.gates_ref, bf16[128,2048]{1,0:T(8,128)(2,1)} %grad_ref.3, bf16[8,128,2048]{2,1,0:T(8,128)(2,1)} %all-to-all-done.1.rows_ref), custom_call_target="tpu_custom_call" | custom-call | flops 805306368 | bytes 5767168 | tf_op jit(solution)/shard_map/combine/pallas_call | solution.py:205
  (160 shorter events, 80.9 us)
Async XLA Ops:
  2.5 21.7 %collective-permute-start = (bf16[512,768]{1,0:T(8,128)(2,1)S(1)}, bf16[512,768]{1,0:T(8,128)(2,1)}, u32[]{:S(2)}, u32[]{:S(2)}) collective-permute-start(bf16[512,768]{1,0:T(8,128)(2,1)S(1)} %pad_maximum_fusion.refs_0_), channel_id=1, source_target_pairs={{0,8},{8,16},{16,24},{1,9},{9,17},{17,25},{2,10},{10,18},{18,26},{... | collective-permute-start | bytes 2359304 | tf_op jit(solution)/shard_map/ppermute | solution.py:218
  8.3 21.0 %collective-permute-start.1 = (bf16[512,768]{1,0:T(8,128)(2,1)S(1)}, bf16[512,768]{1,0:T(8,128)(2,1)}, u32[]{:S(2)}, u32[]{:S(2)}) collective-permute-start(bf16[512,768]{1,0:T(8,128)(2,1)S(1)} %pad_maximum_fusion.refs_0_), channel_id=1, source_target_pairs={{24,16},{16,8},{8,0},{25,17},{17,9},{9,1},{26,18},{18,10},{10,2},{... | collective-permute-start | bytes 2359304 | tf_op jit(solution)/shard_map/ppermute | solution.py:219
  29.3 54.3 %all-to-all-start = ((bf16[8,128,2048]{2,1,0:T(8,128)(2,1)}), bf16[8,128,2048]{2,1,0:T(8,128)(2,1)}, u32[]{:S(2)}, u32[]{:S(2)}) async-start(bf16[8,128,2048]{2,1,0:T(8,128)(2,1)} %dispatch.1), calls=%async_computation | async-start | bytes 8388608 | tf_op jit(solution)/shard_map/all_to_all | solution.py:235
  33.9 21.9 %collective-permute-start.2 = (bf16[512,768]{1,0:T(8,128)(2,1)}, bf16[512,768]{1,0:T(8,128)(2,1)S(1)}, u32[]{:S(2)}, u32[]{:S(2)}) collective-permute-start(bf16[512,768]{1,0:T(8,128)(2,1)} %collective-permute-done.1.refs_1_), channel_id=1, source_target_pairs={{16,8},{8,0},{17,9},{9,1},{18,10},{10,2},{19,11},{11,3},{20,12},{1... | collective-permute-start | bytes 2359304 | tf_op jit(solution)/shard_map/ppermute | solution.py:219
  35.2 21.9 %collective-permute-start.4 = (bf16[512,768]{1,0:T(8,128)(2,1)}, bf16[512,768]{1,0:T(8,128)(2,1)S(1)}, u32[]{:S(2)}, u32[]{:S(2)}) collective-permute-start(bf16[512,768]{1,0:T(8,128)(2,1)} %collective-permute-done.refs_4_), channel_id=1, source_target_pairs={{8,16},{16,24},{9,17},{17,25},{10,18},{18,26},{11,19},{19,27},{12,... | collective-permute-start | bytes 2359304 | tf_op jit(solution)/shard_map/ppermute | solution.py:218
  55.8 21.0 %collective-permute-start.3 = (bf16[512,768]{1,0:T(8,128)(2,1)S(1)}, bf16[512,768]{1,0:T(8,128)(2,1)S(1)}, u32[]{:S(2)}, u32[]{:S(2)}) collective-permute-start(bf16[512,768]{1,0:T(8,128)(2,1)S(1)} %collective-permute-done.2.refs_2_), channel_id=1, source_target_pairs={{8,0},{9,1},{10,2},{11,3},{12,4},{13,5},{14,6},{15,7}} | collective-permute-start | bytes 2359304 | tf_op jit(solution)/shard_map/ppermute | solution.py:219
  78.1 22.5 %collective-permute-start.7 = (bf16[512,768]{1,0:T(8,128)(2,1)S(1)}, bf16[512,768]{1,0:T(8,128)(2,1)}, u32[]{:S(2)}, u32[]{:S(2)}) collective-permute-start(bf16[512,768]{1,0:T(8,128)(2,1)S(1)} %pad_maximum_fusion.1.refs_0_), channel_id=1, source_target_pairs={{0,8},{8,16},{16,24},{1,9},{9,17},{17,25},{2,10},{10,18},{18,26},{... | collective-permute-start | bytes 2359304 | tf_op jit(solution)/shard_map/ppermute | solution.py:218
  92.8 22.4 %collective-permute-start.10 = (bf16[512,768]{1,0:T(8,128)(2,1)}, bf16[512,768]{1,0:T(8,128)(2,1)S(1)}, u32[]{:S(2)}, u32[]{:S(2)}) collective-permute-start(bf16[512,768]{1,0:T(8,128)(2,1)} %get-tuple-element.49), channel_id=1, source_target_pairs={{0,8},{1,9},{2,10},{3,11},{4,12},{5,13},{6,14},{7,15}} | collective-permute-start | bytes 2359304 | tf_op jit(solution)/shard_map/ppermute | solution.py:225
  100.6 21.9 %collective-permute-start.9 = (bf16[512,768]{1,0:T(8,128)(2,1)}, bf16[512,768]{1,0:T(8,128)(2,1)S(1)}, u32[]{:S(2)}, u32[]{:S(2)}) collective-permute-start(bf16[512,768]{1,0:T(8,128)(2,1)} %collective-permute-done.7.refs_4_), channel_id=1, source_target_pairs={{8,16},{16,24},{9,17},{17,25},{10,18},{18,26},{11,19},{19,27},{12,... | collective-permute-start | bytes 2359304 | tf_op jit(solution)/shard_map/ppermute | solution.py:218
  101.4 21.2 %collective-permute-start.8 = (bf16[512,768]{1,0:T(8,128)(2,1)S(1)}, bf16[512,768]{1,0:T(8,128)(2,1)S(1)}, u32[]{:S(2)}, u32[]{:S(2)}) collective-permute-start(bf16[512,768]{1,0:T(8,128)(2,1)S(1)} %collective-permute-done.6.refs_1_), channel_id=1, source_target_pairs={{16,8},{8,0},{17,9},{9,1},{18,10},{10,2},{19,11},{11,3},{20,12},{1... | collective-permute-start | bytes 2359304 | tf_op jit(solution)/shard_map/ppermute | solution.py:219
  122.5 20.6 %collective-permute-start.13 = (bf16[512,768]{1,0:T(8,128)(2,1)S(1)}, bf16[512,768]{1,0:T(8,128)(2,1)S(1)}, u32[]{:S(2)}, u32[]{:S(2)}) collective-permute-start(bf16[512,768]{1,0:T(8,128)(2,1)S(1)} %collective-permute-done.9.refs_5_), channel_id=1, source_target_pairs={{16,24},{17,25},{18,26},{19,27},{20,28},{21,29},{22,30},{23,31}} | collective-permute-start | bytes 2359304 | tf_op jit(solution)/shard_map/ppermute | solution.py:218
  123.3 21.4 %collective-permute-start.12 = (bf16[512,768]{1,0:T(8,128)(2,1)S(1)}, bf16[512,768]{1,0:T(8,128)(2,1)S(1)}, u32[]{:S(2)}, u32[]{:S(2)}) collective-permute-start(bf16[512,768]{1,0:T(8,128)(2,1)S(1)} %collective-permute-done.8.refs_2_), channel_id=1, source_target_pairs={{8,0},{9,1},{10,2},{11,3},{12,4},{13,5},{14,6},{15,7}} | collective-permute-start | bytes 2359304 | tf_op jit(solution)/shard_map/ppermute | solution.py:219
  124.8 38.3 %collective-permute-start.19 = (bf16[512,768]{1,0:T(8,128)(2,1)S(1)}, bf16[512,768]{1,0:T(8,128)(2,1)S(1)}, u32[]{:S(2)}, u32[]{:S(2)}) collective-permute-start(bf16[512,768]{1,0:T(8,128)(2,1)S(1)} %add_convert_fusion.7), channel_id=1, source_target_pairs={{24,16},{16,8},{8,0},{25,17},{17,9},{9,1},{26,18},{18,10},{10,2},{... | collective-permute-start | bytes 2359304 | tf_op jit(solution)/shard_map/ppermute | solution.py:226
  137.2 26.6 %collective-permute-start.18 = (bf16[512,768]{1,0:T(8,128)(2,1)S(1)}, bf16[512,768]{1,0:T(8,128)(2,1)S(1)}, u32[]{:S(2)}, u32[]{:S(2)}) collective-permute-start(bf16[512,768]{1,0:T(8,128)(2,1)S(1)} %add_convert_fusion.8), channel_id=1, source_target_pairs={{0,8},{8,16},{16,24},{1,9},{9,17},{17,25},{2,10},{10,18},{18,26},{... | collective-permute-start | bytes 2359304 | tf_op jit(solution)/shard_map/ppermute | solution.py:225
  144.7 33.2 %collective-permute-start.16 = (bf16[512,768]{1,0:T(8,128)(2,1)S(1)}, bf16[512,768]{1,0:T(8,128)(2,1)S(1)}, u32[]{:S(2)}, u32[]{:S(2)}) collective-permute-start(bf16[512,768]{1,0:T(8,128)(2,1)S(1)} %pad_maximum_fusion.2.refs_0_), channel_id=1, source_target_pairs={{0,8},{8,16},{16,24},{1,9},{9,17},{17,25},{2,10},{10,18},{18,26},{... | collective-permute-start | bytes 2359304 | tf_op jit(solution)/shard_map/ppermute | solution.py:218
  148.0 29.9 %collective-permute-start.17 = (bf16[512,768]{1,0:T(8,128)(2,1)S(1)}, bf16[512,768]{1,0:T(8,128)(2,1)S(1)}, u32[]{:S(2)}, u32[]{:S(2)}) collective-permute-start(bf16[512,768]{1,0:T(8,128)(2,1)S(1)} %pad_maximum_fusion.2.refs_0_), channel_id=1, source_target_pairs={{24,16},{16,8},{8,0},{25,17},{17,9},{9,1},{26,18},{18,10},{10,2},{... | collective-permute-start | bytes 2359304 | tf_op jit(solution)/shard_map/ppermute | solution.py:219
  158.5 32.8 %collective-permute-start.22 = (bf16[512,768]{1,0:T(8,128)(2,1)}, bf16[512,768]{1,0:T(8,128)(2,1)S(1)}, u32[]{:S(2)}, u32[]{:S(2)}) collective-permute-start(bf16[512,768]{1,0:T(8,128)(2,1)} %get-tuple-element.58), channel_id=1, source_target_pairs={{0,8},{1,9},{2,10},{3,11},{4,12},{5,13},{6,14},{7,15}} | collective-permute-start | bytes 2359304 | tf_op jit(solution)/shard_map/ppermute | solution.py:225
  163.1 28.2 %collective-permute-start.23 = (bf16[512,768]{1,0:T(8,128)(2,1)}, bf16[512,768]{1,0:T(8,128)(2,1)S(1)}, u32[]{:S(2)}, u32[]{:S(2)}) collective-permute-start(bf16[512,768]{1,0:T(8,128)(2,1)} %get-tuple-element.59), channel_id=1, source_target_pairs={{24,16},{25,17},{26,18},{27,19},{28,20},{29,21},{30,22},{31,23}} | collective-permute-start | bytes 2359304 | tf_op jit(solution)/shard_map/ppermute | solution.py:226
  240.5 63.0 %all-to-all-start.1 = ((bf16[8,128,2048]{2,1,0:T(8,128)(2,1)}), bf16[8,128,2048]{2,1,0:T(8,128)(2,1)}, u32[]{:S(2)}, u32[]{:S(2)}) async-start(bf16[8,128,2048]{2,1,0:T(8,128)(2,1)} %back_products.1), calls=%async_computation.1 | async-start | bytes 8388608 | tf_op jit(solution)/shard_map/all_to_all | solution.py:235
  249.5 22.6 %collective-permute-start.34 = (bf16[512,768]{1,0:T(8,128)(2,1)S(1)}, bf16[512,768]{1,0:T(8,128)(2,1)S(1)}, u32[]{:S(2)}, u32[]{:S(2)}) collective-permute-start(bf16[512,768]{1,0:T(8,128)(2,1)S(1)} %get-tuple-element.102), channel_id=1, source_target_pairs={{24,16},{16,8},{25,17},{17,9},{26,18},{18,10},{27,19},{19,11},{28,... | collective-permute-start | bytes 2359304 | tf_op jit(solution)/shard_map/ppermute | solution.py:226
  250.7 33.1 %collective-permute-start.28 = (bf16[512,768]{1,0:T(8,128)(2,1)S(1)}, bf16[512,768]{1,0:T(8,128)(2,1)S(1)}, u32[]{:S(2)}, u32[]{:S(2)}) collective-permute-start(bf16[512,768]{1,0:T(8,128)(2,1)S(1)} %add_convert_fusion.5), channel_id=1, source_target_pairs={{0,8},{8,16},{16,24},{1,9},{9,17},{17,25},{2,10},{10,18},{18,26},{... | collective-permute-start | bytes 2359304 | tf_op jit(solution)/shard_map/ppermute | solution.py:225
  256.2 27.7 %collective-permute-start.29 = (bf16[512,768]{1,0:T(8,128)(2,1)S(1)}, bf16[512,768]{1,0:T(8,128)(2,1)S(1)}, u32[]{:S(2)}, u32[]{:S(2)}) collective-permute-start(bf16[512,768]{1,0:T(8,128)(2,1)S(1)} %add_convert_fusion.4), channel_id=1, source_target_pairs={{24,16},{16,8},{8,0},{25,17},{17,9},{9,1},{26,18},{18,10},{10,2},{... | collective-permute-start | bytes 2359304 | tf_op jit(solution)/shard_map/ppermute | solution.py:226
  267.2 33.2 %collective-permute-start.32 = (bf16[512,768]{1,0:T(8,128)(2,1)S(1)}, bf16[512,768]{1,0:T(8,128)(2,1)S(1)}, u32[]{:S(2)}, u32[]{:S(2)}) collective-permute-start(bf16[512,768]{1,0:T(8,128)(2,1)S(1)} %add_convert_fusion.2), channel_id=1, source_target_pairs={{0,8},{8,16},{16,24},{1,9},{9,17},{17,25},{2,10},{10,18},{18,26},{... | collective-permute-start | bytes 2359304 | tf_op jit(solution)/shard_map/ppermute | solution.py:225
  272.3 28.0 %collective-permute-start.35 = (bf16[512,768]{1,0:T(8,128)(2,1)S(1)}, bf16[512,768]{1,0:T(8,128)(2,1)S(1)}, u32[]{:S(2)}, u32[]{:S(2)}) collective-permute-start(bf16[512,768]{1,0:T(8,128)(2,1)S(1)} %add_convert_fusion.1), channel_id=1, source_target_pairs={{24,16},{16,8},{8,0},{25,17},{17,9},{9,1},{26,18},{18,10},{10,2},{... | collective-permute-start | bytes 2359304 | tf_op jit(solution)/shard_map/ppermute | solution.py:226
  (50 other events, 610.4 us)

commit v2 on v1

--- a/solution.py
+++ b/solution.py
@@ -10,7 +10,7 @@
 UNITS = (2, 2, 2)
 BF16 = jnp.bfloat16
 F32 = jnp.float32
-VMEM_LIMIT = 56 * 2**20
+VMEM_LIMIT = 18 * 2**20
 WHOLE = pl.BlockSpec(memory_space=pltpu.VMEM)
 SCALAR = pl.BlockSpec(memory_space=pltpu.SMEM)
 
@@ -70,7 +70,7 @@
     )(index, target, gates, tokens, grad_out)
 
 
-def part_body(n, index_ref, rows_ref, *refs):
+def part_body(n, split, index_ref, rows_ref, *refs):
     own, above, below = refs[0], refs[1:n], refs[n : 2 * n - 1]
     full_ref, hid_ref, both_ref = refs[2 * n - 1 : 2 * n + 2]
     terms = refs[2 * n + 2 :]
@@ -112,20 +112,27 @@
         cols = slice(m * feat, (m + 1) * feat)
         rows = rows_ref[:, :cap, cols].reshape(slots, feat)
         grows = rows_ref[:, cap:, cols].reshape(slots, feat)
-        terms[m][:, : 2 * f] = dot(rows, both_ref[...], 0, 0).astype(BF16)
-        terms[m][:, 2 * f :] = dot(grows, hid_ref[...], 0, 0).astype(BF16)
-
-
-def part(index, rows, own, above, below, n):
+        inner = dot(rows, both_ref[...], 0, 0).astype(BF16)
+        outer = dot(grows, hid_ref[...], 0, 0).astype(BF16)
+        if split:
+            terms[m][...] = inner
+            terms[n + m][...] = outer
+        else:
+            terms[m][:, : 2 * f] = inner
+            terms[m][:, 2 * f :] = outer
+
+
+def part(index, rows, own, above, below, n, split=False):
     feat, three = own.shape
     experts, double, width = rows.shape
     slots = experts * double // 2
     f = three // 3
     sds = jax.ShapeDtypeStruct
     out_shape = [sds((width, three), BF16), sds((slots, f), BF16), sds((slots, 2 * f), BF16)]
-    out_shape += [sds((feat, three), BF16)] * n
+    for columns in (2 * f, f) if split else (three,):
+        out_shape += [sds((feat, columns), BF16)] * n
     res = call(
-        functools.partial(part_body, n),
+        functools.partial(part_body, n, split),
         "part",
         out_shape,
         [SCALAR] + [WHOLE] * (2 * n),
@@ -291,11 +298,12 @@
 
     def run_part(c, waits=()):
         g = gathers[c]
-        full, hid, both, terms = part(index, after(rows, *waits), g.own, g.above, g.below, n)
+        split = SPLIT_LAST and c == count - 1
+        full, hid, both, terms = part(index, after(rows, *waits), g.own, g.above, g.below, n, split)
         fulls.append(full)
         hids.append(hid)
         boths.append(both)
-        scatters.append(Scatter(terms, n))
+        scatters.append([Scatter(terms[k * n : (k + 1) * n], n) for k in range(1 + split)])
 
     gathers[0].go()
     if EXCHANGE_AFTER_GATHER:
@@ -307,53 +315,62 @@
     for c in range(1, count):
         for step in range(1, n):
             if step == 2:
-                run_part(c - 1, PART_WAITS and sum(history[-1:], ()))
+                run_part(c - 1)
             waits = sum(history[-LAG:-LAG + 1 or None], ())
+            if step == 1 and c == 1 and EARLY:
+                waits = (gathers[0].below[-2], gathers[0].above[-2])
             if step == 2 and GATHER_AFTER_PART:
                 waits += (hids[-1],)
             gathers[c].go(waits)
             done = gathers[c].last
-            for s in scatters:
+            for (s,) in scatters:
                 if s.step < n - 1:
                     s.go()
                     done += s.last
             history.append(done)
     run_part(count - 1, TAIL_WAITS and sum(history[-1:], ()))
-    old = scatters[-2] if count > 1 else None
-    if old is not None:
-        while old.step < n - 1:
-            old.go()
+    old = scatters[-2][0]
+    while old.step < n - 1:
+        old.go()
     if SERIAL_TAIL:
-        scatters[-1].go(old.last)
+        scatters[-1][0].go(old.last)
     out = back_products(hids, boths, fulls, experts, n)
-    if RETURN_AFTER_SCATTER:
-        if not SERIAL_TAIL:
-            scatters[-1].go()
-        out = after(out, *scatters[-1].last)
+    if RETURN_AFTER == 1:
+        out = after(out, *old.last)
+    if RETURN_AFTER == 2:
+        scatters[-1][0].go()
+        out = after(out, *scatters[-1][0].last)
     returned = exchange(out)
-    for s in scatters:
-        while s.step < n - 1:
-            s.go()
-    grads = [s.result() for s in scatters]
-
+    for _ in range(n - 1):
+        for s in scatters[-1]:
+            if s.step < n - 1:
+                s.go()
     layer_out, grad_tokens, grad_gates = combine(index, target, routing_gates, grad_out, returned, n)
+    if COMBINE_EARLY:
+        for s in scatters[-1]:
+            s.last = tuple(after(x, layer_out) for x in s.last)
+    grads = [[s.result() for s in group] for group in scatters]
     stacked = []
     for k in range(3):
         pieces = []
         for s, g in zip(spans, grads):
             f = s.stop - s.start
-            pieces.append(g[:, k * f : (k + 1) * f])
+            pieces.append(
+                g[k // 2][:, (k % 2) * f : (k % 2 + 1) * f] if len(g) == 2 else g[0][:, k * f : (k + 1) * f]
+            )
         stacked.append(jnp.concatenate(pieces, axis=1)[None])
     return (layer_out, grad_tokens, grad_gates, *stacked)
 
 
+EARLY = False
+SPLIT_LAST = False
+COMBINE_EARLY = False
+RETURN_AFTER = 1
 DISPATCH_AFTER_PACK = True
 EXCHANGE_AFTER_GATHER = True
 GATHER_AFTER_PART = True
-PART_WAITS = ()
 TAIL_WAITS = True
 SERIAL_TAIL = False
-RETURN_AFTER_SCATTER = False
 LAG = 1
 
 

time: 313 us -> 305 us (0.974)
  Pallas kernels: 46.6 us -> 33.3 us
  local copies, waits for them, and re-layouts: 7.9 us -> 17.2 us
  waiting for transfers between devices: 159 us -> 151 us
  other arithmetic: 9.85 us -> 15.3 us
    ppermute x9, waiting for transfers between devices: 27 us -> 12.3 us  [gather_step(): lax.ppermute(up, 'dp', [(j, j + 1) for j in range(step - 1, n - 1)])]
    unnamed x75 -> x53, local copies, waits for them, and re-layouts: 5.61 us -> 14 us
    pallas_call x3, Pallas kernels: 27.5 us -> 21.7 us  [part(): call(functools.partial(part_body, n, split), 'part', out_shape, [SCALAR]...]
    ppermute x9, waiting for transfers between devices: 0.02 us -> 5.75 us  [scatter_step(): lax.ppermute(down, 'dp', [(j, j - 1) for j in range(n - 1, n - 1 - step,...]
    pallas_call x1, Pallas kernels: 9.97 us -> 5.97 us  [back_products(): pl.pallas_call(functools.partial(back_body, count, cap), name='back_produ...]
    pallas_call x1, Pallas kernels: 4.51 us -> 1.26 us  [dispatch(): call(functools.partial(dispatch_body, n), 'dispatch', jax.ShapeDtypeStruc...]
  transfers between devices with their start and end apart: 38 -> 38, of which waited for: 16 -> 16; matrix products, arithmetic and copies ran while one was open for 4% -> 5% of each run, Pallas kernels for 11% -> 10%
where the time goes in v2:
time: 305 us; the launch traced here: 303 us
  waiting for transfers between devices  151 us (50%)
  starting transfers between devices  85.8 us (28%)
  Pallas kernels  33.3 us (11%)
  local copies, waits for them, and re-layouts  17.2 us (6%)
  other arithmetic  15.3 us (5%)
    ppermute x9, waiting for transfers between devices, scatter_step(): lax.ppermute(up, 'dp', [(j, j + 1) for j in range(step)])  83 us
    ppermute x9, waiting for transfers between devices, gather_step(): lax.ppermute(down, 'dp', [(j, j - 1) for j in range(n - step, 0, -1)])  49.6 us
    ppermute x9, starting transfers between devices, scatter_step(): lax.ppermute(up, 'dp', [(j, j + 1) for j in range(step)])  38.5 us
    pallas_call x3, Pallas kernels, part(): call(functools.partial(part_body, n, split), 'part', out_shape, [SCALAR]...  21.7 us
    ppermute x9, starting transfers between devices, gather_step(): lax.ppermute(up, 'dp', [(j, j + 1) for j in range(step - 1, n - 1)])  16.6 us
    unnamed x53, local copies, waits for them, and re-layouts  14 us
    ppermute x9, waiting for transfers between devices, gather_step(): lax.ppermute(up, 'dp', [(j, j + 1) for j in range(step - 1, n - 1)])  12.3 us
    ppermute x9, starting transfers between devices, gather_step(): lax.ppermute(down, 'dp', [(j, j - 1) for j in range(n - step, 0, -1)])  11.6 us
  transfers between devices with their start and end apart: 38, of which 16 were waited for; matrix products, arithmetic and copies ran while one was open for 5% of the time, Pallas kernels for 10%

profile of v2, /device:TPU:0, one launch (start us, length us, event | category | flops | bytes accessed | tf_op | source)
XLA Modules:
  0.0 303.5 jit_solution(17468035915137783943)
XLA Ops:
  3.7 5.1 %collective-permute-start = (bf16[512,768]{1,0:T(8,128)(2,1)S(1)}, bf16[512,768]{1,0:T(8,128)(2,1)S(1)}, u32[]{:S(2)}, u32[]{:S(2)}) collective-permute-start(bf16[512,768]{1,0:T(8,128)(2,1)S(1)} %pad_maximum_fusion.refs_0_), channel_id=1, source_target_pairs={{0,8},{8,16},{16,24},{1,9},{9,17},{17,25},{2,10},{10,18},{18,26},{... | collective-permute-start | bytes 2359304 | tf_op jit(solution)/shard_map/ppermute | solution.py:225
  15.2 10.3 %collective-permute-done.refs_4_ = bf16[512,768]{1,0:T(8,128)(2,1)S(1)} collective-permute-done((bf16[512,768]{1,0:T(8,128)(2,1)S(1)}, bf16[512,768]{1,0:T(8,128)(2,1)S(1)}, u32[]{:S(2)}, u32[]{:S(2)}) %collective-permute-start) | collective-permute-done | bytes 786464 | tf_op jit(solution)/shard_map/ppermute | solution.py:225
  36.4 19.9 %collective-permute-done.2.refs_2_ = bf16[512,768]{1,0:T(8,128)(2,1)S(1)} collective-permute-done((bf16[512,768]{1,0:T(8,128)(2,1)}, bf16[512,768]{1,0:T(8,128)(2,1)S(1)}, u32[]{:S(2)}, u32[]{:S(2)}) %collective-permute-start.2) | collective-permute-done | bytes 786464 | tf_op jit(solution)/shard_map/ppermute | solution.py:226
  58.4 18.9 %collective-permute-done.3.refs_3_ = bf16[512,768]{1,0:T(8,128)(2,1)S(1)} collective-permute-done((bf16[512,768]{1,0:T(8,128)(2,1)S(1)}, bf16[512,768]{1,0:T(8,128)(2,1)S(1)}, u32[]{:S(2)}, u32[]{:S(2)}) %collective-permute-start.3) | collective-permute-done | bytes 786464 | tf_op jit(solution)/shard_map/ppermute | solution.py:226
  80.4 5.4 %collective-permute-start.7 = (bf16[512,768]{1,0:T(8,128)(2,1)S(1)}, bf16[512,768]{1,0:T(8,128)(2,1)}, u32[]{:S(2)}, u32[]{:S(2)}) collective-permute-start(bf16[512,768]{1,0:T(8,128)(2,1)S(1)} %pad_maximum_fusion.1.refs_0_), channel_id=1, source_target_pairs={{0,8},{8,16},{16,24},{1,9},{9,17},{17,25},{2,10},{10,18},{18,26},{... | collective-permute-start | bytes 2359304 | tf_op jit(solution)/shard_map/ppermute | solution.py:225
  91.5 6.9 %part.3 = (bf16[2048,768]{1,0:T(8,128)(2,1)S(1)}, bf16[512,256]{1,0:T(8,128)(2,1)S(1)}, bf16[512,512]{1,0:T(8,128)(2,1)S(1)}, bf16[512,768]{1,0:T(8,128)(2,1)S(1...) custom-call(s32[1]{0:T(128)} %bitcast.index_ref, ...), custom_call_target="tpu_custom_call" | custom-call | flops 3221225472 | bytes 13631488 | tf_op jit(solution)/shard_map/part/pallas_call | solution.py:134
  104.5 12.8 %collective-permute-done.10 = bf16[512,768]{1,0:T(8,128)(2,1)S(1)} collective-permute-done((bf16[512,768]{1,0:T(8,128)(2,1)S(1)}, bf16[512,768]{1,0:T(8,128)(2,1)S(1)}, u32[]{:S(2)}, u32[]{:S(2)}) %collective-permute-start.10) | collective-permute-done | bytes 786464 | tf_op jit(solution)/shard_map/ppermute | solution.py:232
  118.6 5.0 %collective-permute-start.14 = (bf16[512,768]{1,0:T(8,128)(2,1)S(1)}, bf16[512,768]{1,0:T(8,128)(2,1)S(1)}, u32[]{:S(2)}, u32[]{:S(2)}) collective-permute-start(bf16[512,768]{1,0:T(8,128)(2,1)S(1)} %get-tuple-element.108), channel_id=1, source_target_pairs={{0,8},{8,16},{1,9},{9,17},{2,10},{10,18},{3,11},{11,19},{4,12},{12... | collective-permute-start | bytes 2359304 | tf_op jit(solution)/shard_map/ppermute | solution.py:232
  127.2 11.4 %collective-permute-done.14 = bf16[512,768]{1,0:T(8,128)(2,1)S(1)} collective-permute-done((bf16[512,768]{1,0:T(8,128)(2,1)S(1)}, bf16[512,768]{1,0:T(8,128)(2,1)S(1)}, u32[]{:S(2)}, u32[]{:S(2)}) %collective-permute-start.14) | collective-permute-done | bytes 786464 | tf_op jit(solution)/shard_map/ppermute | solution.py:232
  138.6 5.4 %collective-permute-done.12.refs_3_ = bf16[512,768]{1,0:T(8,128)(2,1)S(1)} collective-permute-done((bf16[512,768]{1,0:T(8,128)(2,1)S(1)}, bf16[512,768]{1,0:T(8,128)(2,1)S(1)}, u32[]{:S(2)}, u32[]{:S(2)}) %collective-permute-start.12) | collective-permute-done | bytes 786464 | tf_op jit(solution)/shard_map/ppermute | solution.py:226
  147.1 4.6 %collective-permute-start.18 = (bf16[512,768]{1,0:T(8,128)(2,1)S(1)}, bf16[512,768]{1,0:T(8,128)(2,1)S(1)}, u32[]{:S(2)}, u32[]{:S(2)}) collective-permute-start(bf16[512,768]{1,0:T(8,128)(2,1)S(1)} %add_convert_fusion.8), channel_id=1, source_target_pairs={{0,8},{8,16},{16,24},{1,9},{9,17},{17,25},{2,10},{10,18},{18,26},{... | collective-permute-start | bytes 2359304 | tf_op jit(solution)/shard_map/ppermute | solution.py:232
  151.7 7.2 %part.4 = (bf16[2048,768]{1,0:T(8,128)(2,1)S(1)}, bf16[512,256]{1,0:T(8,128)(2,1)S(1)}, bf16[512,512]{1,0:T(8,128)(2,1)S(1)}, bf16[512,768]{1,0:T(8,128)(2,1)S(1...) custom-call(s32[1]{0:T(128)} %bitcast.index_ref, ...), custom_call_target="tpu_custom_call" | custom-call | flops 3221225472 | bytes 13631488 | tf_op jit(solution)/shard_map/part/pallas_call | solution.py:134
  163.5 16.9 %collective-permute-done.18 = bf16[512,768]{1,0:T(8,128)(2,1)S(1)} collective-permute-done((bf16[512,768]{1,0:T(8,128)(2,1)S(1)}, bf16[512,768]{1,0:T(8,128)(2,1)S(1)}, u32[]{:S(2)}, u32[]{:S(2)}) %collective-permute-start.18) | collective-permute-done | bytes 786464 | tf_op jit(solution)/shard_map/ppermute | solution.py:232
  182.6 12.1 %collective-permute-done.22 = bf16[512,768]{1,0:T(8,128)(2,1)S(1)} collective-permute-done((bf16[512,768]{1,0:T(8,128)(2,1)S(1)}, bf16[512,768]{1,0:T(8,128)(2,1)S(1)}, u32[]{:S(2)}, u32[]{:S(2)}) %collective-permute-start.22) | collective-permute-done | bytes 786464 | tf_op jit(solution)/shard_map/ppermute | solution.py:232
  195.8 5.0 %collective-permute-start.26 = (bf16[512,768]{1,0:T(8,128)(2,1)S(1)}, bf16[512,768]{1,0:T(8,128)(2,1)S(1)}, u32[]{:S(2)}, u32[]{:S(2)}) collective-permute-start(bf16[512,768]{1,0:T(8,128)(2,1)S(1)} %get-tuple-element.106), channel_id=1, source_target_pairs={{0,8},{8,16},{1,9},{9,17},{2,10},{10,18},{3,11},{11,19},{4,12},{12... | collective-permute-start | bytes 2359304 | tf_op jit(solution)/shard_map/ppermute | solution.py:232
  204.4 10.9 %collective-permute-done.26 = bf16[512,768]{1,0:T(8,128)(2,1)S(1)} collective-permute-done((bf16[512,768]{1,0:T(8,128)(2,1)S(1)}, bf16[512,768]{1,0:T(8,128)(2,1)S(1)}, u32[]{:S(2)}, u32[]{:S(2)}) %collective-permute-start.26) | collective-permute-done | bytes 786464 | tf_op jit(solution)/shard_map/ppermute | solution.py:232
  215.5 6.2 %collective-permute-start.28 = (bf16[512,768]{1,0:T(8,128)(2,1)S(1)}, bf16[512,768]{1,0:T(8,128)(2,1)}, u32[]{:S(2)}, u32[]{:S(2)}) collective-permute-start(bf16[512,768]{1,0:T(8,128)(2,1)S(1)} %add_convert_fusion.6), channel_id=1, source_target_pairs={{0,8},{8,16},{16,24},{1,9},{9,17},{17,25},{2,10},{10,18},{18,26},{... | collective-permute-start | bytes 2359304 | tf_op jit(solution)/shard_map/ppermute | solution.py:232
  222.8 7.6 %part.5 = (bf16[2048,768]{1,0:T(8,128)(2,1)S(1)}, bf16[512,256]{1,0:T(8,128)(2,1)S(1)}, bf16[512,512]{1,0:T(8,128)(2,1)S(1)}, bf16[512,768]{1,0:T(8,128)(2,1)S(1...) custom-call(s32[1]{0:T(128)} %bitcast.index_ref, ...), custom_call_target="tpu_custom_call" | custom-call | flops 3221225472 | bytes 13631488 | tf_op jit(solution)/shard_map/part/pallas_call | solution.py:134
  235.7 6.0 %back_products.1 = bf16[8,128,2048]{2,1,0:T(8,128)(2,1)S(1)} custom-call(bf16[512,256]{1,0:T(8,128)(2,1)S(1)} %get-tuple-element.46.refs_0_, bf16[512,256]{1,0:T(8,128)(2,1)S(1)} %get-tuple-element.54.refs_1_, bf16[512,256]{1,0:T(8,128)(2,1)S(1)} %get-tuple-element.65.refs_2_, bf16[512,512]{1,0:T(8,128)(2,1)S(1)} %get-tuple-element.66.refs_3_, ...), custom_call_target="tpu_custom_call" | custom-call | flops 4831838208 | bytes 13631488 | tf_op jit(solution)/shard_map/back_products/pallas_call | solution.py:167
  243.7 4.6 %all-to-all-start.1 = ((bf16[8,128,2048]{2,1,0:T(8,128)(2,1)}), bf16[8,128,2048]{2,1,0:T(8,128)(2,1)}, u32[]{:S(2)}, u32[]{:S(2)}) async-start(bf16[8,128,2048]{2,1,0:T(8,128)(2,1)} %copy-done.1), calls=%async_computation.1 | async-start | bytes 8388608 | tf_op jit(solution)/shard_map/all_to_all | solution.py:242
  254.5 5.3 %collective-permute-start.31 = (bf16[512,768]{1,0:T(8,128)(2,1)}, bf16[512,768]{1,0:T(8,128)(2,1)}, u32[]{:S(2)}, u32[]{:S(2)}) collective-permute-start(bf16[512,768]{1,0:T(8,128)(2,1)} %get-tuple-element.103), channel_id=1, source_target_pairs={{0,8},{8,16},{1,9},{9,17},{2,10},{10,18},{3,11},{11,19},{4,12},{12... | collective-permute-start | bytes 2359304 | tf_op jit(solution)/shard_map/ppermute | solution.py:232
  263.1 8.8 %collective-permute-done.31 = bf16[512,768]{1,0:T(8,128)(2,1)} collective-permute-done((bf16[512,768]{1,0:T(8,128)(2,1)}, bf16[512,768]{1,0:T(8,128)(2,1)}, u32[]{:S(2)}, u32[]{:S(2)}) %collective-permute-start.31) | collective-permute-done | bytes 786464 | tf_op jit(solution)/shard_map/ppermute | solution.py:232
  282.5 7.1 %collective-permute-done.32 = bf16[512,768]{1,0:T(8,128)(2,1)S(1)} collective-permute-done((bf16[512,768]{1,0:T(8,128)(2,1)S(1)}, bf16[512,768]{1,0:T(8,128)(2,1)S(1)}, u32[]{:S(2)}, u32[]{:S(2)}) %collective-permute-start.32) | collective-permute-done | bytes 786464 | tf_op jit(solution)/shard_map/ppermute | solution.py:232
  289.6 5.7 %collective-permute-done.35 = bf16[512,768]{1,0:T(8,128)(2,1)S(1)} collective-permute-done((bf16[512,768]{1,0:T(8,128)(2,1)S(1)}, bf16[512,768]{1,0:T(8,128)(2,1)S(1)}, u32[]{:S(2)}, u32[]{:S(2)}) %collective-permute-start.35) | collective-permute-done | bytes 786464 | tf_op jit(solution)/shard_map/ppermute | solution.py:233
  (138 shorter events, 93.2 us)
Async XLA Ops:
  3.7 21.8 %collective-permute-start = (bf16[512,768]{1,0:T(8,128)(2,1)S(1)}, bf16[512,768]{1,0:T(8,128)(2,1)S(1)}, u32[]{:S(2)}, u32[]{:S(2)}) collective-permute-start(bf16[512,768]{1,0:T(8,128)(2,1)S(1)} %pad_maximum_fusion.refs_0_), channel_id=1, source_target_pairs={{0,8},{8,16},{16,24},{1,9},{9,17},{17,25},{2,10},{10,18},{18,26},{... | collective-permute-start | bytes 2359304 | tf_op jit(solution)/shard_map/ppermute | solution.py:225
  8.8 21.0 %collective-permute-start.1 = (bf16[512,768]{1,0:T(8,128)(2,1)S(1)}, bf16[512,768]{1,0:T(8,128)(2,1)}, u32[]{:S(2)}, u32[]{:S(2)}) collective-permute-start(bf16[512,768]{1,0:T(8,128)(2,1)S(1)} %pad_maximum_fusion.refs_0_), channel_id=1, source_target_pairs={{24,16},{16,8},{8,0},{25,17},{17,9},{9,1},{26,18},{18,10},{10,2},{... | collective-permute-start | bytes 2359304 | tf_op jit(solution)/shard_map/ppermute | solution.py:226
  29.8 56.0 %all-to-all-start = ((bf16[8,128,2048]{2,1,0:T(8,128)(2,1)}), bf16[8,128,2048]{2,1,0:T(8,128)(2,1)}, u32[]{:S(2)}, u32[]{:S(2)}) async-start(bf16[8,128,2048]{2,1,0:T(8,128)(2,1)} %copy-done), calls=%async_computation | async-start | bytes 8388608 | tf_op jit(solution)/shard_map/all_to_all | solution.py:242
  34.3 21.9 %collective-permute-start.2 = (bf16[512,768]{1,0:T(8,128)(2,1)}, bf16[512,768]{1,0:T(8,128)(2,1)S(1)}, u32[]{:S(2)}, u32[]{:S(2)}) collective-permute-start(bf16[512,768]{1,0:T(8,128)(2,1)} %collective-permute-done.1.refs_1_), channel_id=1, source_target_pairs={{16,8},{8,0},{17,9},{9,1},{18,10},{10,2},{19,11},{11,3},{20,12},{1... | collective-permute-start | bytes 2359304 | tf_op jit(solution)/shard_map/ppermute | solution.py:226
  35.7 21.9 %collective-permute-start.4 = (bf16[512,768]{1,0:T(8,128)(2,1)S(1)}, bf16[512,768]{1,0:T(8,128)(2,1)S(1)}, u32[]{:S(2)}, u32[]{:S(2)}) collective-permute-start(bf16[512,768]{1,0:T(8,128)(2,1)S(1)} %collective-permute-done.refs_4_), channel_id=1, source_target_pairs={{8,16},{16,24},{9,17},{17,25},{10,18},{18,26},{11,19},{19,27},{12,... | collective-permute-start | bytes 2359304 | tf_op jit(solution)/shard_map/ppermute | solution.py:225
  56.3 21.0 %collective-permute-start.3 = (bf16[512,768]{1,0:T(8,128)(2,1)S(1)}, bf16[512,768]{1,0:T(8,128)(2,1)S(1)}, u32[]{:S(2)}, u32[]{:S(2)}) collective-permute-start(bf16[512,768]{1,0:T(8,128)(2,1)S(1)} %collective-permute-done.2.refs_2_), channel_id=1, source_target_pairs={{8,0},{9,1},{10,2},{11,3},{12,4},{13,5},{14,6},{15,7}} | collective-permute-start | bytes 2359304 | tf_op jit(solution)/shard_map/ppermute | solution.py:226
  57.6 20.6 %collective-permute-start.5 = (bf16[512,768]{1,0:T(8,128)(2,1)S(1)}, bf16[512,768]{1,0:T(8,128)(2,1)S(1)}, u32[]{:S(2)}, u32[]{:S(2)}) collective-permute-start(bf16[512,768]{1,0:T(8,128)(2,1)S(1)} %collective-permute-done.4.refs_5_), channel_id=1, source_target_pairs={{16,24},{17,25},{18,26},{19,27},{20,28},{21,29},{22,30},{23,31}} | collective-permute-start | bytes 2359304 | tf_op jit(solution)/shard_map/ppermute | solution.py:225
  79.1 21.4 %collective-permute-start.6 = (bf16[512,768]{1,0:T(8,128)(2,1)S(1)}, bf16[512,768]{1,0:T(8,128)(2,1)}, u32[]{:S(2)}, u32[]{:S(2)}) collective-permute-start(bf16[512,768]{1,0:T(8,128)(2,1)S(1)} %pad_maximum_fusion.1.refs_0_), channel_id=1, source_target_pairs={{24,16},{16,8},{8,0},{25,17},{17,9},{9,1},{26,18},{18,10},{10,2},{... | collective-permute-start | bytes 2359304 | tf_op jit(solution)/shard_map/ppermute | solution.py:226
  80.4 22.1 %collective-permute-start.7 = (bf16[512,768]{1,0:T(8,128)(2,1)S(1)}, bf16[512,768]{1,0:T(8,128)(2,1)}, u32[]{:S(2)}, u32[]{:S(2)}) collective-permute-start(bf16[512,768]{1,0:T(8,128)(2,1)S(1)} %pad_maximum_fusion.1.refs_0_), channel_id=1, source_target_pairs={{0,8},{8,16},{16,24},{1,9},{9,17},{17,25},{2,10},{10,18},{18,26},{... | collective-permute-start | bytes 2359304 | tf_op jit(solution)/shard_map/ppermute | solution.py:225
  102.5 21.1 %collective-permute-start.9 = (bf16[512,768]{1,0:T(8,128)(2,1)}, bf16[512,768]{1,0:T(8,128)(2,1)S(1)}, u32[]{:S(2)}, u32[]{:S(2)}) collective-permute-start(bf16[512,768]{1,0:T(8,128)(2,1)} %collective-permute-done.7.refs_4_), channel_id=1, source_target_pairs={{8,16},{16,24},{9,17},{17,25},{10,18},{18,26},{11,19},{19,27},{12,... | collective-permute-start | bytes 2359304 | tf_op jit(solution)/shard_map/ppermute | solution.py:225
  103.2 20.4 %collective-permute-start.8 = (bf16[512,768]{1,0:T(8,128)(2,1)}, bf16[512,768]{1,0:T(8,128)(2,1)S(1)}, u32[]{:S(2)}, u32[]{:S(2)}) collective-permute-start(bf16[512,768]{1,0:T(8,128)(2,1)} %collective-permute-done.6.refs_1_), channel_id=1, source_target_pairs={{16,8},{8,0},{17,9},{9,1},{18,10},{10,2},{19,11},{11,3},{20,12},{1... | collective-permute-start | bytes 2359304 | tf_op jit(solution)/shard_map/ppermute | solution.py:226
  118.6 20.0 %collective-permute-start.14 = (bf16[512,768]{1,0:T(8,128)(2,1)S(1)}, bf16[512,768]{1,0:T(8,128)(2,1)S(1)}, u32[]{:S(2)}, u32[]{:S(2)}) collective-permute-start(bf16[512,768]{1,0:T(8,128)(2,1)S(1)} %get-tuple-element.108), channel_id=1, source_target_pairs={{0,8},{8,16},{1,9},{9,17},{2,10},{10,18},{3,11},{11,19},{4,12},{12... | collective-permute-start | bytes 2359304 | tf_op jit(solution)/shard_map/ppermute | solution.py:232
  125.8 36.9 %collective-permute-start.19 = (bf16[512,768]{1,0:T(8,128)(2,1)S(1)}, bf16[512,768]{1,0:T(8,128)(2,1)S(1)}, u32[]{:S(2)}, u32[]{:S(2)}) collective-permute-start(bf16[512,768]{1,0:T(8,128)(2,1)S(1)} %add_convert_fusion.7), channel_id=1, source_target_pairs={{24,16},{16,8},{8,0},{25,17},{17,9},{9,1},{26,18},{18,10},{10,2},{... | collective-permute-start | bytes 2359304 | tf_op jit(solution)/shard_map/ppermute | solution.py:233
  144.0 36.4 %collective-permute-start.16 = (bf16[512,768]{1,0:T(8,128)(2,1)S(1)}, bf16[512,768]{1,0:T(8,128)(2,1)S(1)}, u32[]{:S(2)}, u32[]{:S(2)}) collective-permute-start(bf16[512,768]{1,0:T(8,128)(2,1)S(1)} %pad_maximum_fusion.2.refs_0_), channel_id=1, source_target_pairs={{0,8},{8,16},{16,24},{1,9},{9,17},{17,25},{2,10},{10,18},{18,26},{... | collective-permute-start | bytes 2359304 | tf_op jit(solution)/shard_map/ppermute | solution.py:225
  145.6 34.8 %collective-permute-start.17 = (bf16[512,768]{1,0:T(8,128)(2,1)S(1)}, bf16[512,768]{1,0:T(8,128)(2,1)S(1)}, u32[]{:S(2)}, u32[]{:S(2)}) collective-permute-start(bf16[512,768]{1,0:T(8,128)(2,1)S(1)} %pad_maximum_fusion.2.refs_0_), channel_id=1, source_target_pairs={{24,16},{16,8},{8,0},{25,17},{17,9},{9,1},{26,18},{18,10},{10,2},{... | collective-permute-start | bytes 2359304 | tf_op jit(solution)/shard_map/ppermute | solution.py:226
  147.1 33.3 %collective-permute-start.18 = (bf16[512,768]{1,0:T(8,128)(2,1)S(1)}, bf16[512,768]{1,0:T(8,128)(2,1)S(1)}, u32[]{:S(2)}, u32[]{:S(2)}) collective-permute-start(bf16[512,768]{1,0:T(8,128)(2,1)S(1)} %add_convert_fusion.8), channel_id=1, source_target_pairs={{0,8},{8,16},{16,24},{1,9},{9,17},{17,25},{2,10},{10,18},{18,26},{... | collective-permute-start | bytes 2359304 | tf_op jit(solution)/shard_map/ppermute | solution.py:232
  158.9 35.8 %collective-permute-start.22 = (bf16[512,768]{1,0:T(8,128)(2,1)S(1)}, bf16[512,768]{1,0:T(8,128)(2,1)S(1)}, u32[]{:S(2)}, u32[]{:S(2)}) collective-permute-start(bf16[512,768]{1,0:T(8,128)(2,1)S(1)} %get-tuple-element.59), channel_id=1, source_target_pairs={{0,8},{1,9},{2,10},{3,11},{4,12},{5,13},{6,14},{7,15}} | collective-permute-start | bytes 2359304 | tf_op jit(solution)/shard_map/ppermute | solution.py:232
  162.8 31.9 %collective-permute-start.23 = (bf16[512,768]{1,0:T(8,128)(2,1)S(1)}, bf16[512,768]{1,0:T(8,128)(2,1)S(1)}, u32[]{:S(2)}, u32[]{:S(2)}) collective-permute-start(bf16[512,768]{1,0:T(8,128)(2,1)S(1)} %get-tuple-element.60), channel_id=1, source_target_pairs={{24,16},{25,17},{26,18},{27,19},{28,20},{29,21},{30,22},{31,23}} | collective-permute-start | bytes 2359304 | tf_op jit(solution)/shard_map/ppermute | solution.py:233
  180.4 20.5 %collective-permute-start.21 = (bf16[512,768]{1,0:T(8,128)(2,1)S(1)}, bf16[512,768]{1,0:T(8,128)(2,1)S(1)}, u32[]{:S(2)}, u32[]{:S(2)}) collective-permute-start(bf16[512,768]{1,0:T(8,128)(2,1)S(1)} %collective-permute-done.17.refs_1_), channel_id=1, source_target_pairs={{16,8},{8,0},{17,9},{9,1},{18,10},{10,2},{19,11},{11,3},{20,12},{1... | collective-permute-start | bytes 2359304 | tf_op jit(solution)/shard_map/ppermute | solution.py:226
  200.9 21.9 %collective-permute-start.25 = (bf16[512,768]{1,0:T(8,128)(2,1)S(1)}, bf16[512,768]{1,0:T(8,128)(2,1)S(1)}, u32[]{:S(2)}, u32[]{:S(2)}) collective-permute-start(bf16[512,768]{1,0:T(8,128)(2,1)S(1)} %collective-permute-done.21.refs_2_), channel_id=1, source_target_pairs={{8,0},{9,1},{10,2},{11,3},{12,4},{13,5},{14,6},{15,7}} | collective-permute-start | bytes 2359304 | tf_op jit(solution)/shard_map/ppermute | solution.py:226
  202.2 20.6 %collective-permute-start.24 = (bf16[512,768]{1,0:T(8,128)(2,1)S(1)}, bf16[512,768]{1,0:T(8,128)(2,1)S(1)}, u32[]{:S(2)}, u32[]{:S(2)}) collective-permute-start(bf16[512,768]{1,0:T(8,128)(2,1)S(1)} %collective-permute-done.20.refs_5_), channel_id=1, source_target_pairs={{16,24},{17,25},{18,26},{19,27},{20,28},{21,29},{22,30},{23,31}} | collective-permute-start | bytes 2359304 | tf_op jit(solution)/shard_map/ppermute | solution.py:225
  203.1 40.6 %collective-permute-start.29 = (bf16[512,768]{1,0:T(8,128)(2,1)S(1)}, bf16[512,768]{1,0:T(8,128)(2,1)}, u32[]{:S(2)}, u32[]{:S(2)}) collective-permute-start(bf16[512,768]{1,0:T(8,128)(2,1)S(1)} %add_convert_fusion.5), channel_id=1, source_target_pairs={{24,16},{16,8},{8,0},{25,17},{17,9},{9,1},{26,18},{18,10},{10,2},{... | collective-permute-start | bytes 2359304 | tf_op jit(solution)/shard_map/ppermute | solution.py:233
  215.5 28.2 %collective-permute-start.28 = (bf16[512,768]{1,0:T(8,128)(2,1)S(1)}, bf16[512,768]{1,0:T(8,128)(2,1)}, u32[]{:S(2)}, u32[]{:S(2)}) collective-permute-start(bf16[512,768]{1,0:T(8,128)(2,1)S(1)} %add_convert_fusion.6), channel_id=1, source_target_pairs={{0,8},{8,16},{16,24},{1,9},{9,17},{17,25},{2,10},{10,18},{18,26},{... | collective-permute-start | bytes 2359304 | tf_op jit(solution)/shard_map/ppermute | solution.py:232
  243.7 54.8 %all-to-all-start.1 = ((bf16[8,128,2048]{2,1,0:T(8,128)(2,1)}), bf16[8,128,2048]{2,1,0:T(8,128)(2,1)}, u32[]{:S(2)}, u32[]{:S(2)}) async-start(bf16[8,128,2048]{2,1,0:T(8,128)(2,1)} %copy-done.1), calls=%async_computation.1 | async-start | bytes 8388608 | tf_op jit(solution)/shard_map/all_to_all | solution.py:242
  (39 other events, 510.0 us)

commit v3 on v2

--- a/solution.py
+++ b/solution.py
@@ -70,26 +70,32 @@
     )(index, target, gates, tokens, grad_out)
 
 
-def part_body(n, split, index_ref, rows_ref, *refs):
+def part_body(n, index_ref, rows_ref, *refs):
     own, above, below = refs[0], refs[1:n], refs[n : 2 * n - 1]
     full_ref, hid_ref, both_ref = refs[2 * n - 1 : 2 * n + 2]
-    terms = refs[2 * n + 2 :]
+    terms, sems = refs[2 * n + 2 : -1], refs[-1]
     feat, three = own.shape
     f = three // 3
     experts, cap = rows_ref.shape[0], rows_ref.shape[1] // 2
     slots = experts * cap
-    full_ref[:feat] = own[...]
+
+    def fetch(shard, m):
+        return pltpu.make_async_copy(shard, full_ref.at[m * feat : (m + 1) * feat], sems.at[m])
+
+    fetch(own, 0).start()
     for m in range(1, n):
         inside = index_ref[0] + m < n
 
         @pl.when(inside)
         def _():
-            full_ref[m * feat : (m + 1) * feat] = above[m - 1][...]
+            fetch(above[m - 1], m).start()
 
         @pl.when(jnp.logical_not(inside))
         def _():
-            full_ref[m * feat : (m + 1) * feat] = below[n - m - 1][...]
-
+            fetch(below[n - m - 1], m).start()
+
+    for m in range(n):
+        fetch(own, m).wait()
     group = max(1, 128 // cap)
     tile = group * cap
 
@@ -112,35 +118,45 @@
         cols = slice(m * feat, (m + 1) * feat)
         rows = rows_ref[:, :cap, cols].reshape(slots, feat)
         grows = rows_ref[:, cap:, cols].reshape(slots, feat)
-        inner = dot(rows, both_ref[...], 0, 0).astype(BF16)
-        outer = dot(grows, hid_ref[...], 0, 0).astype(BF16)
-        if split:
-            terms[m][...] = inner
-            terms[n + m][...] = outer
-        else:
-            terms[m][:, : 2 * f] = inner
-            terms[m][:, 2 * f :] = outer
-
-
-def part(index, rows, own, above, below, n, split=False):
+        terms[m][:, : 2 * f] = dot(rows, both_ref[...], 0, 0).astype(BF16)
+        terms[m][:, 2 * f :] = dot(grows, hid_ref[...], 0, 0).astype(BF16)
+
+
+def part(index, rows, own, above, below, n):
     feat, three = own.shape
     experts, double, width = rows.shape
     slots = experts * double // 2
     f = three // 3
     sds = jax.ShapeDtypeStruct
     out_shape = [sds((width, three), BF16), sds((slots, f), BF16), sds((slots, 2 * f), BF16)]
-    for columns in (2 * f, f) if split else (three,):
-        out_shape += [sds((feat, columns), BF16)] * n
+    out_shape += [sds((feat, three), BF16)] * n
     res = call(
-        functools.partial(part_body, n, split),
+        functools.partial(part_body, n),
         "part",
         out_shape,
-        [SCALAR] + [WHOLE] * (2 * n),
+        [SCALAR, WHOLE] + [pl.BlockSpec(memory_space=pltpu.HBM)] * (2 * n - 1),
         12 * slots * width * f,
         2 * (2 * slots * width + 3 * width * three),
         out_specs=[WHOLE] * len(out_shape),
+        scratch_shapes=[pltpu.SemaphoreType.DMA((n,))],
     )(index, rows, own, *above, *below)
     return res[0], res[1], res[2], list(res[3:])
+
+
+def touch_body(index_ref, *refs):
+    refs[-1][0] = index_ref[0]
+
+
+def touch(index, arrays, weight):
+    return call(
+        touch_body,
+        "touch",
+        jax.ShapeDtypeStruct(index.shape, index.dtype),
+        [SCALAR] + [pl.BlockSpec(memory_space=pl.ANY)] * len(arrays),
+        weight,
+        0,
+        out_specs=SCALAR,
+    )(index, *arrays)
 
 
 def back_body(count, cap, *refs):
@@ -298,12 +314,12 @@
 
     def run_part(c, waits=()):
         g = gathers[c]
-        split = SPLIT_LAST and c == count - 1
-        full, hid, both, terms = part(index, after(rows, *waits), g.own, g.above, g.below, n, split)
+        ready = touch(index, g.last, WEIGHT) if c == 0 else index
+        full, hid, both, terms = part(ready, after(rows, *waits), g.own, g.above, g.below, n)
         fulls.append(full)
         hids.append(hid)
         boths.append(both)
-        scatters.append([Scatter(terms[k * n : (k + 1) * n], n) for k in range(1 + split)])
+        scatters.append([Scatter(terms, n)])
 
     gathers[0].go()
     if EXCHANGE_AFTER_GATHER:
@@ -363,11 +379,12 @@
 
 
 EARLY = False
-SPLIT_LAST = False
+WEIGHT = 1 << 34
 COMBINE_EARLY = False
+WEIGHT = 1 << 34
 RETURN_AFTER = 1
 DISPATCH_AFTER_PACK = True
-EXCHANGE_AFTER_GATHER = True
+EXCHANGE_AFTER_GATHER = False
 GATHER_AFTER_PART = True
 TAIL_WAITS = True
 SERIAL_TAIL = False

time: 305 us -> 294 us (0.964)
  waiting for transfers between devices: 151 us -> 137 us
    ppermute x9, waiting for transfers between devices: 12.3 us -> 5.63 us  [gather_step(): lax.ppermute(up, 'dp', [(j, j + 1) for j in range(step - 1, n - 1)])]
    ppermute x9, waiting for transfers between devices: 83 us -> 76.4 us  [scatter_step(): lax.ppermute(up, 'dp', [(j, j + 1) for j in range(step)])]
    pallas_call x3 -> x4, Pallas kernels: 21.7 us -> 24.3 us  [the longest x3 23.8 us: part(): call(functools.partial(part_body, n), 'part', out_shape, [SCALAR, WHOLE]...]
  transfers between devices with their start and end apart: 38 -> 38, of which waited for: 16 -> 15; matrix products, arithmetic and copies ran while one was open for 5% -> 6% of each run, Pallas kernels for 10% -> 11%
where the time goes in v3:
time: 294 us; the launch traced here: 293 us
  waiting for transfers between devices  137 us (47%)
  starting transfers between devices  85.5 us (29%)
  Pallas kernels  35.9 us (12%)
  local copies, waits for them, and re-layouts  18.1 us (6%)
  other arithmetic  15.3 us (5%)
    ppermute x9, waiting for transfers between devices, scatter_step(): lax.ppermute(up, 'dp', [(j, j + 1) for j in range(step)])  76.4 us
    ppermute x9, waiting for transfers between devices, gather_step(): lax.ppermute(down, 'dp', [(j, j - 1) for j in range(n - step, 0, -1)])  48.8 us
    ppermute x9, starting transfers between devices, scatter_step(): lax.ppermute(up, 'dp', [(j, j + 1) for j in range(step)])  38.2 us
    pallas_call x3, Pallas kernels, part(): call(functools.partial(part_body, n), 'part', out_shape, [SCALAR, WHOLE]...  23.8 us
    ppermute x9, starting transfers between devices, gather_step(): lax.ppermute(up, 'dp', [(j, j + 1) for j in range(step - 1, n - 1)])  16.3 us
    unnamed x53, local copies, waits for them, and re-layouts  14.8 us
    ppermute x9, starting transfers between devices, gather_step(): lax.ppermute(down, 'dp', [(j, j - 1) for j in range(n - step, 0, -1)])  11.8 us
    ppermute x9, starting transfers between devices, scatter_step(): lax.ppermute(down, 'dp', [(j, j - 1) for j in range(n - 1, n - 1 - step,...  9.95 us
  transfers between devices with their start and end apart: 38, of which 15 were waited for; matrix products, arithmetic and copies ran while one was open for 6% of the time, Pallas kernels for 11%

profile of v3, /device:TPU:0, one launch (start us, length us, event | category | flops | bytes accessed | tf_op | source)
XLA Modules:
  0.0 292.6 jit_solution(1245758257951848844)
XLA Ops:
  3.7 5.1 %collective-permute-start = (bf16[512,768]{1,0:T(8,128)(2,1)S(1)}, bf16[512,768]{1,0:T(8,128)(2,1)S(1)}, u32[]{:S(2)}, u32[]{:S(2)}) collective-permute-start(bf16[512,768]{1,0:T(8,128)(2,1)S(1)} %pad_maximum_fusion.refs_0_), channel_id=1, source_target_pairs={{0,8},{8,16},{16,24},{1,9},{9,17},{17,25},{2,10},{10,18},{18,26},{... | collective-permute-start | bytes 2359304 | tf_op jit(solution)/shard_map/ppermute | solution.py:241
  15.2 4.7 %all-to-all-start = ((bf16[8,128,2048]{2,1,0:T(8,128)(2,1)}), bf16[8,128,2048]{2,1,0:T(8,128)(2,1)}, u32[]{:S(2)}, u32[]{:S(2)}) async-start(bf16[8,128,2048]{2,1,0:T(8,128)(2,1)} %copy-done), calls=%async_computation | async-start | bytes 8388608 | tf_op jit(solution)/shard_map/all_to_all | solution.py:258
  19.9 5.6 %collective-permute-done.refs_4_ = bf16[512,768]{1,0:T(8,128)(2,1)S(1)} collective-permute-done((bf16[512,768]{1,0:T(8,128)(2,1)S(1)}, bf16[512,768]{1,0:T(8,128)(2,1)S(1)}, u32[]{:S(2)}, u32[]{:S(2)}) %collective-permute-start) | collective-permute-done | bytes 786464 | tf_op jit(solution)/shard_map/ppermute | solution.py:241
  31.8 19.2 %collective-permute-done.4.refs_2_ = bf16[512,768]{1,0:T(8,128)(2,1)S(1)} collective-permute-done((bf16[512,768]{1,0:T(8,128)(2,1)}, bf16[512,768]{1,0:T(8,128)(2,1)S(1)}, u32[]{:S(2)}, u32[]{:S(2)}) %collective-permute-start.4) | collective-permute-done | bytes 786464 | tf_op jit(solution)/shard_map/ppermute | solution.py:242
  52.4 18.2 %collective-permute-done.5.refs_1_.refs_3_ = bf16[512,768]{1,0:T(8,128)(2,1)S(1)} collective-permute-done((bf16[512,768]{1,0:T(8,128)(2,1)S(1)}, bf16[512,768]{1,0:T(8,128)(2,1)S(1)}, u32[]{:S(2)}, u32[]{:S(2)}) %collective-permute-start.5) | collective-permute-done | bytes 786464 | tf_op jit(solution)/shard_map/ppermute | solution.py:242
  71.9 5.4 %collective-permute-start.7 = (bf16[512,768]{1,0:T(8,128)(2,1)S(1)}, bf16[512,768]{1,0:T(8,128)(2,1)}, u32[]{:S(2)}, u32[]{:S(2)}) collective-permute-start(bf16[512,768]{1,0:T(8,128)(2,1)S(1)} %pad_maximum_fusion.1.refs_0_), channel_id=1, source_target_pairs={{0,8},{8,16},{16,24},{1,9},{9,17},{17,25},{2,10},{10,18},{18,26},{... | collective-permute-start | bytes 2359304 | tf_op jit(solution)/shard_map/ppermute | solution.py:241
  85.3 8.4 %part.3 = (bf16[2048,768]{1,0:T(8,128)(2,1)S(1)}, bf16[512,256]{1,0:T(8,128)(2,1)S(1)}, bf16[512,512]{1,0:T(8,128)(2,1)S(1)}, bf16[512,768]{1,0:T(8,128)(2,1)S(1...) custom-call(s32[1]{0:T(128)} %touch.1.index_ref, ...), custom_call_target="tpu_custom_call" | custom-call | flops 3221225472 | bytes 13631488 | tf_op jit(solution)/shard_map/part/pallas_call | solution.py:133
  97.8 11.3 %collective-permute-done.10 = bf16[512,768]{1,0:T(8,128)(2,1)S(1)} collective-permute-done((bf16[512,768]{1,0:T(8,128)(2,1)S(1)}, bf16[512,768]{1,0:T(8,128)(2,1)S(1)}, u32[]{:S(2)}, u32[]{:S(2)}) %collective-permute-start.10) | collective-permute-done | bytes 786464 | tf_op jit(solution)/shard_map/ppermute | solution.py:248
  110.4 5.0 %collective-permute-start.14 = (bf16[512,768]{1,0:T(8,128)(2,1)S(1)}, bf16[512,768]{1,0:T(8,128)(2,1)S(1)}, u32[]{:S(2)}, u32[]{:S(2)}) collective-permute-start(bf16[512,768]{1,0:T(8,128)(2,1)S(1)} %get-tuple-element.106), channel_id=1, source_target_pairs={{0,8},{8,16},{1,9},{9,17},{2,10},{10,18},{3,11},{11,19},{4,12},{12... | collective-permute-start | bytes 2359304 | tf_op jit(solution)/shard_map/ppermute | solution.py:248
  119.0 9.5 %collective-permute-done.14 = bf16[512,768]{1,0:T(8,128)(2,1)S(1)} collective-permute-done((bf16[512,768]{1,0:T(8,128)(2,1)S(1)}, bf16[512,768]{1,0:T(8,128)(2,1)S(1)}, u32[]{:S(2)}, u32[]{:S(2)}) %collective-permute-start.14) | collective-permute-done | bytes 786464 | tf_op jit(solution)/shard_map/ppermute | solution.py:248
  128.5 6.1 %collective-permute-done.12.refs_3_ = bf16[512,768]{1,0:T(8,128)(2,1)S(1)} collective-permute-done((bf16[512,768]{1,0:T(8,128)(2,1)S(1)}, bf16[512,768]{1,0:T(8,128)(2,1)S(1)}, u32[]{:S(2)}, u32[]{:S(2)}) %collective-permute-start.12) | collective-permute-done | bytes 786464 | tf_op jit(solution)/shard_map/ppermute | solution.py:242
  137.6 4.6 %collective-permute-start.18 = (bf16[512,768]{1,0:T(8,128)(2,1)S(1)}, bf16[512,768]{1,0:T(8,128)(2,1)S(1)}, u32[]{:S(2)}, u32[]{:S(2)}) collective-permute-start(bf16[512,768]{1,0:T(8,128)(2,1)S(1)} %add_convert_fusion.8), channel_id=1, source_target_pairs={{0,8},{8,16},{16,24},{1,9},{9,17},{17,25},{2,10},{10,18},{18,26},{... | collective-permute-start | bytes 2359304 | tf_op jit(solution)/shard_map/ppermute | solution.py:248
  142.2 7.7 %part.4 = (bf16[2048,768]{1,0:T(8,128)(2,1)S(1)}, bf16[512,256]{1,0:T(8,128)(2,1)S(1)}, bf16[512,512]{1,0:T(8,128)(2,1)S(1)}, bf16[512,768]{1,0:T(8,128)(2,1)S(1...) custom-call(s32[1]{0:T(128)} %bitcast.index_ref, ...), custom_call_target="tpu_custom_call" | custom-call | flops 3221225472 | bytes 13631488 | tf_op jit(solution)/shard_map/part/pallas_call | solution.py:133
  154.7 16.2 %collective-permute-done.18 = bf16[512,768]{1,0:T(8,128)(2,1)S(1)} collective-permute-done((bf16[512,768]{1,0:T(8,128)(2,1)S(1)}, bf16[512,768]{1,0:T(8,128)(2,1)S(1)}, u32[]{:S(2)}, u32[]{:S(2)}) %collective-permute-start.18) | collective-permute-done | bytes 786464 | tf_op jit(solution)/shard_map/ppermute | solution.py:248
  172.9 11.1 %collective-permute-done.22 = bf16[512,768]{1,0:T(8,128)(2,1)S(1)} collective-permute-done((bf16[512,768]{1,0:T(8,128)(2,1)S(1)}, bf16[512,768]{1,0:T(8,128)(2,1)S(1)}, u32[]{:S(2)}, u32[]{:S(2)}) %collective-permute-start.22) | collective-permute-done | bytes 786464 | tf_op jit(solution)/shard_map/ppermute | solution.py:248
  185.1 5.0 %collective-permute-start.26 = (bf16[512,768]{1,0:T(8,128)(2,1)S(1)}, bf16[512,768]{1,0:T(8,128)(2,1)S(1)}, u32[]{:S(2)}, u32[]{:S(2)}) collective-permute-start(bf16[512,768]{1,0:T(8,128)(2,1)S(1)} %get-tuple-element.104), channel_id=1, source_target_pairs={{0,8},{8,16},{1,9},{9,17},{2,10},{10,18},{3,11},{11,19},{4,12},{12... | collective-permute-start | bytes 2359304 | tf_op jit(solution)/shard_map/ppermute | solution.py:248
  193.9 9.6 %collective-permute-done.26 = bf16[512,768]{1,0:T(8,128)(2,1)S(1)} collective-permute-done((bf16[512,768]{1,0:T(8,128)(2,1)S(1)}, bf16[512,768]{1,0:T(8,128)(2,1)S(1)}, u32[]{:S(2)}, u32[]{:S(2)}) %collective-permute-start.26) | collective-permute-done | bytes 786464 | tf_op jit(solution)/shard_map/ppermute | solution.py:248
  203.7 6.2 %collective-permute-start.28 = (bf16[512,768]{1,0:T(8,128)(2,1)S(1)}, bf16[512,768]{1,0:T(8,128)(2,1)}, u32[]{:S(2)}, u32[]{:S(2)}) collective-permute-start(bf16[512,768]{1,0:T(8,128)(2,1)S(1)} %add_convert_fusion.6), channel_id=1, source_target_pairs={{0,8},{8,16},{16,24},{1,9},{9,17},{17,25},{2,10},{10,18},{18,26},{... | collective-permute-start | bytes 2359304 | tf_op jit(solution)/shard_map/ppermute | solution.py:248
  212.5 7.7 %part.5 = (bf16[2048,768]{1,0:T(8,128)(2,1)S(1)}, bf16[512,256]{1,0:T(8,128)(2,1)S(1)}, bf16[512,512]{1,0:T(8,128)(2,1)S(1)}, bf16[512,768]{1,0:T(8,128)(2,1)S(1...) custom-call(s32[1]{0:T(128)} %bitcast.index_ref, ...), custom_call_target="tpu_custom_call" | custom-call | flops 3221225472 | bytes 13631488 | tf_op jit(solution)/shard_map/part/pallas_call | solution.py:133
  225.0 6.0 %back_products.1 = bf16[8,128,2048]{2,1,0:T(8,128)(2,1)S(1)} custom-call(bf16[512,256]{1,0:T(8,128)(2,1)S(1)} %get-tuple-element.44.refs_0_, bf16[512,256]{1,0:T(8,128)(2,1)S(1)} %get-tuple-element.52.refs_1_, bf16[512,256]{1,0:T(8,128)(2,1)S(1)} %get-tuple-element.63.refs_2_, bf16[512,512]{1,0:T(8,128)(2,1)S(1)} %get-tuple-element.64.refs_3_, ...), custom_call_target="tpu_custom_call" | custom-call | flops 4831838208 | bytes 13631488 | tf_op jit(solution)/shard_map/back_products/pallas_call | solution.py:183
  241.5 5.3 %collective-permute-start.31 = (bf16[512,768]{1,0:T(8,128)(2,1)}, bf16[512,768]{1,0:T(8,128)(2,1)}, u32[]{:S(2)}, u32[]{:S(2)}) collective-permute-start(bf16[512,768]{1,0:T(8,128)(2,1)} %get-tuple-element.101), channel_id=1, source_target_pairs={{0,8},{8,16},{1,9},{9,17},{2,10},{10,18},{3,11},{11,19},{4,12},{12... | collective-permute-start | bytes 2359304 | tf_op jit(solution)/shard_map/ppermute | solution.py:248
  250.1 9.9 %collective-permute-done.31 = bf16[512,768]{1,0:T(8,128)(2,1)} collective-permute-done((bf16[512,768]{1,0:T(8,128)(2,1)}, bf16[512,768]{1,0:T(8,128)(2,1)}, u32[]{:S(2)}, u32[]{:S(2)}) %collective-permute-start.31) | collective-permute-done | bytes 786464 | tf_op jit(solution)/shard_map/ppermute | solution.py:248
  270.6 8.1 %collective-permute-done.32 = bf16[512,768]{1,0:T(8,128)(2,1)S(1)} collective-permute-done((bf16[512,768]{1,0:T(8,128)(2,1)S(1)}, bf16[512,768]{1,0:T(8,128)(2,1)S(1)}, u32[]{:S(2)}, u32[]{:S(2)}) %collective-permute-start.32) | collective-permute-done | bytes 786464 | tf_op jit(solution)/shard_map/ppermute | solution.py:248
  278.7 5.7 %collective-permute-done.35 = bf16[512,768]{1,0:T(8,128)(2,1)S(1)} collective-permute-done((bf16[512,768]{1,0:T(8,128)(2,1)S(1)}, bf16[512,768]{1,0:T(8,128)(2,1)S(1)}, u32[]{:S(2)}, u32[]{:S(2)}) %collective-permute-start.35) | collective-permute-done | bytes 786464 | tf_op jit(solution)/shard_map/ppermute | solution.py:249
  (139 shorter events, 89.8 us)
Async XLA Ops:
  3.7 21.8 %collective-permute-start = (bf16[512,768]{1,0:T(8,128)(2,1)S(1)}, bf16[512,768]{1,0:T(8,128)(2,1)S(1)}, u32[]{:S(2)}, u32[]{:S(2)}) collective-permute-start(bf16[512,768]{1,0:T(8,128)(2,1)S(1)} %pad_maximum_fusion.refs_0_), channel_id=1, source_target_pairs={{0,8},{8,16},{16,24},{1,9},{9,17},{17,25},{2,10},{10,18},{18,26},{... | collective-permute-start | bytes 2359304 | tf_op jit(solution)/shard_map/ppermute | solution.py:241
  8.8 21.0 %collective-permute-start.3 = (bf16[512,768]{1,0:T(8,128)(2,1)S(1)}, bf16[512,768]{1,0:T(8,128)(2,1)}, u32[]{:S(2)}, u32[]{:S(2)}) collective-permute-start(bf16[512,768]{1,0:T(8,128)(2,1)S(1)} %pad_maximum_fusion.refs_0_), channel_id=1, source_target_pairs={{24,16},{16,8},{8,0},{25,17},{17,9},{9,1},{26,18},{18,10},{10,2},{... | collective-permute-start | bytes 2359304 | tf_op jit(solution)/shard_map/ppermute | solution.py:242
  15.2 64.5 %all-to-all-start = ((bf16[8,128,2048]{2,1,0:T(8,128)(2,1)}), bf16[8,128,2048]{2,1,0:T(8,128)(2,1)}, u32[]{:S(2)}, u32[]{:S(2)}) async-start(bf16[8,128,2048]{2,1,0:T(8,128)(2,1)} %copy-done), calls=%async_computation | async-start | bytes 8388608 | tf_op jit(solution)/shard_map/all_to_all | solution.py:258
  29.8 21.2 %collective-permute-start.4 = (bf16[512,768]{1,0:T(8,128)(2,1)}, bf16[512,768]{1,0:T(8,128)(2,1)S(1)}, u32[]{:S(2)}, u32[]{:S(2)}) collective-permute-start(bf16[512,768]{1,0:T(8,128)(2,1)} %collective-permute-done.3.refs_1_), channel_id=1, source_target_pairs={{16,8},{8,0},{17,9},{9,1},{18,10},{10,2},{19,11},{11,3},{20,12},{1... | collective-permute-start | bytes 2359304 | tf_op jit(solution)/shard_map/ppermute | solution.py:242
  31.1 21.3 %collective-permute-start.2 = (bf16[512,768]{1,0:T(8,128)(2,1)S(1)}, bf16[512,768]{1,0:T(8,128)(2,1)S(1)}, u32[]{:S(2)}, u32[]{:S(2)}) collective-permute-start(bf16[512,768]{1,0:T(8,128)(2,1)S(1)} %collective-permute-done.1.refs_5_), channel_id=1, source_target_pairs={{16,24},{17,25},{18,26},{19,27},{20,28},{21,29},{22,30},{23,31}} | collective-permute-start | bytes 2359304 | tf_op jit(solution)/shard_map/ppermute | solution.py:241
  51.0 19.6 %collective-permute-start.5 = (bf16[512,768]{1,0:T(8,128)(2,1)S(1)}, bf16[512,768]{1,0:T(8,128)(2,1)S(1)}, u32[]{:S(2)}, u32[]{:S(2)}) collective-permute-start(bf16[512,768]{1,0:T(8,128)(2,1)S(1)} %collective-permute-done.4.refs_2_), channel_id=1, source_target_pairs={{8,0},{9,1},{10,2},{11,3},{12,4},{13,5},{14,6},{15,7}} | collective-permute-start | bytes 2359304 | tf_op jit(solution)/shard_map/ppermute | solution.py:242
  70.6 25.2 %collective-permute-start.6 = (bf16[512,768]{1,0:T(8,128)(2,1)S(1)}, bf16[512,768]{1,0:T(8,128)(2,1)}, u32[]{:S(2)}, u32[]{:S(2)}) collective-permute-start(bf16[512,768]{1,0:T(8,128)(2,1)S(1)} %pad_maximum_fusion.1.refs_0_), channel_id=1, source_target_pairs={{24,16},{16,8},{8,0},{25,17},{17,9},{9,1},{26,18},{18,10},{10,2},{... | collective-permute-start | bytes 2359304 | tf_op jit(solution)/shard_map/ppermute | solution.py:242
  71.9 23.9 %collective-permute-start.7 = (bf16[512,768]{1,0:T(8,128)(2,1)S(1)}, bf16[512,768]{1,0:T(8,128)(2,1)}, u32[]{:S(2)}, u32[]{:S(2)}) collective-permute-start(bf16[512,768]{1,0:T(8,128)(2,1)S(1)} %pad_maximum_fusion.1.refs_0_), channel_id=1, source_target_pairs={{0,8},{8,16},{16,24},{1,9},{9,17},{17,25},{2,10},{10,18},{18,26},{... | collective-permute-start | bytes 2359304 | tf_op jit(solution)/shard_map/ppermute | solution.py:241
  95.8 19.6 %collective-permute-start.9 = (bf16[512,768]{1,0:T(8,128)(2,1)}, bf16[512,768]{1,0:T(8,128)(2,1)S(1)}, u32[]{:S(2)}, u32[]{:S(2)}) collective-permute-start(bf16[512,768]{1,0:T(8,128)(2,1)} %collective-permute-done.7.refs_4_), channel_id=1, source_target_pairs={{8,16},{16,24},{9,17},{17,25},{10,18},{18,26},{11,19},{19,27},{12,... | collective-permute-start | bytes 2359304 | tf_op jit(solution)/shard_map/ppermute | solution.py:241
  96.5 18.9 %collective-permute-start.8 = (bf16[512,768]{1,0:T(8,128)(2,1)}, bf16[512,768]{1,0:T(8,128)(2,1)S(1)}, u32[]{:S(2)}, u32[]{:S(2)}) collective-permute-start(bf16[512,768]{1,0:T(8,128)(2,1)} %collective-permute-done.6.refs_1_), channel_id=1, source_target_pairs={{16,8},{8,0},{17,9},{9,1},{18,10},{10,2},{19,11},{11,3},{20,12},{1... | collective-permute-start | bytes 2359304 | tf_op jit(solution)/shard_map/ppermute | solution.py:242
  116.1 18.5 %collective-permute-start.12 = (bf16[512,768]{1,0:T(8,128)(2,1)S(1)}, bf16[512,768]{1,0:T(8,128)(2,1)S(1)}, u32[]{:S(2)}, u32[]{:S(2)}) collective-permute-start(bf16[512,768]{1,0:T(8,128)(2,1)S(1)} %collective-permute-done.8.refs_2_), channel_id=1, source_target_pairs={{8,0},{9,1},{10,2},{11,3},{12,4},{13,5},{14,6},{15,7}} | collective-permute-start | bytes 2359304 | tf_op jit(solution)/shard_map/ppermute | solution.py:242
  117.6 36.3 %collective-permute-start.19 = (bf16[512,768]{1,0:T(8,128)(2,1)S(1)}, bf16[512,768]{1,0:T(8,128)(2,1)S(1)}, u32[]{:S(2)}, u32[]{:S(2)}) collective-permute-start(bf16[512,768]{1,0:T(8,128)(2,1)S(1)} %add_convert_fusion.7), channel_id=1, source_target_pairs={{24,16},{16,8},{8,0},{25,17},{17,9},{9,1},{26,18},{18,10},{10,2},{... | collective-permute-start | bytes 2359304 | tf_op jit(solution)/shard_map/ppermute | solution.py:249
  134.6 36.3 %collective-permute-start.16 = (bf16[512,768]{1,0:T(8,128)(2,1)S(1)}, bf16[512,768]{1,0:T(8,128)(2,1)S(1)}, u32[]{:S(2)}, u32[]{:S(2)}) collective-permute-start(bf16[512,768]{1,0:T(8,128)(2,1)S(1)} %pad_maximum_fusion.2.refs_0_), channel_id=1, source_target_pairs={{0,8},{8,16},{16,24},{1,9},{9,17},{17,25},{2,10},{10,18},{18,26},{... | collective-permute-start | bytes 2359304 | tf_op jit(solution)/shard_map/ppermute | solution.py:241
  136.1 34.8 %collective-permute-start.17 = (bf16[512,768]{1,0:T(8,128)(2,1)S(1)}, bf16[512,768]{1,0:T(8,128)(2,1)S(1)}, u32[]{:S(2)}, u32[]{:S(2)}) collective-permute-start(bf16[512,768]{1,0:T(8,128)(2,1)S(1)} %pad_maximum_fusion.2.refs_0_), channel_id=1, source_target_pairs={{24,16},{16,8},{8,0},{25,17},{17,9},{9,1},{26,18},{18,10},{10,2},{... | collective-permute-start | bytes 2359304 | tf_op jit(solution)/shard_map/ppermute | solution.py:242
  137.6 33.3 %collective-permute-start.18 = (bf16[512,768]{1,0:T(8,128)(2,1)S(1)}, bf16[512,768]{1,0:T(8,128)(2,1)S(1)}, u32[]{:S(2)}, u32[]{:S(2)}) collective-permute-start(bf16[512,768]{1,0:T(8,128)(2,1)S(1)} %add_convert_fusion.8), channel_id=1, source_target_pairs={{0,8},{8,16},{16,24},{1,9},{9,17},{17,25},{2,10},{10,18},{18,26},{... | collective-permute-start | bytes 2359304 | tf_op jit(solution)/shard_map/ppermute | solution.py:248
  149.9 34.1 %collective-permute-start.22 = (bf16[512,768]{1,0:T(8,128)(2,1)S(1)}, bf16[512,768]{1,0:T(8,128)(2,1)S(1)}, u32[]{:S(2)}, u32[]{:S(2)}) collective-permute-start(bf16[512,768]{1,0:T(8,128)(2,1)S(1)} %get-tuple-element.57), channel_id=1, source_target_pairs={{0,8},{1,9},{2,10},{3,11},{4,12},{5,13},{6,14},{7,15}} | collective-permute-start | bytes 2359304 | tf_op jit(solution)/shard_map/ppermute | solution.py:248
  154.0 30.0 %collective-permute-start.23 = (bf16[512,768]{1,0:T(8,128)(2,1)S(1)}, bf16[512,768]{1,0:T(8,128)(2,1)S(1)}, u32[]{:S(2)}, u32[]{:S(2)}) collective-permute-start(bf16[512,768]{1,0:T(8,128)(2,1)S(1)} %get-tuple-element.58), channel_id=1, source_target_pairs={{24,16},{25,17},{26,18},{27,19},{28,20},{29,21},{30,22},{31,23}} | collective-permute-start | bytes 2359304 | tf_op jit(solution)/shard_map/ppermute | solution.py:249
  170.9 19.3 %collective-permute-start.21 = (bf16[512,768]{1,0:T(8,128)(2,1)S(1)}, bf16[512,768]{1,0:T(8,128)(2,1)S(1)}, u32[]{:S(2)}, u32[]{:S(2)}) collective-permute-start(bf16[512,768]{1,0:T(8,128)(2,1)S(1)} %collective-permute-done.17.refs_1_), channel_id=1, source_target_pairs={{16,8},{8,0},{17,9},{9,1},{18,10},{10,2},{19,11},{11,3},{20,12},{1... | collective-permute-start | bytes 2359304 | tf_op jit(solution)/shard_map/ppermute | solution.py:242
  190.2 22.3 %collective-permute-start.25 = (bf16[512,768]{1,0:T(8,128)(2,1)S(1)}, bf16[512,768]{1,0:T(8,128)(2,1)S(1)}, u32[]{:S(2)}, u32[]{:S(2)}) collective-permute-start(bf16[512,768]{1,0:T(8,128)(2,1)S(1)} %collective-permute-done.21.refs_2_), channel_id=1, source_target_pairs={{8,0},{9,1},{10,2},{11,3},{12,4},{13,5},{14,6},{15,7}} | collective-permute-start | bytes 2359304 | tf_op jit(solution)/shard_map/ppermute | solution.py:242
  191.7 20.8 %collective-permute-start.24 = (bf16[512,768]{1,0:T(8,128)(2,1)S(1)}, bf16[512,768]{1,0:T(8,128)(2,1)S(1)}, u32[]{:S(2)}, u32[]{:S(2)}) collective-permute-start(bf16[512,768]{1,0:T(8,128)(2,1)S(1)} %collective-permute-done.20.refs_5_), channel_id=1, source_target_pairs={{16,24},{17,25},{18,26},{19,27},{20,28},{21,29},{22,30},{23,31}} | collective-permute-start | bytes 2359304 | tf_op jit(solution)/shard_map/ppermute | solution.py:241
  192.6 40.4 %collective-permute-start.29 = (bf16[512,768]{1,0:T(8,128)(2,1)S(1)}, bf16[512,768]{1,0:T(8,128)(2,1)}, u32[]{:S(2)}, u32[]{:S(2)}) collective-permute-start(bf16[512,768]{1,0:T(8,128)(2,1)S(1)} %add_convert_fusion.5), channel_id=1, source_target_pairs={{24,16},{16,8},{8,0},{25,17},{17,9},{9,1},{26,18},{18,10},{10,2},{... | collective-permute-start | bytes 2359304 | tf_op jit(solution)/shard_map/ppermute | solution.py:249
  203.7 29.3 %collective-permute-start.28 = (bf16[512,768]{1,0:T(8,128)(2,1)S(1)}, bf16[512,768]{1,0:T(8,128)(2,1)}, u32[]{:S(2)}, u32[]{:S(2)}) collective-permute-start(bf16[512,768]{1,0:T(8,128)(2,1)S(1)} %add_convert_fusion.6), channel_id=1, source_target_pairs={{0,8},{8,16},{16,24},{1,9},{9,17},{17,25},{2,10},{10,18},{18,26},{... | collective-permute-start | bytes 2359304 | tf_op jit(solution)/shard_map/ppermute | solution.py:248
  233.0 54.7 %all-to-all-start.1 = ((bf16[8,128,2048]{2,1,0:T(8,128)(2,1)}), bf16[8,128,2048]{2,1,0:T(8,128)(2,1)}, u32[]{:S(2)}, u32[]{:S(2)}) async-start(bf16[8,128,2048]{2,1,0:T(8,128)(2,1)} %copy-done.1), calls=%async_computation.1 | async-start | bytes 8388608 | tf_op jit(solution)/shard_map/all_to_all | solution.py:258
  246.7 19.2 %collective-permute-start.34 = (bf16[512,768]{1,0:T(8,128)(2,1)}, bf16[512,768]{1,0:T(8,128)(2,1)}, u32[]{:S(2)}, u32[]{:S(2)}) collective-permute-start(bf16[512,768]{1,0:T(8,128)(2,1)} %get-tuple-element.102), channel_id=1, source_target_pairs={{24,16},{16,8},{25,17},{17,9},{26,18},{18,10},{27,19},{19,11},{28,... | collective-permute-start | bytes 2359304 | tf_op jit(solution)/shard_map/ppermute | solution.py:249
  (39 other events, 474.8 us)

commit v4 on v3

--- a/solution.py
+++ b/solution.py
@@ -183,7 +183,7 @@
     return pl.pallas_call(
         functools.partial(back_body, count, cap),
         name="back_products",
-        out_shape=jax.ShapeDtypeStruct((experts, 2 * cap, width), BF16),
+        out_shape=pltpu.HBM((experts, 2 * cap, width), BF16),
         grid=(n,),
         in_specs=[pl.BlockSpec(x.shape, lambda m: (0, 0)) for x in (*hids, *boths)]
         + [pl.BlockSpec((feat, x.shape[1]), lambda m: (m, 0)) for x in fulls],
@@ -220,7 +220,7 @@
         out_ref[:, to] = total.astype(BF16)
         dtok_ref[:, to] = dot(either, rows_ref[:, cap:, here].reshape(slots, feat), 1, 0).astype(BF16)
     for k in range(top_k):
-        dgate_ref[:, k : k + 1] = sums[k]
+        dgate_ref[k : k + 1, :] = jnp.broadcast_to(sums[k], (tok_dev, 128)).T[:1, :]
 
 
 def combine(index, target, gates, grad_out, rows, n):
@@ -228,7 +228,7 @@
     return call(
         functools.partial(combine_body, n),
         "combine",
-        [shape, shape, jax.ShapeDtypeStruct(gates.shape, F32)],
+        [shape, shape, jax.ShapeDtypeStruct(gates.shape[::-1], F32)],
         [SCALAR, WHOLE, WHOLE, WHOLE, WHOLE],
         3 * rows.shape[0] * rows.shape[1] * grad_out.size,
         2 * (rows.size + 3 * grad_out.size),
@@ -375,7 +375,7 @@
                 g[k // 2][:, (k % 2) * f : (k % 2 + 1) * f] if len(g) == 2 else g[0][:, k * f : (k + 1) * f]
             )
         stacked.append(jnp.concatenate(pieces, axis=1)[None])
-    return (layer_out, grad_tokens, grad_gates, *stacked)
+    return (layer_out, grad_tokens, grad_gates.T, *stacked)
 
 
 EARLY = False
@@ -385,7 +385,7 @@
 RETURN_AFTER = 1
 DISPATCH_AFTER_PACK = True
 EXCHANGE_AFTER_GATHER = False
-GATHER_AFTER_PART = True
+GATHER_AFTER_PART = False
 TAIL_WAITS = True
 SERIAL_TAIL = False
 LAG = 1

time: 294 us -> 291 us (0.990)
  local copies, waits for them, and re-layouts: 18.1 us -> 14.9 us
    unnamed x53 -> x50, local copies, waits for them, and re-layouts: 14.8 us -> 11.6 us
  transfers between devices with their start and end apart: 38 -> 38, of which waited for: 15 -> 16; matrix products, arithmetic and copies ran while one was open for 6% -> 5% of each run, Pallas kernels for 11% -> 11%
where the time goes in v4:
time: 291 us; the launch traced here: 290 us
  waiting for transfers between devices  136 us (47%)
  starting transfers between devices  85.8 us (29%)
  Pallas kernels  36.5 us (13%)
  other arithmetic  15.2 us (5%)
  local copies, waits for them, and re-layouts  14.9 us (5%)
    ppermute x9, waiting for transfers between devices, scatter_step(): lax.ppermute(up, 'dp', [(j, j + 1) for j in range(step)])  75.1 us
    ppermute x9, waiting for transfers between devices, gather_step(): lax.ppermute(down, 'dp', [(j, j - 1) for j in range(n - step, 0, -1)])  47.5 us
    ppermute x9, starting transfers between devices, scatter_step(): lax.ppermute(up, 'dp', [(j, j + 1) for j in range(step)])  38.4 us
    pallas_call x3, Pallas kernels, part(): call(functools.partial(part_body, n), 'part', out_shape, [SCALAR, WHOLE]...  23.7 us
    ppermute x9, starting transfers between devices, gather_step(): lax.ppermute(up, 'dp', [(j, j + 1) for j in range(step - 1, n - 1)])  16.5 us
    ppermute x9, starting transfers between devices, gather_step(): lax.ppermute(down, 'dp', [(j, j - 1) for j in range(n - step, 0, -1)])  11.8 us
    unnamed x50, local copies, waits for them, and re-layouts  11.6 us
    ppermute x9, starting transfers between devices, scatter_step(): lax.ppermute(down, 'dp', [(j, j - 1) for j in range(n - 1, n - 1 - step,...  9.94 us
  transfers between devices with their start and end apart: 38, of which 16 were waited for; matrix products, arithmetic and copies ran while one was open for 5% of the time, Pallas kernels for 11%

profile of v4, /device:TPU:0, one launch (start us, length us, event | category | flops | bytes accessed | tf_op | source)
XLA Modules:
  0.0 289.6 jit_solution(10201421166947936765)
XLA Ops:
  3.7 5.1 %collective-permute-start = (bf16[512,768]{1,0:T(8,128)(2,1)S(1)}, bf16[512,768]{1,0:T(8,128)(2,1)S(1)}, u32[]{:S(2)}, u32[]{:S(2)}) collective-permute-start(bf16[512,768]{1,0:T(8,128)(2,1)S(1)} %pad_maximum_fusion.refs_0_), channel_id=1, source_target_pairs={{0,8},{8,16},{16,24},{1,9},{9,17},{17,25},{2,10},{10,18},{18,26},{... | collective-permute-start | bytes 2359304 | tf_op jit(solution)/shard_map/ppermute | solution.py:241
  18.4 7.2 %collective-permute-done.refs_4_ = bf16[512,768]{1,0:T(8,128)(2,1)S(1)} collective-permute-done((bf16[512,768]{1,0:T(8,128)(2,1)S(1)}, bf16[512,768]{1,0:T(8,128)(2,1)S(1)}, u32[]{:S(2)}, u32[]{:S(2)}) %collective-permute-start) | collective-permute-done | bytes 786464 | tf_op jit(solution)/shard_map/ppermute | solution.py:241
  31.9 19.2 %collective-permute-done.4.refs_2_ = bf16[512,768]{1,0:T(8,128)(2,1)S(1)} collective-permute-done((bf16[512,768]{1,0:T(8,128)(2,1)}, bf16[512,768]{1,0:T(8,128)(2,1)S(1)}, u32[]{:S(2)}, u32[]{:S(2)}) %collective-permute-start.4) | collective-permute-done | bytes 786464 | tf_op jit(solution)/shard_map/ppermute | solution.py:242
  53.5 17.1 %collective-permute-done.5.refs_1_.refs_3_ = bf16[512,768]{1,0:T(8,128)(2,1)S(1)} collective-permute-done((bf16[512,768]{1,0:T(8,128)(2,1)S(1)}, bf16[512,768]{1,0:T(8,128)(2,1)S(1)}, u32[]{:S(2)}, u32[]{:S(2)}) %collective-permute-start.5) | collective-permute-done | bytes 786464 | tf_op jit(solution)/shard_map/ppermute | solution.py:242
  71.9 5.4 %collective-permute-start.7 = (bf16[512,768]{1,0:T(8,128)(2,1)S(1)}, bf16[512,768]{1,0:T(8,128)(2,1)}, u32[]{:S(2)}, u32[]{:S(2)}) collective-permute-start(bf16[512,768]{1,0:T(8,128)(2,1)S(1)} %pad_maximum_fusion.1.refs_0_), channel_id=1, source_target_pairs={{0,8},{8,16},{16,24},{1,9},{9,17},{17,25},{2,10},{10,18},{18,26},{... | collective-permute-start | bytes 2359304 | tf_op jit(solution)/shard_map/ppermute | solution.py:241
  85.4 8.3 %part.3 = (bf16[2048,768]{1,0:T(8,128)(2,1)S(1)}, bf16[512,256]{1,0:T(8,128)(2,1)S(1)}, bf16[512,512]{1,0:T(8,128)(2,1)S(1)}, bf16[512,768]{1,0:T(8,128)(2,1)S(1...) custom-call(s32[1]{0:T(128)} %touch.1.index_ref, ...), custom_call_target="tpu_custom_call" | custom-call | flops 3221225472 | bytes 13631488 | tf_op jit(solution)/shard_map/part/pallas_call | solution.py:133
  97.8 11.2 %collective-permute-done.10 = bf16[512,768]{1,0:T(8,128)(2,1)S(1)} collective-permute-done((bf16[512,768]{1,0:T(8,128)(2,1)S(1)}, bf16[512,768]{1,0:T(8,128)(2,1)S(1)}, u32[]{:S(2)}, u32[]{:S(2)}) %collective-permute-start.10) | collective-permute-done | bytes 786464 | tf_op jit(solution)/shard_map/ppermute | solution.py:248
  110.2 5.0 %collective-permute-start.14 = (bf16[512,768]{1,0:T(8,128)(2,1)S(1)}, bf16[512,768]{1,0:T(8,128)(2,1)S(1)}, u32[]{:S(2)}, u32[]{:S(2)}) collective-permute-start(bf16[512,768]{1,0:T(8,128)(2,1)S(1)} %get-tuple-element.94), channel_id=1, source_target_pairs={{0,8},{8,16},{1,9},{9,17},{2,10},{10,18},{3,11},{11,19},{4,12},{12... | collective-permute-start | bytes 2359304 | tf_op jit(solution)/shard_map/ppermute | solution.py:248
  118.9 9.4 %collective-permute-done.14 = bf16[512,768]{1,0:T(8,128)(2,1)S(1)} collective-permute-done((bf16[512,768]{1,0:T(8,128)(2,1)S(1)}, bf16[512,768]{1,0:T(8,128)(2,1)S(1)}, u32[]{:S(2)}, u32[]{:S(2)}) %collective-permute-start.14) | collective-permute-done | bytes 786464 | tf_op jit(solution)/shard_map/ppermute | solution.py:248
  128.3 5.9 %collective-permute-done.12.refs_3_ = bf16[512,768]{1,0:T(8,128)(2,1)S(1)} collective-permute-done((bf16[512,768]{1,0:T(8,128)(2,1)S(1)}, bf16[512,768]{1,0:T(8,128)(2,1)S(1)}, u32[]{:S(2)}, u32[]{:S(2)}) %collective-permute-start.12) | collective-permute-done | bytes 786464 | tf_op jit(solution)/shard_map/ppermute | solution.py:242
  137.4 4.6 %collective-permute-start.18 = (bf16[512,768]{1,0:T(8,128)(2,1)S(1)}, bf16[512,768]{1,0:T(8,128)(2,1)S(1)}, u32[]{:S(2)}, u32[]{:S(2)}) collective-permute-start(bf16[512,768]{1,0:T(8,128)(2,1)S(1)} %add_convert_fusion.8), channel_id=1, source_target_pairs={{0,8},{8,16},{16,24},{1,9},{9,17},{17,25},{2,10},{10,18},{18,26},{... | collective-permute-start | bytes 2359304 | tf_op jit(solution)/shard_map/ppermute | solution.py:248
  142.0 7.7 %part.4 = (bf16[2048,768]{1,0:T(8,128)(2,1)S(1)}, bf16[512,256]{1,0:T(8,128)(2,1)S(1)}, bf16[512,512]{1,0:T(8,128)(2,1)S(1)}, bf16[512,768]{1,0:T(8,128)(2,1)S(1...) custom-call(s32[1]{0:T(128)} %bitcast.index_ref, ...), custom_call_target="tpu_custom_call" | custom-call | flops 3221225472 | bytes 13631488 | tf_op jit(solution)/shard_map/part/pallas_call | solution.py:133
  154.6 16.1 %collective-permute-done.18 = bf16[512,768]{1,0:T(8,128)(2,1)S(1)} collective-permute-done((bf16[512,768]{1,0:T(8,128)(2,1)S(1)}, bf16[512,768]{1,0:T(8,128)(2,1)S(1)}, u32[]{:S(2)}, u32[]{:S(2)}) %collective-permute-start.18) | collective-permute-done | bytes 786464 | tf_op jit(solution)/shard_map/ppermute | solution.py:248
  172.7 11.2 %collective-permute-done.22 = bf16[512,768]{1,0:T(8,128)(2,1)S(1)} collective-permute-done((bf16[512,768]{1,0:T(8,128)(2,1)S(1)}, bf16[512,768]{1,0:T(8,128)(2,1)S(1)}, u32[]{:S(2)}, u32[]{:S(2)}) %collective-permute-start.22) | collective-permute-done | bytes 786464 | tf_op jit(solution)/shard_map/ppermute | solution.py:248
  185.1 5.0 %collective-permute-start.26 = (bf16[512,768]{1,0:T(8,128)(2,1)S(1)}, bf16[512,768]{1,0:T(8,128)(2,1)S(1)}, u32[]{:S(2)}, u32[]{:S(2)}) collective-permute-start(bf16[512,768]{1,0:T(8,128)(2,1)S(1)} %get-tuple-element.92), channel_id=1, source_target_pairs={{0,8},{8,16},{1,9},{9,17},{2,10},{10,18},{3,11},{11,19},{4,12},{12... | collective-permute-start | bytes 2359304 | tf_op jit(solution)/shard_map/ppermute | solution.py:248
  193.8 9.7 %collective-permute-done.26 = bf16[512,768]{1,0:T(8,128)(2,1)S(1)} collective-permute-done((bf16[512,768]{1,0:T(8,128)(2,1)S(1)}, bf16[512,768]{1,0:T(8,128)(2,1)S(1)}, u32[]{:S(2)}, u32[]{:S(2)}) %collective-permute-start.26) | collective-permute-done | bytes 786464 | tf_op jit(solution)/shard_map/ppermute | solution.py:248
  203.7 6.1 %collective-permute-start.28 = (bf16[512,768]{1,0:T(8,128)(2,1)S(1)}, bf16[512,768]{1,0:T(8,128)(2,1)}, u32[]{:S(2)}, u32[]{:S(2)}) collective-permute-start(bf16[512,768]{1,0:T(8,128)(2,1)S(1)} %add_convert_fusion.6), channel_id=1, source_target_pairs={{0,8},{8,16},{16,24},{1,9},{9,17},{17,25},{2,10},{10,18},{18,26},{... | collective-permute-start | bytes 2359304 | tf_op jit(solution)/shard_map/ppermute | solution.py:248
  212.5 7.6 %part.5 = (bf16[2048,768]{1,0:T(8,128)(2,1)S(1)}, bf16[512,256]{1,0:T(8,128)(2,1)S(1)}, bf16[512,512]{1,0:T(8,128)(2,1)S(1)}, bf16[512,768]{1,0:T(8,128)(2,1)S(1...) custom-call(s32[1]{0:T(128)} %bitcast.index_ref, ...), custom_call_target="tpu_custom_call" | custom-call | flops 3221225472 | bytes 13631488 | tf_op jit(solution)/shard_map/part/pallas_call | solution.py:133
  224.0 6.7 %back_products.1 = bf16[8,128,2048]{2,1,0:T(8,128)(2,1)} custom-call(bf16[512,256]{1,0:T(8,128)(2,1)S(1)} %get-tuple-element.44.refs_0_, bf16[512,256]{1,0:T(8,128)(2,1)S(1)} %get-tuple-element.52.refs_1_, bf16[512,256]{1,0:T(8,128)(2,1)S(1)} %get-tuple-element.63.refs_2_, bf16[512,512]{1,0:T(8,128)(2,1)S(1)} %get-tuple-element.64.refs_3_, ...), custom_call_target="tpu_custom_call" | custom-call | flops 4831838208 | bytes 13631488 | tf_op jit(solution)/shard_map/back_products/pallas_call | solution.py:183
  231.6 4.6 %all-to-all-start.1 = ((bf16[8,128,2048]{2,1,0:T(8,128)(2,1)}), bf16[8,128,2048]{2,1,0:T(8,128)(2,1)}, u32[]{:S(2)}, u32[]{:S(2)}) async-start(bf16[8,128,2048]{2,1,0:T(8,128)(2,1)} %back_products.1), calls=%async_computation.1 | async-start | bytes 8388608 | tf_op jit(solution)/shard_map/all_to_all | solution.py:258
  241.6 5.3 %collective-permute-start.31 = (bf16[512,768]{1,0:T(8,128)(2,1)}, bf16[512,768]{1,0:T(8,128)(2,1)}, u32[]{:S(2)}, u32[]{:S(2)}) collective-permute-start(bf16[512,768]{1,0:T(8,128)(2,1)} %get-tuple-element.89), channel_id=1, source_target_pairs={{0,8},{8,16},{1,9},{9,17},{2,10},{10,18},{3,11},{11,19},{4,12},{12... | collective-permute-start | bytes 2359304 | tf_op jit(solution)/shard_map/ppermute | solution.py:248
  250.2 8.4 %collective-permute-done.31 = bf16[512,768]{1,0:T(8,128)(2,1)} collective-permute-done((bf16[512,768]{1,0:T(8,128)(2,1)}, bf16[512,768]{1,0:T(8,128)(2,1)}, u32[]{:S(2)}, u32[]{:S(2)}) %collective-permute-start.31) | collective-permute-done | bytes 786464 | tf_op jit(solution)/shard_map/ppermute | solution.py:248
  269.2 6.9 %collective-permute-done.32 = bf16[512,768]{1,0:T(8,128)(2,1)S(1)} collective-permute-done((bf16[512,768]{1,0:T(8,128)(2,1)S(1)}, bf16[512,768]{1,0:T(8,128)(2,1)S(1)}, u32[]{:S(2)}, u32[]{:S(2)}) %collective-permute-start.32) | collective-permute-done | bytes 786464 | tf_op jit(solution)/shard_map/ppermute | solution.py:248
  276.1 5.7 %collective-permute-done.35 = bf16[512,768]{1,0:T(8,128)(2,1)S(1)} collective-permute-done((bf16[512,768]{1,0:T(8,128)(2,1)S(1)}, bf16[512,768]{1,0:T(8,128)(2,1)S(1)}, u32[]{:S(2)}, u32[]{:S(2)}) %collective-permute-start.35) | collective-permute-done | bytes 786464 | tf_op jit(solution)/shard_map/ppermute | solution.py:249
  (136 shorter events, 88.8 us)
Async XLA Ops:
  3.7 21.8 %collective-permute-start = (bf16[512,768]{1,0:T(8,128)(2,1)S(1)}, bf16[512,768]{1,0:T(8,128)(2,1)S(1)}, u32[]{:S(2)}, u32[]{:S(2)}) collective-permute-start(bf16[512,768]{1,0:T(8,128)(2,1)S(1)} %pad_maximum_fusion.refs_0_), channel_id=1, source_target_pairs={{0,8},{8,16},{16,24},{1,9},{9,17},{17,25},{2,10},{10,18},{18,26},{... | collective-permute-start | bytes 2359304 | tf_op jit(solution)/shard_map/ppermute | solution.py:241
  8.8 21.0 %collective-permute-start.3 = (bf16[512,768]{1,0:T(8,128)(2,1)S(1)}, bf16[512,768]{1,0:T(8,128)(2,1)}, u32[]{:S(2)}, u32[]{:S(2)}) collective-permute-start(bf16[512,768]{1,0:T(8,128)(2,1)S(1)} %pad_maximum_fusion.refs_0_), channel_id=1, source_target_pairs={{24,16},{16,8},{8,0},{25,17},{17,9},{9,1},{26,18},{18,10},{10,2},{... | collective-permute-start | bytes 2359304 | tf_op jit(solution)/shard_map/ppermute | solution.py:242
  13.8 65.9 %all-to-all-start = ((bf16[8,128,2048]{2,1,0:T(8,128)(2,1)}), bf16[8,128,2048]{2,1,0:T(8,128)(2,1)}, u32[]{:S(2)}, u32[]{:S(2)}) async-start(bf16[8,128,2048]{2,1,0:T(8,128)(2,1)} %copy-done), calls=%async_computation | async-start | bytes 8388608 | tf_op jit(solution)/shard_map/all_to_all | solution.py:258
  29.8 21.2 %collective-permute-start.4 = (bf16[512,768]{1,0:T(8,128)(2,1)}, bf16[512,768]{1,0:T(8,128)(2,1)S(1)}, u32[]{:S(2)}, u32[]{:S(2)}) collective-permute-start(bf16[512,768]{1,0:T(8,128)(2,1)} %collective-permute-done.3.refs_1_), channel_id=1, source_target_pairs={{16,8},{8,0},{17,9},{9,1},{18,10},{10,2},{19,11},{11,3},{20,12},{1... | collective-permute-start | bytes 2359304 | tf_op jit(solution)/shard_map/ppermute | solution.py:242
  31.1 22.4 %collective-permute-start.2 = (bf16[512,768]{1,0:T(8,128)(2,1)S(1)}, bf16[512,768]{1,0:T(8,128)(2,1)S(1)}, u32[]{:S(2)}, u32[]{:S(2)}) collective-permute-start(bf16[512,768]{1,0:T(8,128)(2,1)S(1)} %collective-permute-done.1.refs_5_), channel_id=1, source_target_pairs={{16,24},{17,25},{18,26},{19,27},{20,28},{21,29},{22,30},{23,31}} | collective-permute-start | bytes 2359304 | tf_op jit(solution)/shard_map/ppermute | solution.py:241
  51.0 19.6 %collective-permute-start.5 = (bf16[512,768]{1,0:T(8,128)(2,1)S(1)}, bf16[512,768]{1,0:T(8,128)(2,1)S(1)}, u32[]{:S(2)}, u32[]{:S(2)}) collective-permute-start(bf16[512,768]{1,0:T(8,128)(2,1)S(1)} %collective-permute-done.4.refs_2_), channel_id=1, source_target_pairs={{8,0},{9,1},{10,2},{11,3},{12,4},{13,5},{14,6},{15,7}} | collective-permute-start | bytes 2359304 | tf_op jit(solution)/shard_map/ppermute | solution.py:242
  70.6 25.2 %collective-permute-start.6 = (bf16[512,768]{1,0:T(8,128)(2,1)S(1)}, bf16[512,768]{1,0:T(8,128)(2,1)}, u32[]{:S(2)}, u32[]{:S(2)}) collective-permute-start(bf16[512,768]{1,0:T(8,128)(2,1)S(1)} %pad_maximum_fusion.1.refs_0_), channel_id=1, source_target_pairs={{24,16},{16,8},{8,0},{25,17},{17,9},{9,1},{26,18},{18,10},{10,2},{... | collective-permute-start | bytes 2359304 | tf_op jit(solution)/shard_map/ppermute | solution.py:242
  71.9 23.9 %collective-permute-start.7 = (bf16[512,768]{1,0:T(8,128)(2,1)S(1)}, bf16[512,768]{1,0:T(8,128)(2,1)}, u32[]{:S(2)}, u32[]{:S(2)}) collective-permute-start(bf16[512,768]{1,0:T(8,128)(2,1)S(1)} %pad_maximum_fusion.1.refs_0_), channel_id=1, source_target_pairs={{0,8},{8,16},{16,24},{1,9},{9,17},{17,25},{2,10},{10,18},{18,26},{... | collective-permute-start | bytes 2359304 | tf_op jit(solution)/shard_map/ppermute | solution.py:241
  95.8 19.4 %collective-permute-start.9 = (bf16[512,768]{1,0:T(8,128)(2,1)}, bf16[512,768]{1,0:T(8,128)(2,1)S(1)}, u32[]{:S(2)}, u32[]{:S(2)}) collective-permute-start(bf16[512,768]{1,0:T(8,128)(2,1)} %collective-permute-done.7.refs_4_), channel_id=1, source_target_pairs={{8,16},{16,24},{9,17},{17,25},{10,18},{18,26},{11,19},{19,27},{12,... | collective-permute-start | bytes 2359304 | tf_op jit(solution)/shard_map/ppermute | solution.py:241
  96.5 18.7 %collective-permute-start.8 = (bf16[512,768]{1,0:T(8,128)(2,1)}, bf16[512,768]{1,0:T(8,128)(2,1)S(1)}, u32[]{:S(2)}, u32[]{:S(2)}) collective-permute-start(bf16[512,768]{1,0:T(8,128)(2,1)} %collective-permute-done.6.refs_1_), channel_id=1, source_target_pairs={{16,8},{8,0},{17,9},{9,1},{18,10},{10,2},{19,11},{11,3},{20,12},{1... | collective-permute-start | bytes 2359304 | tf_op jit(solution)/shard_map/ppermute | solution.py:242
  117.5 36.3 %collective-permute-start.19 = (bf16[512,768]{1,0:T(8,128)(2,1)S(1)}, bf16[512,768]{1,0:T(8,128)(2,1)S(1)}, u32[]{:S(2)}, u32[]{:S(2)}) collective-permute-start(bf16[512,768]{1,0:T(8,128)(2,1)S(1)} %add_convert_fusion.7), channel_id=1, source_target_pairs={{24,16},{16,8},{8,0},{25,17},{17,9},{9,1},{26,18},{18,10},{10,2},{... | collective-permute-start | bytes 2359304 | tf_op jit(solution)/shard_map/ppermute | solution.py:249
  134.2 36.6 %collective-permute-start.16 = (bf16[512,768]{1,0:T(8,128)(2,1)S(1)}, bf16[512,768]{1,0:T(8,128)(2,1)S(1)}, u32[]{:S(2)}, u32[]{:S(2)}) collective-permute-start(bf16[512,768]{1,0:T(8,128)(2,1)S(1)} %pad_maximum_fusion.2.refs_0_), channel_id=1, source_target_pairs={{0,8},{8,16},{16,24},{1,9},{9,17},{17,25},{2,10},{10,18},{18,26},{... | collective-permute-start | bytes 2359304 | tf_op jit(solution)/shard_map/ppermute | solution.py:241
  135.9 34.8 %collective-permute-start.17 = (bf16[512,768]{1,0:T(8,128)(2,1)S(1)}, bf16[512,768]{1,0:T(8,128)(2,1)S(1)}, u32[]{:S(2)}, u32[]{:S(2)}) collective-permute-start(bf16[512,768]{1,0:T(8,128)(2,1)S(1)} %pad_maximum_fusion.2.refs_0_), channel_id=1, source_target_pairs={{24,16},{16,8},{8,0},{25,17},{17,9},{9,1},{26,18},{18,10},{10,2},{... | collective-permute-start | bytes 2359304 | tf_op jit(solution)/shard_map/ppermute | solution.py:242
  137.4 33.3 %collective-permute-start.18 = (bf16[512,768]{1,0:T(8,128)(2,1)S(1)}, bf16[512,768]{1,0:T(8,128)(2,1)S(1)}, u32[]{:S(2)}, u32[]{:S(2)}) collective-permute-start(bf16[512,768]{1,0:T(8,128)(2,1)S(1)} %add_convert_fusion.8), channel_id=1, source_target_pairs={{0,8},{8,16},{16,24},{1,9},{9,17},{17,25},{2,10},{10,18},{18,26},{... | collective-permute-start | bytes 2359304 | tf_op jit(solution)/shard_map/ppermute | solution.py:248
  149.7 34.3 %collective-permute-start.22 = (bf16[512,768]{1,0:T(8,128)(2,1)S(1)}, bf16[512,768]{1,0:T(8,128)(2,1)S(1)}, u32[]{:S(2)}, u32[]{:S(2)}) collective-permute-start(bf16[512,768]{1,0:T(8,128)(2,1)S(1)} %get-tuple-element.57), channel_id=1, source_target_pairs={{0,8},{1,9},{2,10},{3,11},{4,12},{5,13},{6,14},{7,15}} | collective-permute-start | bytes 2359304 | tf_op jit(solution)/shard_map/ppermute | solution.py:248
  153.9 30.1 %collective-permute-start.23 = (bf16[512,768]{1,0:T(8,128)(2,1)S(1)}, bf16[512,768]{1,0:T(8,128)(2,1)S(1)}, u32[]{:S(2)}, u32[]{:S(2)}) collective-permute-start(bf16[512,768]{1,0:T(8,128)(2,1)S(1)} %get-tuple-element.58), channel_id=1, source_target_pairs={{24,16},{25,17},{26,18},{27,19},{28,20},{29,21},{30,22},{31,23}} | collective-permute-start | bytes 2359304 | tf_op jit(solution)/shard_map/ppermute | solution.py:249
  170.7 19.4 %collective-permute-start.21 = (bf16[512,768]{1,0:T(8,128)(2,1)S(1)}, bf16[512,768]{1,0:T(8,128)(2,1)S(1)}, u32[]{:S(2)}, u32[]{:S(2)}) collective-permute-start(bf16[512,768]{1,0:T(8,128)(2,1)S(1)} %collective-permute-done.17.refs_1_), channel_id=1, source_target_pairs={{16,8},{8,0},{17,9},{9,1},{18,10},{10,2},{19,11},{11,3},{20,12},{1... | collective-permute-start | bytes 2359304 | tf_op jit(solution)/shard_map/ppermute | solution.py:242
  185.1 18.4 %collective-permute-start.26 = (bf16[512,768]{1,0:T(8,128)(2,1)S(1)}, bf16[512,768]{1,0:T(8,128)(2,1)S(1)}, u32[]{:S(2)}, u32[]{:S(2)}) collective-permute-start(bf16[512,768]{1,0:T(8,128)(2,1)S(1)} %get-tuple-element.92), channel_id=1, source_target_pairs={{0,8},{8,16},{1,9},{9,17},{2,10},{10,18},{3,11},{11,19},{4,12},{12... | collective-permute-start | bytes 2359304 | tf_op jit(solution)/shard_map/ppermute | solution.py:248
  190.1 22.3 %collective-permute-start.25 = (bf16[512,768]{1,0:T(8,128)(2,1)S(1)}, bf16[512,768]{1,0:T(8,128)(2,1)S(1)}, u32[]{:S(2)}, u32[]{:S(2)}) collective-permute-start(bf16[512,768]{1,0:T(8,128)(2,1)S(1)} %collective-permute-done.21.refs_2_), channel_id=1, source_target_pairs={{8,0},{9,1},{10,2},{11,3},{12,4},{13,5},{14,6},{15,7}} | collective-permute-start | bytes 2359304 | tf_op jit(solution)/shard_map/ppermute | solution.py:242
  191.6 20.9 %collective-permute-start.24 = (bf16[512,768]{1,0:T(8,128)(2,1)S(1)}, bf16[512,768]{1,0:T(8,128)(2,1)S(1)}, u32[]{:S(2)}, u32[]{:S(2)}) collective-permute-start(bf16[512,768]{1,0:T(8,128)(2,1)S(1)} %collective-permute-done.20.refs_5_), channel_id=1, source_target_pairs={{16,24},{17,25},{18,26},{19,27},{20,28},{21,29},{22,30},{23,31}} | collective-permute-start | bytes 2359304 | tf_op jit(solution)/shard_map/ppermute | solution.py:241
  192.5 38.2 %collective-permute-start.29 = (bf16[512,768]{1,0:T(8,128)(2,1)S(1)}, bf16[512,768]{1,0:T(8,128)(2,1)S(1)}, u32[]{:S(2)}, u32[]{:S(2)}) collective-permute-start(bf16[512,768]{1,0:T(8,128)(2,1)S(1)} %add_convert_fusion.5), channel_id=1, source_target_pairs={{24,16},{16,8},{8,0},{25,17},{17,9},{9,1},{26,18},{18,10},{10,2},{... | collective-permute-start | bytes 2359304 | tf_op jit(solution)/shard_map/ppermute | solution.py:249
  203.7 27.9 %collective-permute-start.28 = (bf16[512,768]{1,0:T(8,128)(2,1)S(1)}, bf16[512,768]{1,0:T(8,128)(2,1)}, u32[]{:S(2)}, u32[]{:S(2)}) collective-permute-start(bf16[512,768]{1,0:T(8,128)(2,1)S(1)} %add_convert_fusion.6), channel_id=1, source_target_pairs={{0,8},{8,16},{16,24},{1,9},{9,17},{17,25},{2,10},{10,18},{18,26},{... | collective-permute-start | bytes 2359304 | tf_op jit(solution)/shard_map/ppermute | solution.py:248
  220.1 18.3 %collective-permute-start.30 = (bf16[512,768]{1,0:T(8,128)(2,1)}, bf16[512,768]{1,0:T(8,128)(2,1)}, u32[]{:S(2)}, u32[]{:S(2)}) collective-permute-start(bf16[512,768]{1,0:T(8,128)(2,1)} %get-tuple-element.76), channel_id=1, source_target_pairs={{0,8},{1,9},{2,10},{3,11},{4,12},{5,13},{6,14},{7,15}} | collective-permute-start | bytes 2359304 | tf_op jit(solution)/shard_map/ppermute | solution.py:248
  231.6 53.7 %all-to-all-start.1 = ((bf16[8,128,2048]{2,1,0:T(8,128)(2,1)}), bf16[8,128,2048]{2,1,0:T(8,128)(2,1)}, u32[]{:S(2)}, u32[]{:S(2)}) async-start(bf16[8,128,2048]{2,1,0:T(8,128)(2,1)} %back_products.1), calls=%async_computation.1 | async-start | bytes 8388608 | tf_op jit(solution)/shard_map/all_to_all | solution.py:258
  (38 other events, 381.5 us)

commit v5 on v4

--- a/solution.py
+++ b/solution.py
@@ -302,14 +302,18 @@
     spans = [slice(a, b) for a, b in zip(edges, edges[1:])]
     count = len(spans)
 
-    owns = [jnp.concatenate([w[0, :, s] for w in (w_gate, w_up, w_down)], axis=1) for s in spans]
+    def pack(span, weights):
+        return jnp.concatenate([w[0, :, span] for w in weights], axis=1)
+
+    weights = (w_gate, w_up, w_down)
+    own = pack(spans[0], weights)
     target = expert_ids * capacity + slot_index
     if DISPATCH_AFTER_PACK:
-        target = after(target, owns[0])
+        target = after(target, own)
     sent = dispatch(index, target.T, routing_gates.T, tokens, grad_out, experts, capacity, n)
 
     fulls, hids, boths = [], [], []
-    gathers = [Gather(own, n) for own in owns]
+    gathers = [Gather(own, n)]
     scatters = []
 
     def run_part(c, waits=()):
@@ -322,6 +326,8 @@
         scatters.append([Scatter(terms, n)])
 
     gathers[0].go()
+    weights = [after(w, *gathers[0].last) for w in weights]
+    gathers += [Gather(pack(span, weights), n) for span in spans[1:]]
     if EXCHANGE_AFTER_GATHER:
         sent = after(sent, *gathers[0].last)
     rows = exchange(sent)

time: 291 us -> 290 us (level)
  transfers between devices with their start and end apart: 38 -> 38, of which waited for: 16 -> 16; matrix products, arithmetic and copies ran while one was open for 5% -> 6% of each run, Pallas kernels for 11% -> 11%
where the time goes in v5:
time: 290 us; the launch traced here: 288 us
  waiting for transfers between devices  134 us (46%)
  starting transfers between devices  86.9 us (30%)
  Pallas kernels  36.5 us (13%)
  local copies, waits for them, and re-layouts  15 us (5%)
  other arithmetic  14.2 us (5%)
    ppermute x9, waiting for transfers between devices, scatter_step(): lax.ppermute(up, 'dp', [(j, j + 1) for j in range(step)])  74.9 us
    ppermute x9, waiting for transfers between devices, gather_step(): lax.ppermute(down, 'dp', [(j, j - 1) for j in range(n - step, 0, -1)])  46.1 us
    ppermute x9, starting transfers between devices, scatter_step(): lax.ppermute(up, 'dp', [(j, j + 1) for j in range(step)])  38.4 us
    pallas_call x3, Pallas kernels, part(): call(functools.partial(part_body, n), 'part', out_shape, [SCALAR, WHOLE]...  23.7 us
    ppermute x9, starting transfers between devices, gather_step(): lax.ppermute(up, 'dp', [(j, j + 1) for j in range(step - 1, n - 1)])  17.5 us
    ppermute x9, starting transfers between devices, gather_step(): lax.ppermute(down, 'dp', [(j, j - 1) for j in range(n - step, 0, -1)])  11.8 us
    unnamed x50, local copies, waits for them, and re-layouts  10.7 us
    ppermute x9, starting transfers between devices, scatter_step(): lax.ppermute(down, 'dp', [(j, j - 1) for j in range(n - 1, n - 1 - step,...  9.95 us
  transfers between devices with their start and end apart: 38, of which 16 were waited for; matrix products, arithmetic and copies ran while one was open for 6% of the time, Pallas kernels for 11%

profile of v5, /device:TPU:0, one launch (start us, length us, event | category | flops | bytes accessed | tf_op | source)
XLA Modules:
  0.0 287.8 jit_solution(13530467997636556079)
XLA Ops:
  2.9 5.0 %collective-permute-start = (bf16[512,768]{1,0:T(8,128)(2,1)S(1)}, bf16[512,768]{1,0:T(8,128)(2,1)S(1)}, u32[]{:S(2)}, u32[]{:S(2)}) collective-permute-start(bf16[512,768]{1,0:T(8,128)(2,1)S(1)} %pad_maximum_fusion.refs_0_), channel_id=1, source_target_pairs={{0,8},{8,16},{16,24},{1,9},{9,17},{17,25},{2,10},{10,18},{18,26},{... | collective-permute-start | bytes 2359304 | tf_op jit(solution)/shard_map/ppermute | solution.py:241
  12.8 4.7 %all-to-all-start = ((bf16[8,128,2048]{2,1,0:T(8,128)(2,1)}), bf16[8,128,2048]{2,1,0:T(8,128)(2,1)}, u32[]{:S(2)}, u32[]{:S(2)}) async-start(bf16[8,128,2048]{2,1,0:T(8,128)(2,1)} %copy-done), calls=%async_computation | async-start | bytes 8388608 | tf_op jit(solution)/shard_map/all_to_all | solution.py:258
  17.6 7.0 %collective-permute-done.refs_4_ = bf16[512,768]{1,0:T(8,128)(2,1)S(1)} collective-permute-done((bf16[512,768]{1,0:T(8,128)(2,1)S(1)}, bf16[512,768]{1,0:T(8,128)(2,1)S(1)}, u32[]{:S(2)}, u32[]{:S(2)}) %collective-permute-start) | collective-permute-done | bytes 786464 | tf_op jit(solution)/shard_map/ppermute | solution.py:241
  30.9 18.3 %collective-permute-done.4.refs_2_ = bf16[512,768]{1,0:T(8,128)(2,1)S(1)} collective-permute-done((bf16[512,768]{1,0:T(8,128)(2,1)}, bf16[512,768]{1,0:T(8,128)(2,1)S(1)}, u32[]{:S(2)}, u32[]{:S(2)}) %collective-permute-start.4) | collective-permute-done | bytes 786464 | tf_op jit(solution)/shard_map/ppermute | solution.py:242
  52.5 16.1 %collective-permute-done.5.refs_1_.refs_3_ = bf16[512,768]{1,0:T(8,128)(2,1)S(1)} collective-permute-done((bf16[512,768]{1,0:T(8,128)(2,1)S(1)}, bf16[512,768]{1,0:T(8,128)(2,1)S(1)}, u32[]{:S(2)}, u32[]{:S(2)}) %collective-permute-start.5) | collective-permute-done | bytes 786464 | tf_op jit(solution)/shard_map/ppermute | solution.py:242
  69.8 5.4 %collective-permute-start.7 = (bf16[512,768]{1,0:T(8,128)(2,1)S(1)}, bf16[512,768]{1,0:T(8,128)(2,1)}, u32[]{:S(2)}, u32[]{:S(2)}) collective-permute-start(bf16[512,768]{1,0:T(8,128)(2,1)S(1)} %pad_maximum_fusion.1.refs_0_), channel_id=1, source_target_pairs={{0,8},{8,16},{16,24},{1,9},{9,17},{17,25},{2,10},{10,18},{18,26},{... | collective-permute-start | bytes 2359304 | tf_op jit(solution)/shard_map/ppermute | solution.py:241
  83.3 8.3 %part.3 = (bf16[2048,768]{1,0:T(8,128)(2,1)S(1)}, bf16[512,256]{1,0:T(8,128)(2,1)S(1)}, bf16[512,512]{1,0:T(8,128)(2,1)S(1)}, bf16[512,768]{1,0:T(8,128)(2,1)S(1...) custom-call(s32[1]{0:T(128)} %touch.1.index_ref, ...), custom_call_target="tpu_custom_call" | custom-call | flops 3221225472 | bytes 13631488 | tf_op jit(solution)/shard_map/part/pallas_call | solution.py:133
  95.7 11.0 %collective-permute-done.10 = bf16[512,768]{1,0:T(8,128)(2,1)S(1)} collective-permute-done((bf16[512,768]{1,0:T(8,128)(2,1)S(1)}, bf16[512,768]{1,0:T(8,128)(2,1)S(1)}, u32[]{:S(2)}, u32[]{:S(2)}) %collective-permute-start.10) | collective-permute-done | bytes 786464 | tf_op jit(solution)/shard_map/ppermute | solution.py:248
  108.0 5.0 %collective-permute-start.14 = (bf16[512,768]{1,0:T(8,128)(2,1)S(1)}, bf16[512,768]{1,0:T(8,128)(2,1)S(1)}, u32[]{:S(2)}, u32[]{:S(2)}) collective-permute-start(bf16[512,768]{1,0:T(8,128)(2,1)S(1)} %get-tuple-element.100), channel_id=1, source_target_pairs={{0,8},{8,16},{1,9},{9,17},{2,10},{10,18},{3,11},{11,19},{4,12},{12... | collective-permute-start | bytes 2359304 | tf_op jit(solution)/shard_map/ppermute | solution.py:248
  116.7 9.2 %collective-permute-done.14 = bf16[512,768]{1,0:T(8,128)(2,1)S(1)} collective-permute-done((bf16[512,768]{1,0:T(8,128)(2,1)S(1)}, bf16[512,768]{1,0:T(8,128)(2,1)S(1)}, u32[]{:S(2)}, u32[]{:S(2)}) %collective-permute-start.14) | collective-permute-done | bytes 786464 | tf_op jit(solution)/shard_map/ppermute | solution.py:248
  125.9 5.4 %collective-permute-done.12.refs_3_ = bf16[512,768]{1,0:T(8,128)(2,1)S(1)} collective-permute-done((bf16[512,768]{1,0:T(8,128)(2,1)S(1)}, bf16[512,768]{1,0:T(8,128)(2,1)S(1)}, u32[]{:S(2)}, u32[]{:S(2)}) %collective-permute-start.12) | collective-permute-done | bytes 786464 | tf_op jit(solution)/shard_map/ppermute | solution.py:242
  135.7 4.6 %collective-permute-start.18 = (bf16[512,768]{1,0:T(8,128)(2,1)S(1)}, bf16[512,768]{1,0:T(8,128)(2,1)S(1)}, u32[]{:S(2)}, u32[]{:S(2)}) collective-permute-start(bf16[512,768]{1,0:T(8,128)(2,1)S(1)} %add_convert_fusion.8), channel_id=1, source_target_pairs={{0,8},{8,16},{16,24},{1,9},{9,17},{17,25},{2,10},{10,18},{18,26},{... | collective-permute-start | bytes 2359304 | tf_op jit(solution)/shard_map/ppermute | solution.py:248
  140.3 7.7 %part.4 = (bf16[2048,768]{1,0:T(8,128)(2,1)S(1)}, bf16[512,256]{1,0:T(8,128)(2,1)S(1)}, bf16[512,512]{1,0:T(8,128)(2,1)S(1)}, bf16[512,768]{1,0:T(8,128)(2,1)S(1...) custom-call(s32[1]{0:T(128)} %bitcast.index_ref, ...), custom_call_target="tpu_custom_call" | custom-call | flops 3221225472 | bytes 13631488 | tf_op jit(solution)/shard_map/part/pallas_call | solution.py:133
  152.9 16.1 %collective-permute-done.18 = bf16[512,768]{1,0:T(8,128)(2,1)S(1)} collective-permute-done((bf16[512,768]{1,0:T(8,128)(2,1)S(1)}, bf16[512,768]{1,0:T(8,128)(2,1)S(1)}, u32[]{:S(2)}, u32[]{:S(2)}) %collective-permute-start.18) | collective-permute-done | bytes 786464 | tf_op jit(solution)/shard_map/ppermute | solution.py:248
  171.0 11.1 %collective-permute-done.22 = bf16[512,768]{1,0:T(8,128)(2,1)S(1)} collective-permute-done((bf16[512,768]{1,0:T(8,128)(2,1)S(1)}, bf16[512,768]{1,0:T(8,128)(2,1)S(1)}, u32[]{:S(2)}, u32[]{:S(2)}) %collective-permute-start.22) | collective-permute-done | bytes 786464 | tf_op jit(solution)/shard_map/ppermute | solution.py:248
  183.2 5.0 %collective-permute-start.26 = (bf16[512,768]{1,0:T(8,128)(2,1)S(1)}, bf16[512,768]{1,0:T(8,128)(2,1)S(1)}, u32[]{:S(2)}, u32[]{:S(2)}) collective-permute-start(bf16[512,768]{1,0:T(8,128)(2,1)S(1)} %get-tuple-element.98), channel_id=1, source_target_pairs={{0,8},{8,16},{1,9},{9,17},{2,10},{10,18},{3,11},{11,19},{4,12},{12... | collective-permute-start | bytes 2359304 | tf_op jit(solution)/shard_map/ppermute | solution.py:248
  192.0 9.6 %collective-permute-done.26 = bf16[512,768]{1,0:T(8,128)(2,1)S(1)} collective-permute-done((bf16[512,768]{1,0:T(8,128)(2,1)S(1)}, bf16[512,768]{1,0:T(8,128)(2,1)S(1)}, u32[]{:S(2)}, u32[]{:S(2)}) %collective-permute-start.26) | collective-permute-done | bytes 786464 | tf_op jit(solution)/shard_map/ppermute | solution.py:248
  201.7 6.1 %collective-permute-start.28 = (bf16[512,768]{1,0:T(8,128)(2,1)S(1)}, bf16[512,768]{1,0:T(8,128)(2,1)}, u32[]{:S(2)}, u32[]{:S(2)}) collective-permute-start(bf16[512,768]{1,0:T(8,128)(2,1)S(1)} %add_convert_fusion.6), channel_id=1, source_target_pairs={{0,8},{8,16},{16,24},{1,9},{9,17},{17,25},{2,10},{10,18},{18,26},{... | collective-permute-start | bytes 2359304 | tf_op jit(solution)/shard_map/ppermute | solution.py:248
  210.6 7.6 %part.5 = (bf16[2048,768]{1,0:T(8,128)(2,1)S(1)}, bf16[512,256]{1,0:T(8,128)(2,1)S(1)}, bf16[512,512]{1,0:T(8,128)(2,1)S(1)}, bf16[512,768]{1,0:T(8,128)(2,1)S(1...) custom-call(s32[1]{0:T(128)} %bitcast.index_ref, ...), custom_call_target="tpu_custom_call" | custom-call | flops 3221225472 | bytes 13631488 | tf_op jit(solution)/shard_map/part/pallas_call | solution.py:133
  222.1 6.7 %back_products.1 = bf16[8,128,2048]{2,1,0:T(8,128)(2,1)} custom-call(bf16[512,256]{1,0:T(8,128)(2,1)S(1)} %get-tuple-element.47.refs_0_, bf16[512,256]{1,0:T(8,128)(2,1)S(1)} %get-tuple-element.58.refs_1_, bf16[512,256]{1,0:T(8,128)(2,1)S(1)} %get-tuple-element.69.refs_2_, bf16[512,512]{1,0:T(8,128)(2,1)S(1)} %get-tuple-element.70.refs_3_, ...), custom_call_target="tpu_custom_call" | custom-call | flops 4831838208 | bytes 13631488 | tf_op jit(solution)/shard_map/back_products/pallas_call | solution.py:183
  239.5 5.3 %collective-permute-start.31 = (bf16[512,768]{1,0:T(8,128)(2,1)}, bf16[512,768]{1,0:T(8,128)(2,1)}, u32[]{:S(2)}, u32[]{:S(2)}) collective-permute-start(bf16[512,768]{1,0:T(8,128)(2,1)} %get-tuple-element.95), channel_id=1, source_target_pairs={{0,8},{8,16},{1,9},{9,17},{2,10},{10,18},{3,11},{11,19},{4,12},{12... | collective-permute-start | bytes 2359304 | tf_op jit(solution)/shard_map/ppermute | solution.py:248
  248.1 8.7 %collective-permute-done.31 = bf16[512,768]{1,0:T(8,128)(2,1)} collective-permute-done((bf16[512,768]{1,0:T(8,128)(2,1)}, bf16[512,768]{1,0:T(8,128)(2,1)}, u32[]{:S(2)}, u32[]{:S(2)}) %collective-permute-start.31) | collective-permute-done | bytes 786464 | tf_op jit(solution)/shard_map/ppermute | solution.py:248
  267.4 7.2 %collective-permute-done.32 = bf16[512,768]{1,0:T(8,128)(2,1)S(1)} collective-permute-done((bf16[512,768]{1,0:T(8,128)(2,1)S(1)}, bf16[512,768]{1,0:T(8,128)(2,1)S(1)}, u32[]{:S(2)}, u32[]{:S(2)}) %collective-permute-start.32) | collective-permute-done | bytes 786464 | tf_op jit(solution)/shard_map/ppermute | solution.py:248
  274.5 5.7 %collective-permute-done.35 = bf16[512,768]{1,0:T(8,128)(2,1)S(1)} collective-permute-done((bf16[512,768]{1,0:T(8,128)(2,1)S(1)}, bf16[512,768]{1,0:T(8,128)(2,1)S(1)}, u32[]{:S(2)}, u32[]{:S(2)}) %collective-permute-start.35) | collective-permute-done | bytes 786464 | tf_op jit(solution)/shard_map/ppermute | solution.py:249
  (139 shorter events, 89.5 us)
Async XLA Ops:
  2.9 21.7 %collective-permute-start = (bf16[512,768]{1,0:T(8,128)(2,1)S(1)}, bf16[512,768]{1,0:T(8,128)(2,1)S(1)}, u32[]{:S(2)}, u32[]{:S(2)}) collective-permute-start(bf16[512,768]{1,0:T(8,128)(2,1)S(1)} %pad_maximum_fusion.refs_0_), channel_id=1, source_target_pairs={{0,8},{8,16},{16,24},{1,9},{9,17},{17,25},{2,10},{10,18},{18,26},{... | collective-permute-start | bytes 2359304 | tf_op jit(solution)/shard_map/ppermute | solution.py:241
  7.9 21.0 %collective-permute-start.3 = (bf16[512,768]{1,0:T(8,128)(2,1)S(1)}, bf16[512,768]{1,0:T(8,128)(2,1)}, u32[]{:S(2)}, u32[]{:S(2)}) collective-permute-start(bf16[512,768]{1,0:T(8,128)(2,1)S(1)} %pad_maximum_fusion.refs_0_), channel_id=1, source_target_pairs={{24,16},{16,8},{8,0},{25,17},{17,9},{9,1},{26,18},{18,10},{10,2},{... | collective-permute-start | bytes 2359304 | tf_op jit(solution)/shard_map/ppermute | solution.py:242
  12.8 64.8 %all-to-all-start = ((bf16[8,128,2048]{2,1,0:T(8,128)(2,1)}), bf16[8,128,2048]{2,1,0:T(8,128)(2,1)}, u32[]{:S(2)}, u32[]{:S(2)}) async-start(bf16[8,128,2048]{2,1,0:T(8,128)(2,1)} %copy-done), calls=%async_computation | async-start | bytes 8388608 | tf_op jit(solution)/shard_map/all_to_all | solution.py:258
  28.9 20.4 %collective-permute-start.4 = (bf16[512,768]{1,0:T(8,128)(2,1)}, bf16[512,768]{1,0:T(8,128)(2,1)S(1)}, u32[]{:S(2)}, u32[]{:S(2)}) collective-permute-start(bf16[512,768]{1,0:T(8,128)(2,1)} %collective-permute-done.3.refs_1_), channel_id=1, source_target_pairs={{16,8},{8,0},{17,9},{9,1},{18,10},{10,2},{19,11},{11,3},{20,12},{1... | collective-permute-start | bytes 2359304 | tf_op jit(solution)/shard_map/ppermute | solution.py:242
  30.2 22.3 %collective-permute-start.2 = (bf16[512,768]{1,0:T(8,128)(2,1)S(1)}, bf16[512,768]{1,0:T(8,128)(2,1)S(1)}, u32[]{:S(2)}, u32[]{:S(2)}) collective-permute-start(bf16[512,768]{1,0:T(8,128)(2,1)S(1)} %collective-permute-done.1.refs_5_), channel_id=1, source_target_pairs={{16,24},{17,25},{18,26},{19,27},{20,28},{21,29},{22,30},{23,31}} | collective-permute-start | bytes 2359304 | tf_op jit(solution)/shard_map/ppermute | solution.py:241
  49.2 19.3 %collective-permute-start.5 = (bf16[512,768]{1,0:T(8,128)(2,1)S(1)}, bf16[512,768]{1,0:T(8,128)(2,1)S(1)}, u32[]{:S(2)}, u32[]{:S(2)}) collective-permute-start(bf16[512,768]{1,0:T(8,128)(2,1)S(1)} %collective-permute-done.4.refs_2_), channel_id=1, source_target_pairs={{8,0},{9,1},{10,2},{11,3},{12,4},{13,5},{14,6},{15,7}} | collective-permute-start | bytes 2359304 | tf_op jit(solution)/shard_map/ppermute | solution.py:242
  68.6 25.1 %collective-permute-start.6 = (bf16[512,768]{1,0:T(8,128)(2,1)S(1)}, bf16[512,768]{1,0:T(8,128)(2,1)}, u32[]{:S(2)}, u32[]{:S(2)}) collective-permute-start(bf16[512,768]{1,0:T(8,128)(2,1)S(1)} %pad_maximum_fusion.1.refs_0_), channel_id=1, source_target_pairs={{24,16},{16,8},{8,0},{25,17},{17,9},{9,1},{26,18},{18,10},{10,2},{... | collective-permute-start | bytes 2359304 | tf_op jit(solution)/shard_map/ppermute | solution.py:242
  69.8 23.9 %collective-permute-start.7 = (bf16[512,768]{1,0:T(8,128)(2,1)S(1)}, bf16[512,768]{1,0:T(8,128)(2,1)}, u32[]{:S(2)}, u32[]{:S(2)}) collective-permute-start(bf16[512,768]{1,0:T(8,128)(2,1)S(1)} %pad_maximum_fusion.1.refs_0_), channel_id=1, source_target_pairs={{0,8},{8,16},{16,24},{1,9},{9,17},{17,25},{2,10},{10,18},{18,26},{... | collective-permute-start | bytes 2359304 | tf_op jit(solution)/shard_map/ppermute | solution.py:241
  93.7 19.3 %collective-permute-start.9 = (bf16[512,768]{1,0:T(8,128)(2,1)}, bf16[512,768]{1,0:T(8,128)(2,1)S(1)}, u32[]{:S(2)}, u32[]{:S(2)}) collective-permute-start(bf16[512,768]{1,0:T(8,128)(2,1)} %collective-permute-done.7.refs_4_), channel_id=1, source_target_pairs={{8,16},{16,24},{9,17},{17,25},{10,18},{18,26},{11,19},{19,27},{12,... | collective-permute-start | bytes 2359304 | tf_op jit(solution)/shard_map/ppermute | solution.py:241
  94.4 18.6 %collective-permute-start.8 = (bf16[512,768]{1,0:T(8,128)(2,1)}, bf16[512,768]{1,0:T(8,128)(2,1)S(1)}, u32[]{:S(2)}, u32[]{:S(2)}) collective-permute-start(bf16[512,768]{1,0:T(8,128)(2,1)} %collective-permute-done.6.refs_1_), channel_id=1, source_target_pairs={{16,8},{8,0},{17,9},{9,1},{18,10},{10,2},{19,11},{11,3},{20,12},{1... | collective-permute-start | bytes 2359304 | tf_op jit(solution)/shard_map/ppermute | solution.py:242
  115.3 36.8 %collective-permute-start.19 = (bf16[512,768]{1,0:T(8,128)(2,1)S(1)}, bf16[512,768]{1,0:T(8,128)(2,1)S(1)}, u32[]{:S(2)}, u32[]{:S(2)}) collective-permute-start(bf16[512,768]{1,0:T(8,128)(2,1)S(1)} %add_convert_fusion.7), channel_id=1, source_target_pairs={{24,16},{16,8},{8,0},{25,17},{17,9},{9,1},{26,18},{18,10},{10,2},{... | collective-permute-start | bytes 2359304 | tf_op jit(solution)/shard_map/ppermute | solution.py:249
  131.3 37.6 %collective-permute-start.16 = (bf16[512,768]{1,0:T(8,128)(2,1)S(1)}, bf16[512,768]{1,0:T(8,128)(2,1)S(1)}, u32[]{:S(2)}, u32[]{:S(2)}) collective-permute-start(bf16[512,768]{1,0:T(8,128)(2,1)S(1)} %pad_maximum_fusion.2.refs_0_), channel_id=1, source_target_pairs={{0,8},{8,16},{16,24},{1,9},{9,17},{17,25},{2,10},{10,18},{18,26},{... | collective-permute-start | bytes 2359304 | tf_op jit(solution)/shard_map/ppermute | solution.py:241
  134.2 34.8 %collective-permute-start.17 = (bf16[512,768]{1,0:T(8,128)(2,1)S(1)}, bf16[512,768]{1,0:T(8,128)(2,1)S(1)}, u32[]{:S(2)}, u32[]{:S(2)}) collective-permute-start(bf16[512,768]{1,0:T(8,128)(2,1)S(1)} %pad_maximum_fusion.2.refs_0_), channel_id=1, source_target_pairs={{24,16},{16,8},{8,0},{25,17},{17,9},{9,1},{26,18},{18,10},{10,2},{... | collective-permute-start | bytes 2359304 | tf_op jit(solution)/shard_map/ppermute | solution.py:242
  135.7 33.3 %collective-permute-start.18 = (bf16[512,768]{1,0:T(8,128)(2,1)S(1)}, bf16[512,768]{1,0:T(8,128)(2,1)S(1)}, u32[]{:S(2)}, u32[]{:S(2)}) collective-permute-start(bf16[512,768]{1,0:T(8,128)(2,1)S(1)} %add_convert_fusion.8), channel_id=1, source_target_pairs={{0,8},{8,16},{16,24},{1,9},{9,17},{17,25},{2,10},{10,18},{18,26},{... | collective-permute-start | bytes 2359304 | tf_op jit(solution)/shard_map/ppermute | solution.py:248
  148.0 34.1 %collective-permute-start.22 = (bf16[512,768]{1,0:T(8,128)(2,1)S(1)}, bf16[512,768]{1,0:T(8,128)(2,1)S(1)}, u32[]{:S(2)}, u32[]{:S(2)}) collective-permute-start(bf16[512,768]{1,0:T(8,128)(2,1)S(1)} %get-tuple-element.63), channel_id=1, source_target_pairs={{0,8},{1,9},{2,10},{3,11},{4,12},{5,13},{6,14},{7,15}} | collective-permute-start | bytes 2359304 | tf_op jit(solution)/shard_map/ppermute | solution.py:248
  152.1 30.0 %collective-permute-start.23 = (bf16[512,768]{1,0:T(8,128)(2,1)S(1)}, bf16[512,768]{1,0:T(8,128)(2,1)S(1)}, u32[]{:S(2)}, u32[]{:S(2)}) collective-permute-start(bf16[512,768]{1,0:T(8,128)(2,1)S(1)} %get-tuple-element.64), channel_id=1, source_target_pairs={{24,16},{25,17},{26,18},{27,19},{28,20},{29,21},{30,22},{31,23}} | collective-permute-start | bytes 2359304 | tf_op jit(solution)/shard_map/ppermute | solution.py:249
  169.0 19.3 %collective-permute-start.21 = (bf16[512,768]{1,0:T(8,128)(2,1)S(1)}, bf16[512,768]{1,0:T(8,128)(2,1)S(1)}, u32[]{:S(2)}, u32[]{:S(2)}) collective-permute-start(bf16[512,768]{1,0:T(8,128)(2,1)S(1)} %collective-permute-done.17.refs_1_), channel_id=1, source_target_pairs={{16,8},{8,0},{17,9},{9,1},{18,10},{10,2},{19,11},{11,3},{20,12},{1... | collective-permute-start | bytes 2359304 | tf_op jit(solution)/shard_map/ppermute | solution.py:242
  183.2 18.3 %collective-permute-start.26 = (bf16[512,768]{1,0:T(8,128)(2,1)S(1)}, bf16[512,768]{1,0:T(8,128)(2,1)S(1)}, u32[]{:S(2)}, u32[]{:S(2)}) collective-permute-start(bf16[512,768]{1,0:T(8,128)(2,1)S(1)} %get-tuple-element.98), channel_id=1, source_target_pairs={{0,8},{8,16},{1,9},{9,17},{2,10},{10,18},{3,11},{11,19},{4,12},{12... | collective-permute-start | bytes 2359304 | tf_op jit(solution)/shard_map/ppermute | solution.py:248
  188.3 22.3 %collective-permute-start.25 = (bf16[512,768]{1,0:T(8,128)(2,1)S(1)}, bf16[512,768]{1,0:T(8,128)(2,1)S(1)}, u32[]{:S(2)}, u32[]{:S(2)}) collective-permute-start(bf16[512,768]{1,0:T(8,128)(2,1)S(1)} %collective-permute-done.21.refs_2_), channel_id=1, source_target_pairs={{8,0},{9,1},{10,2},{11,3},{12,4},{13,5},{14,6},{15,7}} | collective-permute-start | bytes 2359304 | tf_op jit(solution)/shard_map/ppermute | solution.py:242
  189.7 20.9 %collective-permute-start.24 = (bf16[512,768]{1,0:T(8,128)(2,1)S(1)}, bf16[512,768]{1,0:T(8,128)(2,1)S(1)}, u32[]{:S(2)}, u32[]{:S(2)}) collective-permute-start(bf16[512,768]{1,0:T(8,128)(2,1)S(1)} %collective-permute-done.20.refs_5_), channel_id=1, source_target_pairs={{16,24},{17,25},{18,26},{19,27},{20,28},{21,29},{22,30},{23,31}} | collective-permute-start | bytes 2359304 | tf_op jit(solution)/shard_map/ppermute | solution.py:241
  190.7 38.2 %collective-permute-start.29 = (bf16[512,768]{1,0:T(8,128)(2,1)S(1)}, bf16[512,768]{1,0:T(8,128)(2,1)S(1)}, u32[]{:S(2)}, u32[]{:S(2)}) collective-permute-start(bf16[512,768]{1,0:T(8,128)(2,1)S(1)} %add_convert_fusion.5), channel_id=1, source_target_pairs={{24,16},{16,8},{8,0},{25,17},{17,9},{9,1},{26,18},{18,10},{10,2},{... | collective-permute-start | bytes 2359304 | tf_op jit(solution)/shard_map/ppermute | solution.py:249
  201.7 28.1 %collective-permute-start.28 = (bf16[512,768]{1,0:T(8,128)(2,1)S(1)}, bf16[512,768]{1,0:T(8,128)(2,1)}, u32[]{:S(2)}, u32[]{:S(2)}) collective-permute-start(bf16[512,768]{1,0:T(8,128)(2,1)S(1)} %add_convert_fusion.6), channel_id=1, source_target_pairs={{0,8},{8,16},{16,24},{1,9},{9,17},{17,25},{2,10},{10,18},{18,26},{... | collective-permute-start | bytes 2359304 | tf_op jit(solution)/shard_map/ppermute | solution.py:248
  229.8 53.7 %all-to-all-start.1 = ((bf16[8,128,2048]{2,1,0:T(8,128)(2,1)}), bf16[8,128,2048]{2,1,0:T(8,128)(2,1)}, u32[]{:S(2)}, u32[]{:S(2)}) async-start(bf16[8,128,2048]{2,1,0:T(8,128)(2,1)} %back_products.1), calls=%async_computation.1 | async-start | bytes 8388608 | tf_op jit(solution)/shard_map/all_to_all | solution.py:258
  244.8 18.1 %collective-permute-start.34 = (bf16[512,768]{1,0:T(8,128)(2,1)}, bf16[512,768]{1,0:T(8,128)(2,1)}, u32[]{:S(2)}, u32[]{:S(2)}) collective-permute-start(bf16[512,768]{1,0:T(8,128)(2,1)} %get-tuple-element.96), channel_id=1, source_target_pairs={{24,16},{16,8},{25,17},{17,9},{26,18},{18,10},{27,19},{19,11},{28,... | collective-permute-start | bytes 2359304 | tf_op jit(solution)/shard_map/ppermute | solution.py:249
  (38 other events, 447.5 us)

commit v6 on v5

--- a/solution.py
+++ b/solution.py
@@ -62,7 +62,7 @@
     return call(
         functools.partial(dispatch_body, n),
         "dispatch",
-        jax.ShapeDtypeStruct((experts, 2 * cap, width), BF16),
+        pltpu.HBM((experts, 2 * cap, width), BF16),
         [SCALAR, WHOLE, WHOLE, WHOLE, WHOLE],
         4 * experts * cap * tokens.shape[0] * width,
         4 * (experts * cap + tokens.shape[0]) * width,

time: 290 us -> 290 us (level)
    unnamed x50 -> x48, local copies, waits for them, and re-layouts: 10.7 us -> 8.69 us
  transfers between devices with their start and end apart: 38 -> 38, of which waited for: 16 -> 16; matrix products, arithmetic and copies ran while one was open for 6% -> 6% of each run, Pallas kernels for 11% -> 12%
where the time goes in v6:
time: 290 us; the launch traced here: 288 us
  waiting for transfers between devices  134 us (46%)
  starting transfers between devices  86.9 us (30%)
  Pallas kernels  38.5 us (13%)
  other arithmetic  14.2 us (5%)
  local copies, waits for them, and re-layouts  13 us (4%)
    ppermute x9, waiting for transfers between devices, scatter_step(): lax.ppermute(up, 'dp', [(j, j + 1) for j in range(step)])  74.9 us
    ppermute x9, waiting for transfers between devices, gather_step(): lax.ppermute(down, 'dp', [(j, j - 1) for j in range(n - step, 0, -1)])  46.1 us
    ppermute x9, starting transfers between devices, scatter_step(): lax.ppermute(up, 'dp', [(j, j + 1) for j in range(step)])  38.4 us
    pallas_call x3, Pallas kernels, part(): call(functools.partial(part_body, n), 'part', out_shape, [SCALAR, WHOLE]...  23.6 us
    ppermute x9, starting transfers between devices, gather_step(): lax.ppermute(up, 'dp', [(j, j + 1) for j in range(step - 1, n - 1)])  17.5 us
    ppermute x9, starting transfers between devices, gather_step(): lax.ppermute(down, 'dp', [(j, j - 1) for j in range(n - step, 0, -1)])  11.8 us
    ppermute x9, starting transfers between devices, scatter_step(): lax.ppermute(down, 'dp', [(j, j - 1) for j in range(n - 1, n - 1 - step,...  9.95 us
    all_to_all x2, starting transfers between devices, exchange(): lax.all_to_all(rows, 'expert', split_axis=0, concat_axis=0, tiled=True)  9.27 us
  transfers between devices with their start and end apart: 38, of which 16 were waited for; matrix products, arithmetic and copies ran while one was open for 6% of the time, Pallas kernels for 12%

profile of v6, /device:TPU:0, one launch (start us, length us, event | category | flops | bytes accessed | tf_op | source)
XLA Modules:
  0.0 287.8 jit_solution(17257708404406927150)
XLA Ops:
  2.9 5.0 %collective-permute-start = (bf16[512,768]{1,0:T(8,128)(2,1)S(1)}, bf16[512,768]{1,0:T(8,128)(2,1)S(1)}, u32[]{:S(2)}, u32[]{:S(2)}) collective-permute-start(bf16[512,768]{1,0:T(8,128)(2,1)S(1)} %pad_maximum_fusion.refs_0_), channel_id=1, source_target_pairs={{0,8},{8,16},{16,24},{1,9},{9,17},{17,25},{2,10},{10,18},{18,26},{... | collective-permute-start | bytes 2359304 | tf_op jit(solution)/shard_map/ppermute | solution.py:241
  12.8 4.7 %all-to-all-start = ((bf16[8,128,2048]{2,1,0:T(8,128)(2,1)}), bf16[8,128,2048]{2,1,0:T(8,128)(2,1)}, u32[]{:S(2)}, u32[]{:S(2)}) async-start(bf16[8,128,2048]{2,1,0:T(8,128)(2,1)} %dispatch.1), calls=%async_computation | async-start | bytes 8388608 | tf_op jit(solution)/shard_map/all_to_all | solution.py:258
  17.5 7.1 %collective-permute-done.refs_4_ = bf16[512,768]{1,0:T(8,128)(2,1)S(1)} collective-permute-done((bf16[512,768]{1,0:T(8,128)(2,1)S(1)}, bf16[512,768]{1,0:T(8,128)(2,1)S(1)}, u32[]{:S(2)}, u32[]{:S(2)}) %collective-permute-start) | collective-permute-done | bytes 786464 | tf_op jit(solution)/shard_map/ppermute | solution.py:241
  30.9 18.3 %collective-permute-done.4.refs_2_ = bf16[512,768]{1,0:T(8,128)(2,1)S(1)} collective-permute-done((bf16[512,768]{1,0:T(8,128)(2,1)}, bf16[512,768]{1,0:T(8,128)(2,1)S(1)}, u32[]{:S(2)}, u32[]{:S(2)}) %collective-permute-start.4) | collective-permute-done | bytes 786464 | tf_op jit(solution)/shard_map/ppermute | solution.py:242
  52.5 16.1 %collective-permute-done.5.refs_1_.refs_3_ = bf16[512,768]{1,0:T(8,128)(2,1)S(1)} collective-permute-done((bf16[512,768]{1,0:T(8,128)(2,1)S(1)}, bf16[512,768]{1,0:T(8,128)(2,1)S(1)}, u32[]{:S(2)}, u32[]{:S(2)}) %collective-permute-start.5) | collective-permute-done | bytes 786464 | tf_op jit(solution)/shard_map/ppermute | solution.py:242
  69.8 5.4 %collective-permute-start.7 = (bf16[512,768]{1,0:T(8,128)(2,1)S(1)}, bf16[512,768]{1,0:T(8,128)(2,1)}, u32[]{:S(2)}, u32[]{:S(2)}) collective-permute-start(bf16[512,768]{1,0:T(8,128)(2,1)S(1)} %pad_maximum_fusion.1.refs_0_), channel_id=1, source_target_pairs={{0,8},{8,16},{16,24},{1,9},{9,17},{17,25},{2,10},{10,18},{18,26},{... | collective-permute-start | bytes 2359304 | tf_op jit(solution)/shard_map/ppermute | solution.py:241
  83.3 8.3 %part.3 = (bf16[2048,768]{1,0:T(8,128)(2,1)S(1)}, bf16[512,256]{1,0:T(8,128)(2,1)S(1)}, bf16[512,512]{1,0:T(8,128)(2,1)S(1)}, bf16[512,768]{1,0:T(8,128)(2,1)S(1...) custom-call(s32[1]{0:T(128)} %touch.1.index_ref, ...), custom_call_target="tpu_custom_call" | custom-call | flops 3221225472 | bytes 13631488 | tf_op jit(solution)/shard_map/part/pallas_call | solution.py:133
  95.7 11.0 %collective-permute-done.10 = bf16[512,768]{1,0:T(8,128)(2,1)S(1)} collective-permute-done((bf16[512,768]{1,0:T(8,128)(2,1)S(1)}, bf16[512,768]{1,0:T(8,128)(2,1)S(1)}, u32[]{:S(2)}, u32[]{:S(2)}) %collective-permute-start.10) | collective-permute-done | bytes 786464 | tf_op jit(solution)/shard_map/ppermute | solution.py:248
  108.0 5.0 %collective-permute-start.14 = (bf16[512,768]{1,0:T(8,128)(2,1)S(1)}, bf16[512,768]{1,0:T(8,128)(2,1)S(1)}, u32[]{:S(2)}, u32[]{:S(2)}) collective-permute-start(bf16[512,768]{1,0:T(8,128)(2,1)S(1)} %get-tuple-element.100), channel_id=1, source_target_pairs={{0,8},{8,16},{1,9},{9,17},{2,10},{10,18},{3,11},{11,19},{4,12},{12... | collective-permute-start | bytes 2359304 | tf_op jit(solution)/shard_map/ppermute | solution.py:248
  116.7 9.2 %collective-permute-done.14 = bf16[512,768]{1,0:T(8,128)(2,1)S(1)} collective-permute-done((bf16[512,768]{1,0:T(8,128)(2,1)S(1)}, bf16[512,768]{1,0:T(8,128)(2,1)S(1)}, u32[]{:S(2)}, u32[]{:S(2)}) %collective-permute-start.14) | collective-permute-done | bytes 786464 | tf_op jit(solution)/shard_map/ppermute | solution.py:248
  125.9 5.4 %collective-permute-done.12.refs_3_ = bf16[512,768]{1,0:T(8,128)(2,1)S(1)} collective-permute-done((bf16[512,768]{1,0:T(8,128)(2,1)S(1)}, bf16[512,768]{1,0:T(8,128)(2,1)S(1)}, u32[]{:S(2)}, u32[]{:S(2)}) %collective-permute-start.12) | collective-permute-done | bytes 786464 | tf_op jit(solution)/shard_map/ppermute | solution.py:242
  135.7 4.6 %collective-permute-start.18 = (bf16[512,768]{1,0:T(8,128)(2,1)S(1)}, bf16[512,768]{1,0:T(8,128)(2,1)S(1)}, u32[]{:S(2)}, u32[]{:S(2)}) collective-permute-start(bf16[512,768]{1,0:T(8,128)(2,1)S(1)} %add_convert_fusion.8), channel_id=1, source_target_pairs={{0,8},{8,16},{16,24},{1,9},{9,17},{17,25},{2,10},{10,18},{18,26},{... | collective-permute-start | bytes 2359304 | tf_op jit(solution)/shard_map/ppermute | solution.py:248
  140.3 7.7 %part.4 = (bf16[2048,768]{1,0:T(8,128)(2,1)S(1)}, bf16[512,256]{1,0:T(8,128)(2,1)S(1)}, bf16[512,512]{1,0:T(8,128)(2,1)S(1)}, bf16[512,768]{1,0:T(8,128)(2,1)S(1...) custom-call(s32[1]{0:T(128)} %bitcast.index_ref, ...), custom_call_target="tpu_custom_call" | custom-call | flops 3221225472 | bytes 13631488 | tf_op jit(solution)/shard_map/part/pallas_call | solution.py:133
  152.9 16.1 %collective-permute-done.18 = bf16[512,768]{1,0:T(8,128)(2,1)S(1)} collective-permute-done((bf16[512,768]{1,0:T(8,128)(2,1)S(1)}, bf16[512,768]{1,0:T(8,128)(2,1)S(1)}, u32[]{:S(2)}, u32[]{:S(2)}) %collective-permute-start.18) | collective-permute-done | bytes 786464 | tf_op jit(solution)/shard_map/ppermute | solution.py:248
  171.0 11.1 %collective-permute-done.22 = bf16[512,768]{1,0:T(8,128)(2,1)S(1)} collective-permute-done((bf16[512,768]{1,0:T(8,128)(2,1)S(1)}, bf16[512,768]{1,0:T(8,128)(2,1)S(1)}, u32[]{:S(2)}, u32[]{:S(2)}) %collective-permute-start.22) | collective-permute-done | bytes 786464 | tf_op jit(solution)/shard_map/ppermute | solution.py:248
  183.2 5.0 %collective-permute-start.26 = (bf16[512,768]{1,0:T(8,128)(2,1)S(1)}, bf16[512,768]{1,0:T(8,128)(2,1)S(1)}, u32[]{:S(2)}, u32[]{:S(2)}) collective-permute-start(bf16[512,768]{1,0:T(8,128)(2,1)S(1)} %get-tuple-element.98), channel_id=1, source_target_pairs={{0,8},{8,16},{1,9},{9,17},{2,10},{10,18},{3,11},{11,19},{4,12},{12... | collective-permute-start | bytes 2359304 | tf_op jit(solution)/shard_map/ppermute | solution.py:248
  192.0 9.6 %collective-permute-done.26 = bf16[512,768]{1,0:T(8,128)(2,1)S(1)} collective-permute-done((bf16[512,768]{1,0:T(8,128)(2,1)S(1)}, bf16[512,768]{1,0:T(8,128)(2,1)S(1)}, u32[]{:S(2)}, u32[]{:S(2)}) %collective-permute-start.26) | collective-permute-done | bytes 786464 | tf_op jit(solution)/shard_map/ppermute | solution.py:248
  201.7 6.1 %collective-permute-start.28 = (bf16[512,768]{1,0:T(8,128)(2,1)S(1)}, bf16[512,768]{1,0:T(8,128)(2,1)}, u32[]{:S(2)}, u32[]{:S(2)}) collective-permute-start(bf16[512,768]{1,0:T(8,128)(2,1)S(1)} %add_convert_fusion.6), channel_id=1, source_target_pairs={{0,8},{8,16},{16,24},{1,9},{9,17},{17,25},{2,10},{10,18},{18,26},{... | collective-permute-start | bytes 2359304 | tf_op jit(solution)/shard_map/ppermute | solution.py:248
  210.6 7.6 %part.5 = (bf16[2048,768]{1,0:T(8,128)(2,1)S(1)}, bf16[512,256]{1,0:T(8,128)(2,1)S(1)}, bf16[512,512]{1,0:T(8,128)(2,1)S(1)}, bf16[512,768]{1,0:T(8,128)(2,1)S(1...) custom-call(s32[1]{0:T(128)} %bitcast.index_ref, ...), custom_call_target="tpu_custom_call" | custom-call | flops 3221225472 | bytes 13631488 | tf_op jit(solution)/shard_map/part/pallas_call | solution.py:133
  222.1 6.8 %back_products.1 = bf16[8,128,2048]{2,1,0:T(8,128)(2,1)} custom-call(bf16[512,256]{1,0:T(8,128)(2,1)S(1)} %get-tuple-element.47.refs_0_, bf16[512,256]{1,0:T(8,128)(2,1)S(1)} %get-tuple-element.58.refs_1_, bf16[512,256]{1,0:T(8,128)(2,1)S(1)} %get-tuple-element.69.refs_2_, bf16[512,512]{1,0:T(8,128)(2,1)S(1)} %get-tuple-element.70.refs_3_, ...), custom_call_target="tpu_custom_call" | custom-call | flops 4831838208 | bytes 13631488 | tf_op jit(solution)/shard_map/back_products/pallas_call | solution.py:183
  239.5 5.3 %collective-permute-start.31 = (bf16[512,768]{1,0:T(8,128)(2,1)}, bf16[512,768]{1,0:T(8,128)(2,1)}, u32[]{:S(2)}, u32[]{:S(2)}) collective-permute-start(bf16[512,768]{1,0:T(8,128)(2,1)} %get-tuple-element.95), channel_id=1, source_target_pairs={{0,8},{8,16},{1,9},{9,17},{2,10},{10,18},{3,11},{11,19},{4,12},{12... | collective-permute-start | bytes 2359304 | tf_op jit(solution)/shard_map/ppermute | solution.py:248
  248.1 8.7 %collective-permute-done.31 = bf16[512,768]{1,0:T(8,128)(2,1)} collective-permute-done((bf16[512,768]{1,0:T(8,128)(2,1)}, bf16[512,768]{1,0:T(8,128)(2,1)}, u32[]{:S(2)}, u32[]{:S(2)}) %collective-permute-start.31) | collective-permute-done | bytes 786464 | tf_op jit(solution)/shard_map/ppermute | solution.py:248
  267.4 7.1 %collective-permute-done.32 = bf16[512,768]{1,0:T(8,128)(2,1)S(1)} collective-permute-done((bf16[512,768]{1,0:T(8,128)(2,1)S(1)}, bf16[512,768]{1,0:T(8,128)(2,1)S(1)}, u32[]{:S(2)}, u32[]{:S(2)}) %collective-permute-start.32) | collective-permute-done | bytes 786464 | tf_op jit(solution)/shard_map/ppermute | solution.py:248
  274.5 5.7 %collective-permute-done.35 = bf16[512,768]{1,0:T(8,128)(2,1)S(1)} collective-permute-done((bf16[512,768]{1,0:T(8,128)(2,1)S(1)}, bf16[512,768]{1,0:T(8,128)(2,1)S(1)}, u32[]{:S(2)}, u32[]{:S(2)}) %collective-permute-start.35) | collective-permute-done | bytes 786464 | tf_op jit(solution)/shard_map/ppermute | solution.py:249
  (137 shorter events, 89.5 us)
Async XLA Ops:
  2.9 21.7 %collective-permute-start = (bf16[512,768]{1,0:T(8,128)(2,1)S(1)}, bf16[512,768]{1,0:T(8,128)(2,1)S(1)}, u32[]{:S(2)}, u32[]{:S(2)}) collective-permute-start(bf16[512,768]{1,0:T(8,128)(2,1)S(1)} %pad_maximum_fusion.refs_0_), channel_id=1, source_target_pairs={{0,8},{8,16},{16,24},{1,9},{9,17},{17,25},{2,10},{10,18},{18,26},{... | collective-permute-start | bytes 2359304 | tf_op jit(solution)/shard_map/ppermute | solution.py:241
  7.9 21.0 %collective-permute-start.3 = (bf16[512,768]{1,0:T(8,128)(2,1)S(1)}, bf16[512,768]{1,0:T(8,128)(2,1)}, u32[]{:S(2)}, u32[]{:S(2)}) collective-permute-start(bf16[512,768]{1,0:T(8,128)(2,1)S(1)} %pad_maximum_fusion.refs_0_), channel_id=1, source_target_pairs={{24,16},{16,8},{8,0},{25,17},{17,9},{9,1},{26,18},{18,10},{10,2},{... | collective-permute-start | bytes 2359304 | tf_op jit(solution)/shard_map/ppermute | solution.py:242
  12.8 64.8 %all-to-all-start = ((bf16[8,128,2048]{2,1,0:T(8,128)(2,1)}), bf16[8,128,2048]{2,1,0:T(8,128)(2,1)}, u32[]{:S(2)}, u32[]{:S(2)}) async-start(bf16[8,128,2048]{2,1,0:T(8,128)(2,1)} %dispatch.1), calls=%async_computation | async-start | bytes 8388608 | tf_op jit(solution)/shard_map/all_to_all | solution.py:258
  28.9 20.4 %collective-permute-start.4 = (bf16[512,768]{1,0:T(8,128)(2,1)}, bf16[512,768]{1,0:T(8,128)(2,1)S(1)}, u32[]{:S(2)}, u32[]{:S(2)}) collective-permute-start(bf16[512,768]{1,0:T(8,128)(2,1)} %collective-permute-done.3.refs_1_), channel_id=1, source_target_pairs={{16,8},{8,0},{17,9},{9,1},{18,10},{10,2},{19,11},{11,3},{20,12},{1... | collective-permute-start | bytes 2359304 | tf_op jit(solution)/shard_map/ppermute | solution.py:242
  30.2 22.3 %collective-permute-start.2 = (bf16[512,768]{1,0:T(8,128)(2,1)S(1)}, bf16[512,768]{1,0:T(8,128)(2,1)S(1)}, u32[]{:S(2)}, u32[]{:S(2)}) collective-permute-start(bf16[512,768]{1,0:T(8,128)(2,1)S(1)} %collective-permute-done.1.refs_5_), channel_id=1, source_target_pairs={{16,24},{17,25},{18,26},{19,27},{20,28},{21,29},{22,30},{23,31}} | collective-permute-start | bytes 2359304 | tf_op jit(solution)/shard_map/ppermute | solution.py:241
  49.2 19.3 %collective-permute-start.5 = (bf16[512,768]{1,0:T(8,128)(2,1)S(1)}, bf16[512,768]{1,0:T(8,128)(2,1)S(1)}, u32[]{:S(2)}, u32[]{:S(2)}) collective-permute-start(bf16[512,768]{1,0:T(8,128)(2,1)S(1)} %collective-permute-done.4.refs_2_), channel_id=1, source_target_pairs={{8,0},{9,1},{10,2},{11,3},{12,4},{13,5},{14,6},{15,7}} | collective-permute-start | bytes 2359304 | tf_op jit(solution)/shard_map/ppermute | solution.py:242
  68.6 25.1 %collective-permute-start.6 = (bf16[512,768]{1,0:T(8,128)(2,1)S(1)}, bf16[512,768]{1,0:T(8,128)(2,1)}, u32[]{:S(2)}, u32[]{:S(2)}) collective-permute-start(bf16[512,768]{1,0:T(8,128)(2,1)S(1)} %pad_maximum_fusion.1.refs_0_), channel_id=1, source_target_pairs={{24,16},{16,8},{8,0},{25,17},{17,9},{9,1},{26,18},{18,10},{10,2},{... | collective-permute-start | bytes 2359304 | tf_op jit(solution)/shard_map/ppermute | solution.py:242
  69.8 23.9 %collective-permute-start.7 = (bf16[512,768]{1,0:T(8,128)(2,1)S(1)}, bf16[512,768]{1,0:T(8,128)(2,1)}, u32[]{:S(2)}, u32[]{:S(2)}) collective-permute-start(bf16[512,768]{1,0:T(8,128)(2,1)S(1)} %pad_maximum_fusion.1.refs_0_), channel_id=1, source_target_pairs={{0,8},{8,16},{16,24},{1,9},{9,17},{17,25},{2,10},{10,18},{18,26},{... | collective-permute-start | bytes 2359304 | tf_op jit(solution)/shard_map/ppermute | solution.py:241
  93.7 19.3 %collective-permute-start.9 = (bf16[512,768]{1,0:T(8,128)(2,1)}, bf16[512,768]{1,0:T(8,128)(2,1)S(1)}, u32[]{:S(2)}, u32[]{:S(2)}) collective-permute-start(bf16[512,768]{1,0:T(8,128)(2,1)} %collective-permute-done.7.refs_4_), channel_id=1, source_target_pairs={{8,16},{16,24},{9,17},{17,25},{10,18},{18,26},{11,19},{19,27},{12,... | collective-permute-start | bytes 2359304 | tf_op jit(solution)/shard_map/ppermute | solution.py:241
  94.4 18.6 %collective-permute-start.8 = (bf16[512,768]{1,0:T(8,128)(2,1)}, bf16[512,768]{1,0:T(8,128)(2,1)S(1)}, u32[]{:S(2)}, u32[]{:S(2)}) collective-permute-start(bf16[512,768]{1,0:T(8,128)(2,1)} %collective-permute-done.6.refs_1_), channel_id=1, source_target_pairs={{16,8},{8,0},{17,9},{9,1},{18,10},{10,2},{19,11},{11,3},{20,12},{1... | collective-permute-start | bytes 2359304 | tf_op jit(solution)/shard_map/ppermute | solution.py:242
  115.3 36.8 %collective-permute-start.19 = (bf16[512,768]{1,0:T(8,128)(2,1)S(1)}, bf16[512,768]{1,0:T(8,128)(2,1)S(1)}, u32[]{:S(2)}, u32[]{:S(2)}) collective-permute-start(bf16[512,768]{1,0:T(8,128)(2,1)S(1)} %add_convert_fusion.7), channel_id=1, source_target_pairs={{24,16},{16,8},{8,0},{25,17},{17,9},{9,1},{26,18},{18,10},{10,2},{... | collective-permute-start | bytes 2359304 | tf_op jit(solution)/shard_map/ppermute | solution.py:249
  131.3 37.6 %collective-permute-start.16 = (bf16[512,768]{1,0:T(8,128)(2,1)S(1)}, bf16[512,768]{1,0:T(8,128)(2,1)S(1)}, u32[]{:S(2)}, u32[]{:S(2)}) collective-permute-start(bf16[512,768]{1,0:T(8,128)(2,1)S(1)} %pad_maximum_fusion.2.refs_0_), channel_id=1, source_target_pairs={{0,8},{8,16},{16,24},{1,9},{9,17},{17,25},{2,10},{10,18},{18,26},{... | collective-permute-start | bytes 2359304 | tf_op jit(solution)/shard_map/ppermute | solution.py:241
  134.2 34.8 %collective-permute-start.17 = (bf16[512,768]{1,0:T(8,128)(2,1)S(1)}, bf16[512,768]{1,0:T(8,128)(2,1)S(1)}, u32[]{:S(2)}, u32[]{:S(2)}) collective-permute-start(bf16[512,768]{1,0:T(8,128)(2,1)S(1)} %pad_maximum_fusion.2.refs_0_), channel_id=1, source_target_pairs={{24,16},{16,8},{8,0},{25,17},{17,9},{9,1},{26,18},{18,10},{10,2},{... | collective-permute-start | bytes 2359304 | tf_op jit(solution)/shard_map/ppermute | solution.py:242
  135.7 33.3 %collective-permute-start.18 = (bf16[512,768]{1,0:T(8,128)(2,1)S(1)}, bf16[512,768]{1,0:T(8,128)(2,1)S(1)}, u32[]{:S(2)}, u32[]{:S(2)}) collective-permute-start(bf16[512,768]{1,0:T(8,128)(2,1)S(1)} %add_convert_fusion.8), channel_id=1, source_target_pairs={{0,8},{8,16},{16,24},{1,9},{9,17},{17,25},{2,10},{10,18},{18,26},{... | collective-permute-start | bytes 2359304 | tf_op jit(solution)/shard_map/ppermute | solution.py:248
  148.0 34.1 %collective-permute-start.22 = (bf16[512,768]{1,0:T(8,128)(2,1)S(1)}, bf16[512,768]{1,0:T(8,128)(2,1)S(1)}, u32[]{:S(2)}, u32[]{:S(2)}) collective-permute-start(bf16[512,768]{1,0:T(8,128)(2,1)S(1)} %get-tuple-element.63), channel_id=1, source_target_pairs={{0,8},{1,9},{2,10},{3,11},{4,12},{5,13},{6,14},{7,15}} | collective-permute-start | bytes 2359304 | tf_op jit(solution)/shard_map/ppermute | solution.py:248
  152.1 30.0 %collective-permute-start.23 = (bf16[512,768]{1,0:T(8,128)(2,1)S(1)}, bf16[512,768]{1,0:T(8,128)(2,1)S(1)}, u32[]{:S(2)}, u32[]{:S(2)}) collective-permute-start(bf16[512,768]{1,0:T(8,128)(2,1)S(1)} %get-tuple-element.64), channel_id=1, source_target_pairs={{24,16},{25,17},{26,18},{27,19},{28,20},{29,21},{30,22},{31,23}} | collective-permute-start | bytes 2359304 | tf_op jit(solution)/shard_map/ppermute | solution.py:249
  169.0 19.3 %collective-permute-start.21 = (bf16[512,768]{1,0:T(8,128)(2,1)S(1)}, bf16[512,768]{1,0:T(8,128)(2,1)S(1)}, u32[]{:S(2)}, u32[]{:S(2)}) collective-permute-start(bf16[512,768]{1,0:T(8,128)(2,1)S(1)} %collective-permute-done.17.refs_1_), channel_id=1, source_target_pairs={{16,8},{8,0},{17,9},{9,1},{18,10},{10,2},{19,11},{11,3},{20,12},{1... | collective-permute-start | bytes 2359304 | tf_op jit(solution)/shard_map/ppermute | solution.py:242
  183.2 18.3 %collective-permute-start.26 = (bf16[512,768]{1,0:T(8,128)(2,1)S(1)}, bf16[512,768]{1,0:T(8,128)(2,1)S(1)}, u32[]{:S(2)}, u32[]{:S(2)}) collective-permute-start(bf16[512,768]{1,0:T(8,128)(2,1)S(1)} %get-tuple-element.98), channel_id=1, source_target_pairs={{0,8},{8,16},{1,9},{9,17},{2,10},{10,18},{3,11},{11,19},{4,12},{12... | collective-permute-start | bytes 2359304 | tf_op jit(solution)/shard_map/ppermute | solution.py:248
  188.3 22.3 %collective-permute-start.25 = (bf16[512,768]{1,0:T(8,128)(2,1)S(1)}, bf16[512,768]{1,0:T(8,128)(2,1)S(1)}, u32[]{:S(2)}, u32[]{:S(2)}) collective-permute-start(bf16[512,768]{1,0:T(8,128)(2,1)S(1)} %collective-permute-done.21.refs_2_), channel_id=1, source_target_pairs={{8,0},{9,1},{10,2},{11,3},{12,4},{13,5},{14,6},{15,7}} | collective-permute-start | bytes 2359304 | tf_op jit(solution)/shard_map/ppermute | solution.py:242
  189.7 20.9 %collective-permute-start.24 = (bf16[512,768]{1,0:T(8,128)(2,1)S(1)}, bf16[512,768]{1,0:T(8,128)(2,1)S(1)}, u32[]{:S(2)}, u32[]{:S(2)}) collective-permute-start(bf16[512,768]{1,0:T(8,128)(2,1)S(1)} %collective-permute-done.20.refs_5_), channel_id=1, source_target_pairs={{16,24},{17,25},{18,26},{19,27},{20,28},{21,29},{22,30},{23,31}} | collective-permute-start | bytes 2359304 | tf_op jit(solution)/shard_map/ppermute | solution.py:241
  190.7 38.3 %collective-permute-start.29 = (bf16[512,768]{1,0:T(8,128)(2,1)S(1)}, bf16[512,768]{1,0:T(8,128)(2,1)S(1)}, u32[]{:S(2)}, u32[]{:S(2)}) collective-permute-start(bf16[512,768]{1,0:T(8,128)(2,1)S(1)} %add_convert_fusion.5), channel_id=1, source_target_pairs={{24,16},{16,8},{8,0},{25,17},{17,9},{9,1},{26,18},{18,10},{10,2},{... | collective-permute-start | bytes 2359304 | tf_op jit(solution)/shard_map/ppermute | solution.py:249
  201.7 28.1 %collective-permute-start.28 = (bf16[512,768]{1,0:T(8,128)(2,1)S(1)}, bf16[512,768]{1,0:T(8,128)(2,1)}, u32[]{:S(2)}, u32[]{:S(2)}) collective-permute-start(bf16[512,768]{1,0:T(8,128)(2,1)S(1)} %add_convert_fusion.6), channel_id=1, source_target_pairs={{0,8},{8,16},{16,24},{1,9},{9,17},{17,25},{2,10},{10,18},{18,26},{... | collective-permute-start | bytes 2359304 | tf_op jit(solution)/shard_map/ppermute | solution.py:248
  229.8 53.7 %all-to-all-start.1 = ((bf16[8,128,2048]{2,1,0:T(8,128)(2,1)}), bf16[8,128,2048]{2,1,0:T(8,128)(2,1)}, u32[]{:S(2)}, u32[]{:S(2)}) async-start(bf16[8,128,2048]{2,1,0:T(8,128)(2,1)} %back_products.1), calls=%async_computation.1 | async-start | bytes 8388608 | tf_op jit(solution)/shard_map/all_to_all | solution.py:258
  244.8 18.1 %collective-permute-start.34 = (bf16[512,768]{1,0:T(8,128)(2,1)}, bf16[512,768]{1,0:T(8,128)(2,1)}, u32[]{:S(2)}, u32[]{:S(2)}) collective-permute-start(bf16[512,768]{1,0:T(8,128)(2,1)} %get-tuple-element.96), channel_id=1, source_target_pairs={{24,16},{16,8},{25,17},{17,9},{26,18},{18,10},{27,19},{19,11},{28,... | collective-permute-start | bytes 2359304 | tf_op jit(solution)/shard_map/ppermute | solution.py:249
  (37 other events, 445.5 us)
